TPU v7x, 256 devices: a whole 4x4x8 slice. The times are simulated.
256 devices in a mesh: tok: 32 (over x, z), head: 8 (over y, core).
Axes of the slice: x: 4, y: 4, z: 8, core: 2. Of those that a mesh axis runs over, the one named last changes fastest.
Arguments:
- query: bfloat16 [32768, 5120], P(('tok', 'head')), may hold values from -40 to 40
- key: bfloat16 [32768, 5120], P(('tok', 'head')), may hold values from -5 to 5
- value: bfloat16 [32768, 5120], P(('tok', 'head')), may hold values from -6 to 6
- out_grad: bfloat16 [32768, 5120], P(('tok', 'head')), may hold values from -6 to 6
- intersection: int32 [32, 16], replicated, may hold values from -1 to 1023, as said below
- counts: int32 [32], replicated, may hold values from 12 to 16, as said below
Outputs:
- query_grad: bfloat16 [32768, 5120], P(('tok', 'head'))
- key_grad: bfloat16 [32768, 5120], P(('tok', 'head'))
- value_grad: bfloat16 [32768, 5120], P(('tok', 'head'))
Inputs may be any that keep to these rules, and one draw needn't show every extreme that they name: `intersection`: entries j < counts[f] of row f name blocks of distinct frames, none of them f itself; the others are -1. `counts`: some frame retrieves 16 blocks.
All inputs are finite; a program needn't handle non-finite values.
Results may differ from a plain program's by a relative error of at most 0.027.
Values may be sent and summed in bfloat16 or wider, within the bound.
No kernel may reach another device: no remote copies, remote signals or barrier semaphores. Data moves between devices by JAX's collectives and lax.ppermute only.
A program may use at most 64 MiB of HBM per device.

v0:
```python
import math

import jax
import jax.numpy as jnp
from jax import lax
from jax.sharding import PartitionSpec as P

HD = 128
FBLK = 32


def score_rows(qh, kh, keymask):
    scale = 1.0 / math.sqrt(HD)
    scores = jnp.dot(qh, kh.T, preferred_element_type=jnp.float32) * scale
    return jnp.where(keymask[None, :], scores, -jnp.inf)


def head_forward(qh, kh, vh, keymask):
    scores = score_rows(qh, kh, keymask)
    top = jnp.max(scores, axis=1, keepdims=True)
    expo = jnp.exp(scores - top)
    total = jnp.sum(expo, axis=1, keepdims=True)
    weights = (expo / total).astype(jnp.bfloat16)
    output = jnp.dot(weights, vh, preferred_element_type=jnp.float32).astype(jnp.bfloat16)
    return (output, top + jnp.log(total))


def head_backward(qh, kh, vh, dh, keymask, output, logsum):
    scale = 1.0 / math.sqrt(HD)
    scores = score_rows(qh, kh, keymask)
    prob = jnp.exp(scores - logsum)
    weights = prob.astype(jnp.bfloat16)
    dprob = jnp.dot(dh, vh.T, preferred_element_type=jnp.float32)
    delta = jnp.sum(dh.astype(jnp.float32) * output.astype(jnp.float32), axis=1, keepdims=True)
    dscore = (prob * (dprob - delta)).astype(jnp.bfloat16)
    dquery = (jnp.dot(dscore, kh, preferred_element_type=jnp.float32) * scale).astype(jnp.bfloat16)
    dkey = jnp.dot(dscore.T, qh, preferred_element_type=jnp.float32) * scale
    dvalue = jnp.dot(weights.T, dh, preferred_element_type=jnp.float32)
    return (dquery, dkey, dvalue)


def body(query, key, value, out_grad, intersection, counts):
    frames = lax.axis_size("tok")
    frame = lax.axis_index("tok")
    q_head, k_head, v_head, d_head = (
        lax.all_to_all(query, "head", split_axis=1, concat_axis=0, tiled=True),
        lax.all_to_all(key, "head", split_axis=1, concat_axis=0, tiled=True),
        lax.all_to_all(value, "head", split_axis=1, concat_axis=0, tiled=True),
        lax.all_to_all(out_grad, "head", split_axis=1, concat_axis=0, tiled=True),
    )
    frame_tok, width = q_head.shape
    heads_local = width // HD
    blk_dev = frame_tok // FBLK
    memd = intersection.shape[1]
    slots = jnp.arange(memd, dtype=jnp.int32)
    live_all = slots[None, :] < counts[:, None]
    safe = jnp.maximum(intersection, 0)
    owner = safe // blk_dev
    mine = live_all & (owner == frame)
    wanted = jnp.any(mine, axis=1)
    picked = jnp.sum(jnp.where(mine, safe % blk_dev, 0), axis=1)

    def outgoing(x):
        return x.reshape(blk_dev, FBLK, width)[picked]

    my_ids = lax.dynamic_index_in_dim(safe, frame, 0, keepdims=False)
    my_count = lax.dynamic_index_in_dim(counts, frame, 0, keepdims=False)
    my_live = slots < my_count
    sources = my_ids // blk_dev
    keymask = jnp.concatenate([jnp.ones((frame_tok,), bool), jnp.repeat(my_live, FBLK)])

    def key_list(local, received):
        return jnp.concatenate([local, received[sources].reshape(memd * FBLK, width)], axis=0)

    recv_k, recv_v = (
        lax.all_to_all(outgoing(k_head), "tok", split_axis=0, concat_axis=0, tiled=True),
        lax.all_to_all(outgoing(v_head), "tok", split_axis=0, concat_axis=0, tiled=True),
    )
    keys = key_list(k_head, recv_k)
    vals = key_list(v_head, recv_v)

    def cols(x, head):
        return lax.dynamic_slice_in_dim(x, head * HD, HD, 1)

    def forward_head(head, carry):
        out_all, lse_all = carry
        output, logsum = head_forward(
            cols(q_head, head), cols(keys, head), cols(vals, head), keymask
        )
        out_all = lax.dynamic_update_slice_in_dim(out_all, output, head * HD, 1)
        lse_all = lax.dynamic_update_index_in_dim(lse_all, logsum[:, 0], head, 0)
        return (out_all, lse_all)

    out_all, lse_all = lax.fori_loop(
        0,
        heads_local,
        forward_head,
        (
            jnp.zeros((frame_tok, width), jnp.bfloat16),
            jnp.zeros((heads_local, frame_tok), jnp.float32),
        ),
    )
    total_keys = keys.shape[0]

    def backward_head(head, carry):
        dq_all, dk_all, dv_all = carry
        logsum = lax.dynamic_index_in_dim(lse_all, head, 0, keepdims=False)[:, None]
        dquery, dkey, dvalue = head_backward(
            cols(q_head, head),
            cols(keys, head),
            cols(vals, head),
            cols(d_head, head),
            keymask,
            cols(out_all, head),
            logsum,
        )
        dq_all = lax.dynamic_update_slice_in_dim(dq_all, dquery, head * HD, 1)
        dk_all = lax.dynamic_update_slice_in_dim(dk_all, dkey, head * HD, 1)
        dv_all = lax.dynamic_update_slice_in_dim(dv_all, dvalue, head * HD, 1)
        return (dq_all, dk_all, dv_all)

    dq_all, dk_all, dv_all = lax.fori_loop(
        0,
        heads_local,
        backward_head,
        (
            jnp.zeros((frame_tok, width), jnp.bfloat16),
            jnp.zeros((total_keys, width), jnp.float32),
            jnp.zeros((total_keys, width), jnp.float32),
        ),
    )
    sender = (
        (sources[None, :] == jnp.arange(frames, dtype=jnp.int32)[:, None]) & my_live[None, :]
    ).astype(jnp.bfloat16)

    def returning(grads):
        terms = grads[frame_tok:].astype(jnp.bfloat16).reshape(memd, FBLK, width)
        return jnp.einsum("sj,jbw->sbw", sender, terms, preferred_element_type=jnp.float32).astype(
            jnp.bfloat16
        )

    back_k, back_v = (
        lax.all_to_all(returning(dk_all), "tok", split_axis=0, concat_axis=0, tiled=True),
        lax.all_to_all(returning(dv_all), "tok", split_axis=0, concat_axis=0, tiled=True),
    )
    collect = (
        (picked[None, :] == jnp.arange(blk_dev, dtype=jnp.int32)[:, None]) & wanted[None, :]
    ).astype(jnp.float32)

    def owned(grads, back):
        local = grads[:frame_tok].reshape(blk_dev, FBLK, width)
        extra = jnp.einsum("bs,sfw->bfw", collect, back.astype(jnp.float32))
        return (local + extra).reshape(frame_tok, width).astype(jnp.bfloat16)

    dk_out = owned(dk_all, back_k)
    dv_out = owned(dv_all, back_v)
    return (
        lax.all_to_all(dq_all, "head", split_axis=0, concat_axis=1, tiled=True),
        lax.all_to_all(dk_out, "head", split_axis=0, concat_axis=1, tiled=True),
        lax.all_to_all(dv_out, "head", split_axis=0, concat_axis=1, tiled=True),
    )


def solution(mesh):
    placed = (
        P(("tok", "head"), None),
        P(("tok", "head"), None),
        P(("tok", "head"), None),
        P(("tok", "head"), None),
        P(),
        P(),
    )
    return jax.shard_map(
        body,
        mesh=mesh,
        in_specs=placed,
        out_specs=(P(("tok", "head"), None), P(("tok", "head"), None), P(("tok", "head"), None)),
        check_vma=False,
    )
```

profile of v0, /device:TPU:1, one launch (start us, length us, event | category | flops | bytes accessed | tf_op | source)
XLA Modules:
  0.0 411.5 jit_solution(9007275266249091375)
XLA Ops:
  0.6 2.5 copy.113
  3.1 6.8 %all-to-all-start.1 = ((bf16[128,8,640]{2,0,1:T(8,128)(2,1)}), bf16[128,8,640]{2,0,1:T(8,128)(2,1)S(1)}, u32[]{:S(2)}, u32[]{:S(2)}) async-start(bf16[128,8,640]{2,0,1:T(8,128)(2,1)} %bitcast.75), calls=%async_computation.1 | async-start | bytes 2621440 | tf_op jit(solution)/shard_map/all_to_all | solution.py:47
  11.2 16.7 %all-to-all-done.1 = bf16[128,8,640]{2,0,1:T(8,128)(2,1)S(1)} async-done(((bf16[128,8,640]{2,0,1:T(8,128)(2,1)}), bf16[128,8,640]{2,0,1:T(8,128)(2,1)S(1)}, u32[]{:S(2)}, u32[]{:S(2)}) %all-to-all-start.1) | async-done | bytes 1310752 | tf_op jit(solution)/shard_map/all_to_all | solution.py:47
  27.9 4.3 %all-to-all-start.3 = ((bf16[128,8,640]{2,0,1:T(8,128)(2,1)}), bf16[128,8,640]{2,0,1:T(8,128)(2,1)S(1)}, u32[]{:S(2)}, u32[]{:S(2)}) async-start(bf16[128,8,640]{2,0,1:T(8,128)(2,1)} %bitcast.93), calls=%async_computation.3 | async-start | bytes 2621440 | tf_op jit(solution)/shard_map/all_to_all | solution.py:48
  34.1 16.1 %all-to-all-done.3 = bf16[128,8,640]{2,0,1:T(8,128)(2,1)S(1)} async-done(((bf16[128,8,640]{2,0,1:T(8,128)(2,1)}), bf16[128,8,640]{2,0,1:T(8,128)(2,1)S(1)}, u32[]{:S(2)}, u32[]{:S(2)}) %all-to-all-start.3) | async-done | bytes 1310752 | tf_op jit(solution)/shard_map/all_to_all | solution.py:48
  50.2 10.3 %all-to-all-start.2 = ((bf16[32,32,640]{2,1,0:T(8,128)(2,1)}), bf16[32,32,640]{2,1,0:T(8,128)(2,1)S(1)}, u32[]{:S(2)}, u32[]{:S(2)}) async-start(bf16[32,32,640]{2,1,0:T(8,128)(2,1)} %gather_fusion), calls=%async_computation.2 | async-start | bytes 2621440 | tf_op jit(solution)/shard_map/all_to_all | solution.py:76
  62.2 28.3 %all-to-all-done.2 = bf16[32,32,640]{2,1,0:T(8,128)(2,1)S(1)} async-done(((bf16[32,32,640]{2,1,0:T(8,128)(2,1)}), bf16[32,32,640]{2,1,0:T(8,128)(2,1)S(1)}, u32[]{:S(2)}, u32[]{:S(2)}) %all-to-all-start.2) | async-done | bytes 1310752 | tf_op jit(solution)/shard_map/all_to_all | solution.py:76
  90.6 8.7 %all-to-all-start.4 = ((bf16[32,32,640]{2,1,0:T(8,128)(2,1)}), bf16[32,32,640]{2,1,0:T(8,128)(2,1)S(1)}, u32[]{:S(2)}, u32[]{:S(2)}) async-start(bf16[32,32,640]{2,1,0:T(8,128)(2,1)} %gather_fusion.2), calls=%async_computation.4 | async-start | bytes 2621440 | tf_op jit(solution)/shard_map/all_to_all | solution.py:77
  99.3 2.5 copy.114
  101.8 28.6 %all-to-all-done.4 = bf16[32,32,640]{2,1,0:T(8,128)(2,1)S(1)} async-done(((bf16[32,32,640]{2,1,0:T(8,128)(2,1)}), bf16[32,32,640]{2,1,0:T(8,128)(2,1)S(1)}, u32[]{:S(2)}, u32[]{:S(2)}) %all-to-all-start.4) | async-done | bytes 1310752 | tf_op jit(solution)/shard_map/all_to_all | solution.py:77
  131.5 7.4 %all-to-all-start = ((bf16[128,8,640]{2,0,1:T(8,128)(2,1)}), bf16[128,8,640]{2,0,1:T(8,128)(2,1)S(1)}, u32[]{:S(2)}, u32[]{:S(2)}) async-start(bf16[128,8,640]{2,0,1:T(8,128)(2,1)} %bitcast.76), calls=%async_computation | async-start | bytes 2621440 | tf_op jit(solution)/shard_map/all_to_all | solution.py:46
  140.3 2.5 copy.111
  144.5 2.8 gather_fusion.3
  150.9 6.0 %all-to-all-done = bf16[128,8,640]{2,0,1:T(8,128)(2,1)S(1)} async-done(((bf16[128,8,640]{2,0,1:T(8,128)(2,1)}), bf16[128,8,640]{2,0,1:T(8,128)(2,1)S(1)}, u32[]{:S(2)}, u32[]{:S(2)}) %all-to-all-start) | async-done | bytes 1310752 | tf_op jit(solution)/shard_map/all_to_all | solution.py:46
  156.8 5.0 %all-to-all-start.5 = ((bf16[128,8,640]{2,0,1:T(8,128)(2,1)}), bf16[128,8,640]{2,0,1:T(8,128)(2,1)}, u32[]{:S(2)}, u32[]{:S(2)}) async-start(bf16[128,8,640]{2,0,1:T(8,128)(2,1)} %bitcast.92), calls=%async_computation.5 | async-start | bytes 2621440 | tf_op jit(solution)/shard_map/all_to_all | solution.py:49
  163.0 31.0 %while.32 = (s32[]{:T(128)}, bf16[1024,640]{1,0:T(8,128)(2,1)}, f32[5,1024]{1,0:T(8,128)S(1)}, pred[1536]{0:T(1024)(128)(4,1)S(1)}, bf16[1024,640]{1,0:T(8,128)(...) while((s32[]{:T(128)}, bf16[1024,640]{1,0:T(8,128)(2,1)}, ...), condition=%wide.region_4.5_spmd, body=%wide.region_1.4_spmd.sunk | while | flops 824310784 | bytes 20233384 | solution.py:94
  165.5 3.6 fusion.95
  171.7 3.6 fusion.95
  177.9 3.6 fusion.95
  184.1 3.6 fusion.95
  190.3 3.6 fusion.95
  195.2 2.1 broadcast.160.clone
  197.3 2.1 broadcast.160
  199.4 60.8 %while.33 = (s32[]{:T(128)}, bf16[1024,640]{1,0:T(8,128)(2,1)}, f32[1536,640]{1,0:T(8,128)}, f32[1536,640]{1,0:T(8,128)}, pred[1536]{0:T(1024)(128)(4,1)S(1)}, /...) while((s32[]{:T(128)}, bf16[1024,640]{1,0:T(8,128)(2,1)}, ...), condition=%wide.region_7.8_spmd, body=%wide.region_5.7_spmd.sunk | while | flops 2029976576 | bytes 32932044 | solution.py:122
  201.7 2.8 multiply_convert_fusion.2
  204.5 3.4 fusion.109
  213.8 2.8 multiply_convert_fusion.2
  216.6 3.4 fusion.109
  225.9 2.8 multiply_convert_fusion.2
  228.7 3.4 fusion.109
  238.1 2.8 multiply_convert_fusion.2
  240.9 3.4 fusion.109
  246.0 2.1 fusion.108
  250.3 2.8 multiply_convert_fusion.2
  253.1 3.4 fusion.109
  260.2 4.8 %all-to-all-start.6 = ((bf16[8,128,640]{2,1,0:T(8,128)(2,1)}), bf16[8,128,640]{2,1,0:T(8,128)(2,1)S(1)}, u32[]{:S(2)}, u32[]{:S(2)}) async-start(bf16[8,128,640]{2,1,0:T(8,128)(2,1)} %bitcast.97), calls=%async_computation.6 | async-start | bytes 2621440 | tf_op jit(solution)/shard_map/all_to_all | solution.py:158
  268.5 14.4 %all-to-all-done.6 = bf16[8,128,640]{2,1,0:T(8,128)(2,1)S(1)} async-done(((bf16[8,128,640]{2,1,0:T(8,128)(2,1)}), bf16[8,128,640]{2,1,0:T(8,128)(2,1)S(1)}, u32[]{:S(2)}, u32[]{:S(2)}) %all-to-all-start.6) | async-done | bytes 1310752 | tf_op jit(solution)/shard_map/all_to_all | solution.py:158
  282.9 5.1 %all-to-all-start.9 = ((bf16[32,32,640]{2,1,0:T(8,128)(2,1)}), bf16[32,32,640]{2,1,0:T(8,128)(2,1)S(1)}, u32[]{:S(2)}, u32[]{:S(2)}) async-start(bf16[32,32,640]{2,1,0:T(8,128)(2,1)} %copy.81), calls=%async_computation.9 | async-start | bytes 2621440 | tf_op jit(solution)/shard_map/all_to_all | solution.py:144
  291.6 26.4 %all-to-all-done.9 = bf16[32,32,640]{2,1,0:T(8,128)(2,1)S(1)} async-done(((bf16[32,32,640]{2,1,0:T(8,128)(2,1)}), bf16[32,32,640]{2,1,0:T(8,128)(2,1)S(1)}, u32[]{:S(2)}, u32[]{:S(2)}) %all-to-all-start.9) | async-done | bytes 1310752 | tf_op jit(solution)/shard_map/all_to_all | solution.py:144
  319.0 8.7 %all-to-all-start.7 = ((bf16[32,32,640]{2,1,0:T(8,128)(2,1)}), bf16[32,32,640]{2,1,0:T(8,128)(2,1)S(1)}, u32[]{:S(2)}, u32[]{:S(2)}) async-start(bf16[32,32,640]{2,1,0:T(8,128)(2,1)} %copy.75), calls=%async_computation.7 | async-start | bytes 2621440 | tf_op jit(solution)/shard_map/all_to_all | solution.py:143
  327.8 2.0 slice.16
  333.3 25.6 %all-to-all-done.7 = bf16[32,32,640]{2,1,0:T(8,128)(2,1)S(1)} async-done(((bf16[32,32,640]{2,1,0:T(8,128)(2,1)}), bf16[32,32,640]{2,1,0:T(8,128)(2,1)S(1)}, u32[]{:S(2)}, u32[]{:S(2)}) %all-to-all-start.7) | async-done | bytes 1310752 | tf_op jit(solution)/shard_map/all_to_all | solution.py:143
  359.9 7.4 %all-to-all-start.10 = ((bf16[8,128,640]{2,1,0:T(8,128)(2,1)}), bf16[8,128,640]{2,1,0:T(8,128)(2,1)S(1)}, u32[]{:S(2)}, u32[]{:S(2)}) async-start(bf16[8,128,640]{2,1,0:T(8,128)(2,1)} %bitcast.95), calls=%async_computation.10 | async-start | bytes 2621440 | tf_op jit(solution)/shard_map/all_to_all | solution.py:160
  367.4 2.0 slice.14
  372.9 12.3 %all-to-all-done.10 = bf16[8,128,640]{2,1,0:T(8,128)(2,1)S(1)} async-done(((bf16[8,128,640]{2,1,0:T(8,128)(2,1)}), bf16[8,128,640]{2,1,0:T(8,128)(2,1)S(1)}, u32[]{:S(2)}, u32[]{:S(2)}) %all-to-all-start.10) | async-done | bytes 1310752 | tf_op jit(solution)/shard_map/all_to_all | solution.py:160
  385.3 5.0 %all-to-all-start.8 = ((bf16[8,128,640]{2,1,0:T(8,128)(2,1)}), bf16[8,128,640]{2,1,0:T(8,128)(2,1)}, u32[]{:S(2)}, u32[]{:S(2)}) async-start(bf16[8,128,640]{2,1,0:T(8,128)(2,1)} %bitcast.96), calls=%async_computation.8 | async-start | bytes 2621440 | tf_op jit(solution)/shard_map/all_to_all | solution.py:159
  391.8 2.4 copy.86
  396.4 11.9 %all-to-all-done.8 = bf16[8,128,640]{2,1,0:T(8,128)(2,1)} async-done(((bf16[8,128,640]{2,1,0:T(8,128)(2,1)}), bf16[8,128,640]{2,1,0:T(8,128)(2,1)}, u32[]{:S(2)}, u32[]{:S(2)}) %all-to-all-start.8) | async-done | bytes 1310752 | tf_op jit(solution)/shard_map/all_to_all | solution.py:159
  (109 shorter events, 78.2 us)
Async XLA Ops:
  3.1 6.8 %copy-start.11 = (bf16[128,5120]{1,0:T(8,128)(2,1)S(1)}, bf16[128,5120]{1,0:T(8,128)(2,1)}, u32[]{:S(2)}) copy-start(bf16[128,5120]{1,0:T(8,128)(2,1)} %param.12) | copy-start | bytes 3932164
  3.1 24.8 %all-to-all-start.1 = ((bf16[128,8,640]{2,0,1:T(8,128)(2,1)}), bf16[128,8,640]{2,0,1:T(8,128)(2,1)S(1)}, u32[]{:S(2)}, u32[]{:S(2)}) async-start(bf16[128,8,640]{2,0,1:T(8,128)(2,1)} %bitcast.75), calls=%async_computation.1 | async-start | bytes 2621440 | tf_op jit(solution)/shard_map/all_to_all | solution.py:47
  11.2 21.1 %copy-start.12 = (s32[32,16]{0,1:T(8,128)S(1)}, s32[32,16]{0,1:T(8,128)}, u32[]{:S(2)}) copy-start(s32[32,16]{0,1:T(8,128)} %param.14) | copy-start | bytes 6148
  11.2 21.1 %copy-start.13 = (s32[32]{0:T(128)S(1)}, s32[32]{0:T(128)}, u32[]{:S(2)}) copy-start(s32[32]{0:T(128)} %param.15) | copy-start | bytes 388
  27.9 6.2 %copy-start = (bf16[128,8,640]{2,0,1:T(8,128)(2,1)}, bf16[128,8,640]{2,0,1:T(8,128)(2,1)S(1)}, u32[]{:S(2)}) copy-start(bf16[128,8,640]{2,0,1:T(8,128)(2,1)S(1)} %all-to-all-done.1) | copy-start | bytes 3932164
  27.9 22.3 %all-to-all-start.3 = ((bf16[128,8,640]{2,0,1:T(8,128)(2,1)}), bf16[128,8,640]{2,0,1:T(8,128)(2,1)S(1)}, u32[]{:S(2)}, u32[]{:S(2)}) async-start(bf16[128,8,640]{2,0,1:T(8,128)(2,1)} %bitcast.93), calls=%async_computation.3 | async-start | bytes 2621440 | tf_op jit(solution)/shard_map/all_to_all | solution.py:48
  50.2 12.1 %copy-start.1 = (bf16[128,8,640]{2,0,1:T(8,128)(2,1)}, bf16[128,8,640]{2,0,1:T(8,128)(2,1)S(1)}, u32[]{:S(2)}) copy-start(bf16[128,8,640]{2,0,1:T(8,128)(2,1)S(1)} %all-to-all-done.3) | copy-start | bytes 3932164
  50.2 40.4 %all-to-all-start.2 = ((bf16[32,32,640]{2,1,0:T(8,128)(2,1)}), bf16[32,32,640]{2,1,0:T(8,128)(2,1)S(1)}, u32[]{:S(2)}, u32[]{:S(2)}) async-start(bf16[32,32,640]{2,1,0:T(8,128)(2,1)} %gather_fusion), calls=%async_computation.2 | async-start | bytes 2621440 | tf_op jit(solution)/shard_map/all_to_all | solution.py:76
  90.6 11.2 %copy-start.7 = (bf16[32,32,640]{2,1,0:T(8,128)(2,1)}, bf16[32,32,640]{2,1,0:T(8,128)(2,1)S(1)}, u32[]{:S(2)}) copy-start(bf16[32,32,640]{2,1,0:T(8,128)(2,1)S(1)} %all-to-all-done.2) | copy-start | bytes 3932164
  90.6 39.9 %all-to-all-start.4 = ((bf16[32,32,640]{2,1,0:T(8,128)(2,1)}), bf16[32,32,640]{2,1,0:T(8,128)(2,1)S(1)}, u32[]{:S(2)}, u32[]{:S(2)}) async-start(bf16[32,32,640]{2,1,0:T(8,128)(2,1)} %gather_fusion.2), calls=%async_computation.4 | async-start | bytes 2621440 | tf_op jit(solution)/shard_map/all_to_all | solution.py:77
  130.4 1.1 copy-start.9
  131.5 25.3 %all-to-all-start = ((bf16[128,8,640]{2,0,1:T(8,128)(2,1)}), bf16[128,8,640]{2,0,1:T(8,128)(2,1)S(1)}, u32[]{:S(2)}, u32[]{:S(2)}) async-start(bf16[128,8,640]{2,0,1:T(8,128)(2,1)} %bitcast.76), calls=%async_computation | async-start | bytes 2621440 | tf_op jit(solution)/shard_map/all_to_all | solution.py:46
  138.9 4.1 %copy-start.8 = (bf16[32,32,640]{2,1,0:T(8,128)(2,1)S(1)}, bf16[32,32,640]{2,1,0:T(8,128)(2,1)}, u32[]{:S(2)}) copy-start(bf16[32,32,640]{2,1,0:T(8,128)(2,1)} %copy-done.7) | copy-start | bytes 3932164
  147.3 1.9 copy-start.2
  147.3 2.1 copy-start.10
  156.8 37.2 %all-to-all-start.5 = ((bf16[128,8,640]{2,0,1:T(8,128)(2,1)}), bf16[128,8,640]{2,0,1:T(8,128)(2,1)}, u32[]{:S(2)}, u32[]{:S(2)}) async-start(bf16[128,8,640]{2,0,1:T(8,128)(2,1)} %bitcast.92), calls=%async_computation.5 | async-start | bytes 2621440 | tf_op jit(solution)/shard_map/all_to_all | solution.py:49
  260.2 22.7 %all-to-all-start.6 = ((bf16[8,128,640]{2,1,0:T(8,128)(2,1)}), bf16[8,128,640]{2,1,0:T(8,128)(2,1)S(1)}, u32[]{:S(2)}, u32[]{:S(2)}) async-start(bf16[8,128,640]{2,1,0:T(8,128)(2,1)} %bitcast.97), calls=%async_computation.6 | async-start | bytes 2621440 | tf_op jit(solution)/shard_map/all_to_all | solution.py:158
  282.9 35.0 %all-to-all-start.9 = ((bf16[32,32,640]{2,1,0:T(8,128)(2,1)}), bf16[32,32,640]{2,1,0:T(8,128)(2,1)S(1)}, u32[]{:S(2)}, u32[]{:S(2)}) async-start(bf16[32,32,640]{2,1,0:T(8,128)(2,1)} %copy.81), calls=%async_computation.9 | async-start | bytes 2621440 | tf_op jit(solution)/shard_map/all_to_all | solution.py:144
  317.9 1.1 copy-start.5
  319.0 39.9 %all-to-all-start.7 = ((bf16[32,32,640]{2,1,0:T(8,128)(2,1)}), bf16[32,32,640]{2,1,0:T(8,128)(2,1)S(1)}, u32[]{:S(2)}, u32[]{:S(2)}) async-start(bf16[32,32,640]{2,1,0:T(8,128)(2,1)} %copy.75), calls=%async_computation.7 | async-start | bytes 2621440 | tf_op jit(solution)/shard_map/all_to_all | solution.py:143
  327.7 2.1 copy-start.6
  358.9 1.1 copy-start.3
  359.9 25.3 %all-to-all-start.10 = ((bf16[8,128,640]{2,1,0:T(8,128)(2,1)}), bf16[8,128,640]{2,1,0:T(8,128)(2,1)S(1)}, u32[]{:S(2)}, u32[]{:S(2)}) async-start(bf16[8,128,640]{2,1,0:T(8,128)(2,1)} %bitcast.95), calls=%async_computation.10 | async-start | bytes 2621440 | tf_op jit(solution)/shard_map/all_to_all | solution.py:160
  367.4 2.1 copy-start.4
  385.3 23.0 %all-to-all-start.8 = ((bf16[8,128,640]{2,1,0:T(8,128)(2,1)}), bf16[8,128,640]{2,1,0:T(8,128)(2,1)}, u32[]{:S(2)}, u32[]{:S(2)}) async-start(bf16[8,128,640]{2,1,0:T(8,128)(2,1)} %bitcast.96), calls=%async_computation.8 | async-start | bytes 2621440 | tf_op jit(solution)/shard_map/all_to_all | solution.py:159
where the time goes:
time: 413 us; the launch traced here: 412 us
  waiting for transfers between devices  186 us (45%)
  matrix products  83.3 us (20%)
  starting transfers between devices  73.7 us (18%)
  local copies, waits for them, and re-layouts  49.9 us (12%)
  other arithmetic  17.2 us (4%)
    all_to_all x1, waiting for transfers between devices, body(): lax.all_to_all(outgoing(v_head), 'tok', split_axis=0, concat_axis=0, tile...  28.6 us
    all_to_all x1, waiting for transfers between devices, body(): lax.all_to_all(outgoing(k_head), 'tok', split_axis=0, concat_axis=0, tile...  28.3 us
    all_to_all x1, waiting for transfers between devices, body(): lax.all_to_all(returning(dv_all), 'tok', split_axis=0, concat_axis=0, til...  26.4 us
    all_to_all x1, waiting for transfers between devices, body(): lax.all_to_all(returning(dk_all), 'tok', split_axis=0, concat_axis=0, til...  25.6 us
    dot_general x5, matrix products, head_forward(): jnp.dot(weights, vh, preferred_element_type=jnp.float32)  18.1 us
    dot_general x5, matrix products, head_backward(): dvalue = jnp.dot(weights.T, dh, preferred_element_type=jnp.float32)  17.1 us
    all_to_all x1, waiting for transfers between devices, body(): lax.all_to_all(key, 'head', split_axis=1, concat_axis=0, tiled=True)  16.7 us
    all_to_all x1, waiting for transfers between devices, body(): lax.all_to_all(value, 'head', split_axis=1, concat_axis=0, tiled=True)  16.1 us
  transfers between devices with their start and end apart: 11, of which 10 were waited for; matrix products, arithmetic and copies ran while one was open for 18% of the time, Pallas kernels for 0%

commit v1 on v0

v1 whole, which is shorter than its diff:
```python
import functools
import math

import jax
import jax.numpy as jnp
from jax import lax
from jax.experimental import pallas as pl
from jax.experimental.pallas import tpu as pltpu
from jax.sharding import PartitionSpec as P

HD = 128
FBLK = 32
SCALE = 1.0 / math.sqrt(HD)
LOG2E = math.log2(math.e)
VMEM_LIMIT = 48 * 2**20
NN = (((1,), (0,)), ((), ()))
NT = (((1,), (1,)), ((), ()))
TN = (((0,), (0,)), ((), ()))
F32 = jnp.float32
BF16 = jnp.bfloat16


def in_vmem():
    return pl.BlockSpec(memory_space=pltpu.VMEM)


def in_smem():
    return pl.BlockSpec(memory_space=pltpu.SMEM)


def dot(a, b, dims):
    return lax.dot_general(a, b, dims, preferred_element_type=F32)


def attend_kernel(pieces, memd, tq, kc, lists_ref, kv_ref, *refs):
    qd_refs, recv_ref = refs[:pieces], refs[pieces]
    dq_ref, own_ref, ret_ref = refs[pieces + 1 : pieces + 4]
    k_s, v_s, q_s, d_s, s_s, e_s, gk_s, gv_s = refs[pieces + 4 :]
    tok = kv_ref.shape[2]
    own = tok * pieces
    total = own + memd * FBLK
    count = lists_ref[memd]

    def head(h, _):
        hs = pl.ds(pl.multiple_of(h * HD, HD), HD)
        for i in range(pieces):
            rows = slice(i * tok, (i + 1) * tok)
            k_s[rows] = kv_ref[i, 0, :, hs]
            v_s[rows] = kv_ref[i, 1, :, hs]
            q_s[rows] = qd_refs[i][0, :, hs]
            d_s[rows] = qd_refs[i][1, :, hs]
        for j in range(memd):
            rows = slice(own + j * FBLK, own + (j + 1) * FBLK)
            k_s[rows] = recv_ref[lists_ref[j], 0, :, hs]
            v_s[rows] = recv_ref[lists_ref[j], 1, :, hs]

        def tile(t, _):
            qs = pl.ds(pl.multiple_of(t * tq, tq), tq)
            q, d = q_s[qs, :], d_s[qs, :]
            top = jnp.full((1, tq), -jnp.inf, F32)
            for c in range(0, total, kc):
                s = dot(k_s[c : c + kc], q, NT)
                if c + kc > own:
                    entry = (lax.broadcasted_iota(jnp.int32, (kc, tq), 0) + (c - own)) // FBLK
                    s = jnp.where(entry < count, s, -jnp.inf)
                s_s[c : c + kc] = s
                top = jnp.maximum(top, jnp.max(s, axis=0, keepdims=True))
            norm = jnp.zeros((1, tq), F32)
            delta = jnp.zeros((1, tq), F32)
            for c in range(0, total, kc):
                e = jnp.exp2((s_s[c : c + kc] - top) * (SCALE * LOG2E))
                dp = dot(v_s[c : c + kc], d, NT)
                s_s[c : c + kc] = e
                e_s[c : c + kc] = dp
                norm = norm + jnp.sum(e, axis=0, keepdims=True)
                delta = delta + jnp.sum(e * dp, axis=0, keepdims=True)
            inv = 1.0 / norm
            delta = delta * inv
            dq = jnp.zeros((tq, HD), F32)
            for c in range(0, total, kc):
                p = s_s[c : c + kc] * inv
                ds = (p * (e_s[c : c + kc] - delta)).astype(BF16)
                gv = dot(p.astype(BF16), d, NN)
                gk = dot(ds, q, NN)
                gk_s[c : c + kc] = jnp.where(t == 0, gk, gk_s[c : c + kc] + gk)
                gv_s[c : c + kc] = jnp.where(t == 0, gv, gv_s[c : c + kc] + gv)
                dq = dq + dot(ds, k_s[c : c + kc], TN)
            dq_ref[qs, hs] = (dq * SCALE).astype(BF16)
            return 0

        lax.fori_loop(0, own // tq, tile, 0)
        own_ref[0, :, hs] = gk_s[:own] * SCALE
        own_ref[1, :, hs] = gv_s[:own]
        for j in range(memd):
            rows = slice(own + j * FBLK, own + (j + 1) * FBLK)

            @pl.when(j < count)
            def _():
                ret_ref[lists_ref[j], 0, :, hs] = (gk_s[rows] * SCALE).astype(BF16)
                ret_ref[lists_ref[j], 1, :, hs] = gv_s[rows].astype(BF16)

        return 0

    lax.fori_loop(0, kv_ref.shape[3] // HD, head, 0)


def attend(lists, kv, qd, recv, tq=512, kc=512):
    pieces, _, tok, width = kv.shape
    memd, slots = lists.shape[0] - 1, recv.shape[0]
    own = pieces * tok
    total = own + memd * FBLK
    return pl.pallas_call(
        functools.partial(attend_kernel, pieces, memd, tq, kc),
        out_shape=(
            jax.ShapeDtypeStruct((own, width), BF16),
            jax.ShapeDtypeStruct((2, own, width), F32),
            jax.ShapeDtypeStruct((slots, 2, FBLK, width), BF16),
        ),
        in_specs=[in_smem()] + [in_vmem()] * (pieces + 2),
        out_specs=(in_vmem(),) * 3,
        scratch_shapes=[
            pltpu.VMEM((total, HD), BF16),
            pltpu.VMEM((total, HD), BF16),
            pltpu.VMEM((own, HD), BF16),
            pltpu.VMEM((own, HD), BF16),
            pltpu.VMEM((total, tq), F32),
            pltpu.VMEM((total, tq), F32),
            pltpu.VMEM((total, HD), F32),
            pltpu.VMEM((total, HD), F32),
        ],
        compiler_params=pltpu.CompilerParams(vmem_limit_bytes=VMEM_LIMIT),
        cost_estimate=pl.CostEstimate(
            flops=10 * own * total * width, bytes_accessed=16 * own * width, transcendentals=own * total * width // HD
        ),
        name="attend",
    )(lists, kv, *qd, recv)


def pick_kernel(picks_ref, kv_ref, out_ref):
    def slot(s, _):
        block = picks_ref[s]
        rows = pl.ds(pl.multiple_of(lax.rem(block, 4) * FBLK, FBLK), FBLK)
        out_ref[s] = kv_ref[lax.div(block, 4), :, rows, :]
        return 0

    lax.fori_loop(0, out_ref.shape[0], slot, 0)


def pick(picks, kv, slots):
    return pl.pallas_call(
        pick_kernel,
        out_shape=jax.ShapeDtypeStruct((slots, 2, FBLK, kv.shape[3]), BF16),
        in_specs=[in_smem(), in_vmem()],
        out_specs=in_vmem(),
        compiler_params=pltpu.CompilerParams(vmem_limit_bytes=VMEM_LIMIT),
        name="pick",
    )(picks, kv)


def collect_kernel(picks_ref, wanted_ref, own_ref, back_ref, out_ref, acc):
    acc[...] = own_ref[...]

    def slot(s, _):
        @pl.when(wanted_ref[s] != 0)
        def _():
            rows = pl.ds(pl.multiple_of(picks_ref[s] * FBLK, FBLK), FBLK)
            acc[:, rows, :] += back_ref[s].astype(F32)

        return 0

    lax.fori_loop(0, back_ref.shape[0], slot, 0)
    tok = out_ref.shape[2]
    for i in range(out_ref.shape[0]):
        out_ref[i] = acc[:, i * tok : (i + 1) * tok, :].astype(BF16)


def collect(picks, wanted, own, back, pieces):
    _, rows, width = own.shape
    return pl.pallas_call(
        collect_kernel,
        out_shape=jax.ShapeDtypeStruct((pieces, 2, rows // pieces, width), BF16),
        in_specs=[in_smem(), in_smem(), in_vmem(), in_vmem()],
        out_specs=in_vmem(),
        scratch_shapes=[pltpu.VMEM(own.shape, F32)],
        compiler_params=pltpu.CompilerParams(vmem_limit_bytes=VMEM_LIMIT),
        name="collect",
    )(picks, wanted, own, back)


def place_kernel(count, me_ref, *refs):
    for k, ref in enumerate(refs[:count]):
        width = ref.shape[-1]
        at = pl.multiple_of((me_ref[0] ^ k) * width, HD)
        for i, out_ref in enumerate(refs[count:]):
            out_ref[:, pl.ds(at, width)] = ref[i]


def place(me, pieces):
    arrays, tok, width = pieces[0].shape
    return pl.pallas_call(
        functools.partial(place_kernel, len(pieces)),
        out_shape=[jax.ShapeDtypeStruct((tok, width * len(pieces)), BF16)] * arrays,
        in_specs=[in_smem()] + [in_vmem()] * len(pieces),
        out_specs=[in_vmem()] * arrays,
        compiler_params=pltpu.CompilerParams(vmem_limit_bytes=VMEM_LIMIT),
        name="place",
    )(me, *pieces)


def swap(parts):
    got = {0: parts[0]}
    for k in (4, 5, 2, 3, 6, 7, 1):
        got[k] = lax.ppermute(parts[k], "head", [(i, i ^ k) for i in range(len(parts))])
    return [got[k] for k in range(len(parts))]


def body(query, key, value, out_grad, intersection, counts):
    frames, heads = lax.axis_size("tok"), lax.axis_size("head")
    frame, me = lax.axis_index("tok"), lax.axis_index("head")
    tok, width = query.shape
    cols = width // heads
    blk_tok = tok // FBLK
    blk_dev = blk_tok * heads
    memd = intersection.shape[1]

    def to_heads(a, b):
        return swap(
            [
                jnp.stack([lax.dynamic_slice(x, (0, (me ^ k) * cols), (tok, cols)) for x in (a, b)])
                for k in range(heads)
            ]
        )

    slots = jnp.arange(memd, dtype=jnp.int32)
    live = slots[None, :] < counts[:, None]
    safe = jnp.maximum(intersection, 0)
    mine = live & (safe // blk_dev == frame)
    wanted = jnp.any(mine, axis=1).astype(jnp.int32)
    block = jnp.sum(jnp.where(mine, safe % blk_dev, 0), axis=1)
    picks = ((block // blk_tok) ^ me) * blk_tok + block % blk_tok
    my_ids = lax.dynamic_index_in_dim(safe, frame, 0, keepdims=False) // blk_dev
    my_count = lax.dynamic_index_in_dim(counts, frame, 0, keepdims=True)
    lists = jnp.concatenate([my_ids, my_count])

    kv = jnp.stack(to_heads(key, value))
    sent = pick(picks, kv, frames)
    query, out_grad, sent = lax.optimization_barrier((query, out_grad, sent))
    recv = lax.all_to_all(sent, "tok", split_axis=0, concat_axis=0, tiled=True)
    qd = to_heads(query, out_grad)
    dq, own, ret = attend(lists, kv, qd, recv)
    back = lax.all_to_all(ret, "tok", split_axis=0, concat_axis=0, tiled=True)
    me1 = me[None]
    dq_out = place(me1, swap([dq[None, k * tok : (k + 1) * tok] for k in range(heads)]))
    dkv = collect(picks, wanted, own, back, heads)
    dkv = swap([dkv[k] for k in range(heads)])
    return (*dq_out, *place(me1, dkv))


def solution(mesh):
    rows = P(("tok", "head"), None)
    return jax.shard_map(
        body,
        mesh=mesh,
        in_specs=(rows, rows, rows, rows, P(), P()),
        out_specs=(rows, rows, rows),
        check_vma=False,
    )
```

time: 413 us -> 271 us (0.66)
  matrix products: 83.3 us -> 0 us
  Pallas kernels: 0 us -> 45.8 us
  waiting for transfers between devices: 186 us -> 145 us
  local copies, waits for them, and re-layouts: 49.9 us -> 13.7 us
  starting transfers between devices: 73.7 us -> 60.1 us
  other arithmetic: 17.2 us -> 4.33 us
    all_to_all x11 -> x2, waiting for transfers between devices: 186 us -> 69.7 us  [the longest x1 51.3 us: body(): back = lax.all_to_all(ret, 'tok', split_axis=0, concat_axis=0, tiled=True)]
    dot_general x39 -> x0, matrix products: 83.3 us -> none  [the longest x5 18.1 us: head_forward(): jnp.dot(weights, vh, preferred_element_type=jnp.float32)]
    ppermute x0 -> x28, waiting for transfers between devices: none -> 75.6 us  [swap(): lax.ppermute(parts[k], 'head', [(i, i ^ k) for i in range(len(parts))])]
    all_to_all x11 -> x2, starting transfers between devices: 73.7 us -> 18.5 us  [the longest x1 11.1 us: body(): recv = lax.all_to_all(sent, 'tok', split_axis=0, concat_axis=0, tiled=True)]
    pallas_call x0 -> x5, Pallas kernels: none -> 45.8 us  [the longest x1 36.6 us: attend(): pl.pallas_call(functools.partial(attend_kernel, pieces, memd, tq, kc), ou...]
    ppermute x0 -> x28, starting transfers between devices: none -> 41.6 us  [swap(): lax.ppermute(parts[k], 'head', [(i, i ^ k) for i in range(len(parts))])]
    reduce_sum x10 -> x1, other arithmetic: 13 us -> 0.02 us  [body(): block = jnp.sum(jnp.where(mine, safe % blk_dev, 0), axis=1)]
    all_to_all x7 -> x0, local copies, waits for them, and re-layouts: 12.7 us -> none  [the longest x1 2.52 us: body(): lax.all_to_all(out_grad, 'head', split_axis=1, concat_axis=0, tiled=True)]
  transfers between devices with their start and end apart: 11 -> 30, of which waited for: 10 -> 16; matrix products, arithmetic and copies ran while one was open for 18% -> 6% of each run, Pallas kernels for 0% -> 2%
where the time goes in v1:
time: 271 us; the launch traced here: 270 us
  waiting for transfers between devices  145 us (54%)
  starting transfers between devices  60.1 us (22%)
  Pallas kernels  45.8 us (17%)
  local copies, waits for them, and re-layouts  13.7 us (5%)
  other arithmetic  4.33 us (2%)
    ppermute x28, waiting for transfers between devices, swap(): lax.ppermute(parts[k], 'head', [(i, i ^ k) for i in range(len(parts))])  75.6 us
    all_to_all x1, waiting for transfers between devices, body(): back = lax.all_to_all(ret, 'tok', split_axis=0, concat_axis=0, tiled=True)  51.3 us
    ppermute x28, starting transfers between devices, swap(): lax.ppermute(parts[k], 'head', [(i, i ^ k) for i in range(len(parts))])  41.6 us
    pallas_call x1, Pallas kernels, attend(): pl.pallas_call(functools.partial(attend_kernel, pieces, memd, tq, kc), ou...  36.6 us
    all_to_all x1, waiting for transfers between devices, body(): recv = lax.all_to_all(sent, 'tok', split_axis=0, concat_axis=0, tiled=True)  18.4 us
    all_to_all x1, starting transfers between devices, body(): recv = lax.all_to_all(sent, 'tok', split_axis=0, concat_axis=0, tiled=True)  11.1 us
    all_to_all x1, starting transfers between devices, body(): back = lax.all_to_all(ret, 'tok', split_axis=0, concat_axis=0, tiled=True)  7.32 us
    unnamed x22, local copies, waits for them, and re-layouts  6.34 us
  transfers between devices with their start and end apart: 30, of which 16 were waited for; matrix products, arithmetic and copies ran while one was open for 6% of the time, Pallas kernels for 2%

profile of v1, /device:TPU:1, one launch (start us, length us, event | category | flops | bytes accessed | tf_op | source)
XLA Modules:
  0.0 270.2 jit_solution(4736126685176001326)
XLA Ops:
  0.7 1.6 dynamic-slice_bitcast_fusion.17
  2.7 3.7 %collective-permute-start.5 = (bf16[2,128,640]{2,1,0:T(8,128)(2,1)S(1)}, bf16[2,128,640]{2,1,0:T(8,128)(2,1)}, u32[]{:S(2)}, u32[]{:S(2)}) collective-permute-start(bf16[2,128,640]{2,1,0:T(8,128)(2,1)S(1)} %pad_maximum_fusion.5), channel_id=1, source_target_pairs={{0,6},{1,7},{2,4},{3,5},{4,2},{5,3},{6,0},{7,1},{8,14},{9,15},{10,... | collective-permute-start | bytes 983048 | tf_op jit(solution)/shard_map/ppermute | solution.py:213
  9.6 1.6 collective-permute-start.2
  12.0 1.2 collective-permute-start.3
  13.4 2.2 collective-permute-start.4
  16.7 1.8 collective-permute-done.1
  18.5 2.7 %collective-permute-start.6 = (bf16[2,128,640]{2,1,0:T(8,128)(2,1)S(1)}, bf16[2,128,640]{2,1,0:T(8,128)(2,1)S(1)}, u32[]{:S(2)}, u32[]{:S(2)}) collective-permute-start(bf16[2,128,640]{2,1,0:T(8,128)(2,1)S(1)} %pad_maximum_fusion.6), channel_id=1, source_target_pairs={{0,7},{1,6},{2,5},{3,4},{4,3},{5,2},{6,1},{7,0},{8,15},{9,14},{10,... | collective-permute-start | bytes 983048 | tf_op jit(solution)/shard_map/ppermute | solution.py:213
  21.2 1.0 bitcast_dynamic-update-slice_fusion.5
  22.2 4.0 %collective-permute-done.2 = bf16[2,128,640]{2,1,0:T(8,128)(2,1)} collective-permute-done((bf16[2,128,640]{2,1,0:T(8,128)(2,1)}, bf16[2,128,640]{2,1,0:T(8,128)(2,1)}, u32[]{:S(2)}, u32[]{:S(2)}) %collective-permute-start.2) | collective-permute-done | bytes 327712 | tf_op jit(solution)/shard_map/ppermute | solution.py:213
  26.2 1.0 bitcast_dynamic-update-slice_fusion.4
  27.2 6.8 %collective-permute-done.3 = bf16[2,128,640]{2,1,0:T(8,128)(2,1)} collective-permute-done((bf16[2,128,640]{2,1,0:T(8,128)(2,1)}, bf16[2,128,640]{2,1,0:T(8,128)(2,1)}, u32[]{:S(2)}, u32[]{:S(2)}) %collective-permute-start.3) | collective-permute-done | bytes 327712 | tf_op jit(solution)/shard_map/ppermute | solution.py:213
  33.9 1.0 bitcast_dynamic-update-slice_fusion.3
  35.0 6.1 %collective-permute-done.4 = bf16[2,128,640]{2,1,0:T(8,128)(2,1)S(1)} collective-permute-done((bf16[2,128,640]{2,1,0:T(8,128)(2,1)S(1)}, bf16[2,128,640]{2,1,0:T(8,128)(2,1)S(1)}, u32[]{:S(2)}, u32[]{:S(2)}) %collective-permute-start.4) | collective-permute-done | bytes 327712 | tf_op jit(solution)/shard_map/ppermute | solution.py:213
  41.1 1.0 bitcast_dynamic-update-slice_fusion.1
  42.1 1.5 collective-permute-done.6
  43.7 2.6 pick.1
  46.2 11.1 %all-to-all-start = ((bf16[32,2,32,640]{3,2,1,0:T(8,128)(2,1)}), bf16[32,2,32,640]{3,2,1,0:T(8,128)(2,1)}, u32[]{:S(2)}, u32[]{:S(2)}) async-start(bf16[32,2,32,640]{3,2,1,0:T(8,128)(2,1)} %pick.1), calls=%async_computation | async-start | bytes 5242880 | tf_op jit(solution)/shard_map/all_to_all | solution.py:248
  57.6 2.1 dynamic-slice_bitcast_fusion
  59.7 1.2 collective-permute-start.7
  61.1 1.7 collective-permute-start.9
  63.0 3.4 %collective-permute-start.11 = (bf16[2,128,640]{2,1,0:T(8,128)(2,1)S(1)}, bf16[2,128,640]{2,1,0:T(8,128)(2,1)S(1)}, u32[]{:S(2)}, u32[]{:S(2)}) collective-permute-start(bf16[2,128,640]{2,1,0:T(8,128)(2,1)S(1)} %pad_maximum_fusion.12), channel_id=1, source_target_pairs={{0,5},{1,4},{2,7},{3,6},{4,1},{5,0},{6,3},{7,2},{8,13},{9,12},{10,... | collective-permute-start | bytes 983048 | tf_op jit(solution)/shard_map/ppermute | solution.py:213
  66.7 3.7 %collective-permute-done.8.refs_2_ = bf16[2,128,640]{2,1,0:T(8,128)(2,1)S(1)} collective-permute-done((bf16[2,128,640]{2,1,0:T(8,128)(2,1)S(1)}, bf16[2,128,640]{2,1,0:T(8,128)(2,1)S(1)}, u32[]{:S(2)}, u32[]{:S(2)}) %collective-permute-start.8) | collective-permute-done | bytes 327712 | tf_op jit(solution)/shard_map/ppermute | solution.py:213
  70.5 1.1 collective-permute-start.13
  72.9 5.4 %collective-permute-done.9.refs_3_ = bf16[2,128,640]{2,1,0:T(8,128)(2,1)S(1)} collective-permute-done((bf16[2,128,640]{2,1,0:T(8,128)(2,1)S(1)}, bf16[2,128,640]{2,1,0:T(8,128)(2,1)S(1)}, u32[]{:S(2)}, u32[]{:S(2)}) %collective-permute-start.9) | collective-permute-done | bytes 327712 | tf_op jit(solution)/shard_map/ppermute | solution.py:213
  78.3 6.1 %collective-permute-done.10.refs_4_ = bf16[2,128,640]{2,1,0:T(8,128)(2,1)S(1)} collective-permute-done((bf16[2,128,640]{2,1,0:T(8,128)(2,1)S(1)}, bf16[2,128,640]{2,1,0:T(8,128)(2,1)S(1)}, u32[]{:S(2)}, u32[]{:S(2)}) %collective-permute-start.10) | collective-permute-done | bytes 327712 | tf_op jit(solution)/shard_map/ppermute | solution.py:213
  84.4 7.4 %collective-permute-done.11.refs_5_ = bf16[2,128,640]{2,1,0:T(8,128)(2,1)S(1)} collective-permute-done((bf16[2,128,640]{2,1,0:T(8,128)(2,1)S(1)}, bf16[2,128,640]{2,1,0:T(8,128)(2,1)S(1)}, u32[]{:S(2)}, u32[]{:S(2)}) %collective-permute-start.11) | collective-permute-done | bytes 327712 | tf_op jit(solution)/shard_map/ppermute | solution.py:213
  91.8 6.9 %collective-permute-done.13.refs_7_ = bf16[2,128,640]{2,1,0:T(8,128)(2,1)S(1)} collective-permute-done((bf16[2,128,640]{2,1,0:T(8,128)(2,1)S(1)}, bf16[2,128,640]{2,1,0:T(8,128)(2,1)S(1)}, u32[]{:S(2)}, u32[]{:S(2)}) %collective-permute-start.13) | collective-permute-done | bytes 327712 | tf_op jit(solution)/shard_map/ppermute | solution.py:213
  98.7 18.4 %all-to-all-done.refs_8_ = bf16[32,2,32,640]{3,2,1,0:T(8,128)(2,1)} async-done(((bf16[32,2,32,640]{3,2,1,0:T(8,128)(2,1)}), bf16[32,2,32,640]{3,2,1,0:T(8,128)(2,1)}, u32[]{:S(2)}, u32[]{:S(2)}) %all-to-all-start) | async-done | bytes 2621472 | tf_op jit(solution)/shard_map/all_to_all | solution.py:248
  117.1 36.6 %attend.1 = (bf16[1024,640]{1,0:T(8,128)(2,1)S(1)}, f32[2,1024,640]{2,1,0:T(8,128)}, bf16[32,2,32,640]{3,2,1,0:T(8,128)(2,1)}) custom-call(s32[17]{0:T(128)S(1)} %pad_add_fusion.lists_ref, bf16[8,2,128,640]{3,2,1,0:T(8,128)(2,1)} %copy-done, bf16[2,128,640]{2,1,0:T(8,128)(2,1)S(1)} %pad_maximum_fusion.7.refs_0_, ...), custom_call_target="tpu_custom_call" | custom-call | flops 10066329600 | bytes 10485760 | tf_op jit(solution)/shard_map/attend/pallas_call | solution.py:112
  153.8 1.1 copy-done.1
  154.8 7.3 %all-to-all-start.1 = ((bf16[32,2,32,640]{3,2,1,0:T(8,128)(2,1)}), bf16[32,2,32,640]{3,2,1,0:T(8,128)(2,1)S(1)}, u32[]{:S(2)}, u32[]{:S(2)}) async-start(bf16[32,2,32,640]{3,2,1,0:T(8,128)(2,1)} %get-tuple-element.16), calls=%async_computation.1 | async-start | bytes 5242880 | tf_op jit(solution)/shard_map/all_to_all | solution.py:251
  162.2 2.4 slice_bitcast_fusion.8
  164.6 2.1 collective-permute-start.20
  166.7 1.8 collective-permute-start.19
  168.5 2.3 collective-permute-start.17
  170.8 51.3 %all-to-all-done.1.back_ref = bf16[32,2,32,640]{3,2,1,0:T(8,128)(2,1)S(1)} async-done(((bf16[32,2,32,640]{3,2,1,0:T(8,128)(2,1)}), bf16[32,2,32,640]{3,2,1,0:T(8,128)(2,1)S(1)}, u32[]{:S(2)}, u32[]{:S(2)}) %all-to-all-start.1) | async-done | bytes 2621472 | tf_op jit(solution)/shard_map/all_to_all | solution.py:251
  222.1 3.7 %collect.1 = bf16[8,2,128,640]{3,2,1,0:T(8,128)(2,1)S(1)} custom-call(s32[32]{0:T(128)S(1)} %fusion.7.picks_ref, s32[32]{0:T(128)S(1)} %convert_element_type.3.wanted_ref, f32[2,1024,640]{2,1,0:T(8,128)} %get-tuple-element.15.own_ref, bf16[32,2,32,640]{3,2,1,0:T(8,128)(2,1)S(1)} %all-to-all-done.1.back_ref), custom_call_target="tpu_custom_call" | custom-call | tf_op jit(solution)/shard_map/collect/pallas_call | solution.py:179
  226.1 5.7 %collective-permute-start.27 = (bf16[2,128,640]{2,1,0:T(8,128)(2,1)S(1)}, bf16[2,128,640]{2,1,0:T(8,128)(2,1)S(1)}, u32[]{:S(2)}, u32[]{:S(2)}) collective-permute-start(bf16[2,128,640]{2,1,0:T(8,128)(2,1)S(1)} %get-tuple-element.21), channel_id=1, source_target_pairs={{0,7},{1,6},{2,5},{3,4},{4,3},{5,2},{6,1},{7,0},{8,15},{9,14},{10,... | collective-permute-start | bytes 983048 | tf_op jit(solution)/shard_map/ppermute | solution.py:213
  231.8 1.4 collective-permute-start.26
  233.7 1.6 collective-permute-start.14
  235.4 4.7 %collective-permute-done.16.refs_3_ = bf16[1,128,640]{2,1,0:T(8,128)(2,1)S(1)} collective-permute-done((bf16[1,128,640]{2,1,0:T(8,128)(2,1)S(1)}, bf16[1,128,640]{2,1,0:T(8,128)(2,1)S(1)}, u32[]{:S(2)}, u32[]{:S(2)}) %collective-permute-start.16) | collective-permute-done | bytes 163872 | tf_op jit(solution)/shard_map/ppermute | solution.py:213
  240.6 2.7 collective-permute-start.24
  243.3 2.7 collective-permute-start.23
  246.0 15.1 %collective-permute-done.26.refs_6_ = bf16[2,128,640]{2,1,0:T(8,128)(2,1)S(1)} collective-permute-done((bf16[2,128,640]{2,1,0:T(8,128)(2,1)S(1)}, bf16[2,128,640]{2,1,0:T(8,128)(2,1)S(1)}, u32[]{:S(2)}, u32[]{:S(2)}) %collective-permute-start.26) | collective-permute-done | bytes 327712 | tf_op jit(solution)/shard_map/ppermute | solution.py:213
  261.2 1.2 place.2
  262.3 2.3 collective-permute-done.23.refs_3_
  264.6 3.8 %collective-permute-done.22.refs_2_ = bf16[2,128,640]{2,1,0:T(8,128)(2,1)S(1)} collective-permute-done((bf16[2,128,640]{2,1,0:T(8,128)(2,1)S(1)}, bf16[2,128,640]{2,1,0:T(8,128)(2,1)S(1)}, u32[]{:S(2)}, u32[]{:S(2)}) %collective-permute-start.22) | collective-permute-done | bytes 327712 | tf_op jit(solution)/shard_map/ppermute | solution.py:213
  268.5 1.7 place.3
  (69 shorter events, 9.3 us)
Async XLA Ops:
  0.6 1.8 copy-start.2
  2.5 10.8 %copy-start.6 = (s32[32,16]{0,1:T(8,128)S(1)}, s32[32,16]{0,1:T(8,128)}, u32[]{:S(2)}) copy-start(s32[32,16]{0,1:T(8,128)} %param.10) | copy-start | bytes 6148
  2.5 10.8 %copy-start.7 = (s32[32]{0:T(128)S(1)}, s32[32]{0:T(128)}, u32[]{:S(2)}) copy-start(s32[32]{0:T(128)} %param.11) | copy-start | bytes 388
  2.7 38.4 %collective-permute-start.5 = (bf16[2,128,640]{2,1,0:T(8,128)(2,1)S(1)}, bf16[2,128,640]{2,1,0:T(8,128)(2,1)}, u32[]{:S(2)}, u32[]{:S(2)}) collective-permute-start(bf16[2,128,640]{2,1,0:T(8,128)(2,1)S(1)} %pad_maximum_fusion.5), channel_id=1, source_target_pairs={{0,6},{1,7},{2,4},{3,5},{4,2},{5,3},{6,0},{7,1},{8,14},{9,15},{10,... | collective-permute-start | bytes 983048 | tf_op jit(solution)/shard_map/ppermute | solution.py:213
  7.1 6.3 %collective-permute-start = (bf16[2,128,640]{2,1,0:T(8,128)(2,1)}, bf16[2,128,640]{2,1,0:T(8,128)(2,1)}, u32[]{:S(2)}, u32[]{:S(2)}) collective-permute-start(bf16[2,128,640]{2,1,0:T(8,128)(2,1)} %pad_maximum_fusion), channel_id=1, source_target_pairs={{0,1},{1,0},{2,3},{3,2},{4,5},{5,4},{6,7},{7,6},{8,9},{9,8},{10,11... | collective-permute-start | bytes 983048 | tf_op jit(solution)/shard_map/ppermute | solution.py:213
  8.8 9.7 %collective-permute-start.1 = (bf16[2,128,640]{2,1,0:T(8,128)(2,1)}, bf16[2,128,640]{2,1,0:T(8,128)(2,1)}, u32[]{:S(2)}, u32[]{:S(2)}) collective-permute-start(bf16[2,128,640]{2,1,0:T(8,128)(2,1)} %pad_maximum_fusion.1), channel_id=1, source_target_pairs={{0,2},{1,3},{2,0},{3,1},{4,6},{5,7},{6,4},{7,5},{8,10},{9,11},{10,... | collective-permute-start | bytes 983048 | tf_op jit(solution)/shard_map/ppermute | solution.py:213
  9.6 16.6 %collective-permute-start.2 = (bf16[2,128,640]{2,1,0:T(8,128)(2,1)}, bf16[2,128,640]{2,1,0:T(8,128)(2,1)}, u32[]{:S(2)}, u32[]{:S(2)}) collective-permute-start(bf16[2,128,640]{2,1,0:T(8,128)(2,1)} %pad_maximum_fusion.2), channel_id=1, source_target_pairs={{0,3},{1,2},{2,1},{3,0},{4,7},{5,6},{6,5},{7,4},{8,11},{9,10},{10,... | collective-permute-start | bytes 983048 | tf_op jit(solution)/shard_map/ppermute | solution.py:213
  12.0 22.0 %collective-permute-start.3 = (bf16[2,128,640]{2,1,0:T(8,128)(2,1)}, bf16[2,128,640]{2,1,0:T(8,128)(2,1)}, u32[]{:S(2)}, u32[]{:S(2)}) collective-permute-start(bf16[2,128,640]{2,1,0:T(8,128)(2,1)} %pad_maximum_fusion.3), channel_id=1, source_target_pairs={{0,4},{1,5},{2,6},{3,7},{4,0},{5,1},{6,2},{7,3},{8,12},{9,13},{10,... | collective-permute-start | bytes 983048 | tf_op jit(solution)/shard_map/ppermute | solution.py:213
  13.4 27.6 %collective-permute-start.4 = (bf16[2,128,640]{2,1,0:T(8,128)(2,1)S(1)}, bf16[2,128,640]{2,1,0:T(8,128)(2,1)S(1)}, u32[]{:S(2)}, u32[]{:S(2)}) collective-permute-start(bf16[2,128,640]{2,1,0:T(8,128)(2,1)S(1)} %pad_maximum_fusion.4), channel_id=1, source_target_pairs={{0,5},{1,4},{2,7},{3,6},{4,1},{5,0},{6,3},{7,2},{8,13},{9,12},{10,... | collective-permute-start | bytes 983048 | tf_op jit(solution)/shard_map/ppermute | solution.py:213
  18.5 25.2 %collective-permute-start.6 = (bf16[2,128,640]{2,1,0:T(8,128)(2,1)S(1)}, bf16[2,128,640]{2,1,0:T(8,128)(2,1)S(1)}, u32[]{:S(2)}, u32[]{:S(2)}) collective-permute-start(bf16[2,128,640]{2,1,0:T(8,128)(2,1)S(1)} %pad_maximum_fusion.6), channel_id=1, source_target_pairs={{0,7},{1,6},{2,5},{3,4},{4,3},{5,2},{6,1},{7,0},{8,15},{9,14},{10,... | collective-permute-start | bytes 983048 | tf_op jit(solution)/shard_map/ppermute | solution.py:213
  43.7 2.6 copy-start
  46.2 70.9 %all-to-all-start = ((bf16[32,2,32,640]{3,2,1,0:T(8,128)(2,1)}), bf16[32,2,32,640]{3,2,1,0:T(8,128)(2,1)}, u32[]{:S(2)}, u32[]{:S(2)}) async-start(bf16[32,2,32,640]{3,2,1,0:T(8,128)(2,1)} %pick.1), calls=%async_computation | async-start | bytes 5242880 | tf_op jit(solution)/shard_map/all_to_all | solution.py:248
  59.7 6.8 %collective-permute-start.7 = (bf16[2,128,640]{2,1,0:T(8,128)(2,1)S(1)}, bf16[2,128,640]{2,1,0:T(8,128)(2,1)S(1)}, u32[]{:S(2)}, u32[]{:S(2)}) collective-permute-start(bf16[2,128,640]{2,1,0:T(8,128)(2,1)S(1)} %pad_maximum_fusion.8), channel_id=1, source_target_pairs={{0,1},{1,0},{2,3},{3,2},{4,5},{5,4},{6,7},{7,6},{8,9},{9,8},{10,11... | collective-permute-start | bytes 983048 | tf_op jit(solution)/shard_map/ppermute | solution.py:213
  61.0 9.5 %collective-permute-start.8 = (bf16[2,128,640]{2,1,0:T(8,128)(2,1)S(1)}, bf16[2,128,640]{2,1,0:T(8,128)(2,1)S(1)}, u32[]{:S(2)}, u32[]{:S(2)}) collective-permute-start(bf16[2,128,640]{2,1,0:T(8,128)(2,1)S(1)} %pad_maximum_fusion.9), channel_id=1, source_target_pairs={{0,2},{1,3},{2,0},{3,1},{4,6},{5,7},{6,4},{7,5},{8,10},{9,11},{10,... | collective-permute-start | bytes 983048 | tf_op jit(solution)/shard_map/ppermute | solution.py:213
  61.1 17.2 %collective-permute-start.9 = (bf16[2,128,640]{2,1,0:T(8,128)(2,1)S(1)}, bf16[2,128,640]{2,1,0:T(8,128)(2,1)S(1)}, u32[]{:S(2)}, u32[]{:S(2)}) collective-permute-start(bf16[2,128,640]{2,1,0:T(8,128)(2,1)S(1)} %pad_maximum_fusion.10), channel_id=1, source_target_pairs={{0,3},{1,2},{2,1},{3,0},{4,7},{5,6},{6,5},{7,4},{8,11},{9,10},{10,... | collective-permute-start | bytes 983048 | tf_op jit(solution)/shard_map/ppermute | solution.py:213
  62.9 21.6 %collective-permute-start.10 = (bf16[2,128,640]{2,1,0:T(8,128)(2,1)S(1)}, bf16[2,128,640]{2,1,0:T(8,128)(2,1)S(1)}, u32[]{:S(2)}, u32[]{:S(2)}) collective-permute-start(bf16[2,128,640]{2,1,0:T(8,128)(2,1)S(1)} %pad_maximum_fusion.11), channel_id=1, source_target_pairs={{0,4},{1,5},{2,6},{3,7},{4,0},{5,1},{6,2},{7,3},{8,12},{9,13},{10,... | collective-permute-start | bytes 983048 | tf_op jit(solution)/shard_map/ppermute | solution.py:213
  63.0 28.8 %collective-permute-start.11 = (bf16[2,128,640]{2,1,0:T(8,128)(2,1)S(1)}, bf16[2,128,640]{2,1,0:T(8,128)(2,1)S(1)}, u32[]{:S(2)}, u32[]{:S(2)}) collective-permute-start(bf16[2,128,640]{2,1,0:T(8,128)(2,1)S(1)} %pad_maximum_fusion.12), channel_id=1, source_target_pairs={{0,5},{1,4},{2,7},{3,6},{4,1},{5,0},{6,3},{7,2},{8,13},{9,12},{10,... | collective-permute-start | bytes 983048 | tf_op jit(solution)/shard_map/ppermute | solution.py:213
  66.5 25.3 %collective-permute-start.12 = (bf16[2,128,640]{2,1,0:T(8,128)(2,1)S(1)}, bf16[2,128,640]{2,1,0:T(8,128)(2,1)S(1)}, u32[]{:S(2)}, u32[]{:S(2)}) collective-permute-start(bf16[2,128,640]{2,1,0:T(8,128)(2,1)S(1)} %pad_maximum_fusion.13), channel_id=1, source_target_pairs={{0,6},{1,7},{2,4},{3,5},{4,2},{5,3},{6,0},{7,1},{8,14},{9,15},{10,... | collective-permute-start | bytes 983048 | tf_op jit(solution)/shard_map/ppermute | solution.py:213
  70.5 28.2 %collective-permute-start.13 = (bf16[2,128,640]{2,1,0:T(8,128)(2,1)S(1)}, bf16[2,128,640]{2,1,0:T(8,128)(2,1)S(1)}, u32[]{:S(2)}, u32[]{:S(2)}) collective-permute-start(bf16[2,128,640]{2,1,0:T(8,128)(2,1)S(1)} %pad_maximum_fusion.14), channel_id=1, source_target_pairs={{0,7},{1,6},{2,5},{3,4},{4,3},{5,2},{6,1},{7,0},{8,15},{9,14},{10,... | collective-permute-start | bytes 983048 | tf_op jit(solution)/shard_map/ppermute | solution.py:213
  153.8 1.1 copy-start.1
  154.8 67.2 %all-to-all-start.1 = ((bf16[32,2,32,640]{3,2,1,0:T(8,128)(2,1)}), bf16[32,2,32,640]{3,2,1,0:T(8,128)(2,1)S(1)}, u32[]{:S(2)}, u32[]{:S(2)}) async-start(bf16[32,2,32,640]{3,2,1,0:T(8,128)(2,1)} %get-tuple-element.16), calls=%async_computation.1 | async-start | bytes 5242880 | tf_op jit(solution)/shard_map/all_to_all | solution.py:251
  164.6 67.3 %collective-permute-start.20 = (bf16[1,128,640]{2,1,0:T(8,128)(2,1)}, bf16[1,128,640]{2,1,0:T(8,128)(2,1)S(1)}, u32[]{:S(2)}, u32[]{:S(2)}) collective-permute-start(bf16[1,128,640]{2,1,0:T(8,128)(2,1)} %get-tuple-element.29), channel_id=1, source_target_pairs={{0,7},{1,6},{2,5},{3,4},{4,3},{5,2},{6,1},{7,0},{8,15},{9,14},{10,... | collective-permute-start | bytes 491528 | tf_op jit(solution)/shard_map/ppermute | solution.py:213
  166.7 66.5 %collective-permute-start.19 = (bf16[1,128,640]{2,1,0:T(8,128)(2,1)}, bf16[1,128,640]{2,1,0:T(8,128)(2,1)S(1)}, u32[]{:S(2)}, u32[]{:S(2)}) collective-permute-start(bf16[1,128,640]{2,1,0:T(8,128)(2,1)} %get-tuple-element.30), channel_id=1, source_target_pairs={{0,6},{1,7},{2,4},{3,5},{4,2},{5,3},{6,0},{7,1},{8,14},{9,15},{10,... | collective-permute-start | bytes 491528 | tf_op jit(solution)/shard_map/ppermute | solution.py:213
  168.5 64.7 %collective-permute-start.18 = (bf16[1,128,640]{2,1,0:T(8,128)(2,1)}, bf16[1,128,640]{2,1,0:T(8,128)(2,1)S(1)}, u32[]{:S(2)}, u32[]{:S(2)}) collective-permute-start(bf16[1,128,640]{2,1,0:T(8,128)(2,1)} %get-tuple-element.31), channel_id=1, source_target_pairs={{0,5},{1,4},{2,7},{3,6},{4,1},{5,0},{6,3},{7,2},{8,13},{9,12},{10,... | collective-permute-start | bytes 491528 | tf_op jit(solution)/shard_map/ppermute | solution.py:213
  168.5 65.2 %collective-permute-start.17 = (bf16[1,128,640]{2,1,0:T(8,128)(2,1)}, bf16[1,128,640]{2,1,0:T(8,128)(2,1)S(1)}, u32[]{:S(2)}, u32[]{:S(2)}) collective-permute-start(bf16[1,128,640]{2,1,0:T(8,128)(2,1)} %get-tuple-element.32), channel_id=1, source_target_pairs={{0,4},{1,5},{2,6},{3,7},{4,0},{5,1},{6,2},{7,3},{8,12},{9,13},{10,... | collective-permute-start | bytes 491528 | tf_op jit(solution)/shard_map/ppermute | solution.py:213
  225.8 7.4 %copy-start.5 = (bf16[1,128,640]{2,1,0:T(8,128)(2,1)S(1)}, bf16[1,128,640]{2,1,0:T(8,128)(2,1)}, u32[]{:S(2)}) copy-start(bf16[1,128,640]{2,1,0:T(8,128)(2,1)} %get-tuple-element.33) | copy-start | bytes 491524
  225.8 7.4 %copy-start.4 = (bf16[1,128,640]{2,1,0:T(8,128)(2,1)S(1)}, bf16[1,128,640]{2,1,0:T(8,128)(2,1)}, u32[]{:S(2)}) copy-start(bf16[1,128,640]{2,1,0:T(8,128)(2,1)} %get-tuple-element.34) | copy-start | bytes 491524
  225.8 7.9 %copy-start.3 = (bf16[1,128,640]{2,1,0:T(8,128)(2,1)S(1)}, bf16[1,128,640]{2,1,0:T(8,128)(2,1)}, u32[]{:S(2)}) copy-start(bf16[1,128,640]{2,1,0:T(8,128)(2,1)} %get-tuple-element.35) | copy-start | bytes 491524
  226.1 19.9 %collective-permute-start.27 = (bf16[2,128,640]{2,1,0:T(8,128)(2,1)S(1)}, bf16[2,128,640]{2,1,0:T(8,128)(2,1)S(1)}, u32[]{:S(2)}, u32[]{:S(2)}) collective-permute-start(bf16[2,128,640]{2,1,0:T(8,128)(2,1)S(1)} %get-tuple-element.21), channel_id=1, source_target_pairs={{0,7},{1,6},{2,5},{3,4},{4,3},{5,2},{6,1},{7,0},{8,15},{9,14},{10,... | collective-permute-start | bytes 983048 | tf_op jit(solution)/shard_map/ppermute | solution.py:213
  231.8 29.3 %collective-permute-start.26 = (bf16[2,128,640]{2,1,0:T(8,128)(2,1)S(1)}, bf16[2,128,640]{2,1,0:T(8,128)(2,1)S(1)}, u32[]{:S(2)}, u32[]{:S(2)}) collective-permute-start(bf16[2,128,640]{2,1,0:T(8,128)(2,1)S(1)} %get-tuple-element.22), channel_id=1, source_target_pairs={{0,6},{1,7},{2,4},{3,5},{4,2},{5,3},{6,0},{7,1},{8,14},{9,15},{10,... | collective-permute-start | bytes 983048 | tf_op jit(solution)/shard_map/ppermute | solution.py:213
  233.2 6.9 %collective-permute-start.16 = (bf16[1,128,640]{2,1,0:T(8,128)(2,1)S(1)}, bf16[1,128,640]{2,1,0:T(8,128)(2,1)S(1)}, u32[]{:S(2)}, u32[]{:S(2)}) collective-permute-start(bf16[1,128,640]{2,1,0:T(8,128)(2,1)S(1)} %copy-done.5), channel_id=1, source_target_pairs={{0,3},{1,2},{2,1},{3,0},{4,7},{5,6},{6,5},{7,4},{8,11},{9,10},{10,... | collective-permute-start | bytes 491528 | tf_op jit(solution)/shard_map/ppermute | solution.py:213
  233.2 7.4 %collective-permute-start.15 = (bf16[1,128,640]{2,1,0:T(8,128)(2,1)S(1)}, bf16[1,128,640]{2,1,0:T(8,128)(2,1)S(1)}, u32[]{:S(2)}, u32[]{:S(2)}) collective-permute-start(bf16[1,128,640]{2,1,0:T(8,128)(2,1)S(1)} %copy-done.4), channel_id=1, source_target_pairs={{0,2},{1,3},{2,0},{3,1},{4,6},{5,7},{6,4},{7,5},{8,10},{9,11},{10,... | collective-permute-start | bytes 491528 | tf_op jit(solution)/shard_map/ppermute | solution.py:213
  233.7 9.6 %collective-permute-start.14 = (bf16[1,128,640]{2,1,0:T(8,128)(2,1)S(1)}, bf16[1,128,640]{2,1,0:T(8,128)(2,1)S(1)}, u32[]{:S(2)}, u32[]{:S(2)}) collective-permute-start(bf16[1,128,640]{2,1,0:T(8,128)(2,1)S(1)} %copy-done.3), channel_id=1, source_target_pairs={{0,1},{1,0},{2,3},{3,2},{4,5},{5,4},{6,7},{7,6},{8,9},{9,8},{10,11... | collective-permute-start | bytes 491528 | tf_op jit(solution)/shard_map/ppermute | solution.py:213
  240.1 22.3 %collective-permute-start.25 = (bf16[2,128,640]{2,1,0:T(8,128)(2,1)S(1)}, bf16[2,128,640]{2,1,0:T(8,128)(2,1)S(1)}, u32[]{:S(2)}, u32[]{:S(2)}) collective-permute-start(bf16[2,128,640]{2,1,0:T(8,128)(2,1)S(1)} %get-tuple-element.23), channel_id=1, source_target_pairs={{0,5},{1,4},{2,7},{3,6},{4,1},{5,0},{6,3},{7,2},{8,13},{9,12},{10,... | collective-permute-start | bytes 983048 | tf_op jit(solution)/shard_map/ppermute | solution.py:213
  240.6 21.7 %collective-permute-start.24 = (bf16[2,128,640]{2,1,0:T(8,128)(2,1)S(1)}, bf16[2,128,640]{2,1,0:T(8,128)(2,1)S(1)}, u32[]{:S(2)}, u32[]{:S(2)}) collective-permute-start(bf16[2,128,640]{2,1,0:T(8,128)(2,1)S(1)} %get-tuple-element.24), channel_id=1, source_target_pairs={{0,4},{1,5},{2,6},{3,7},{4,0},{5,1},{6,2},{7,3},{8,12},{9,13},{10,... | collective-permute-start | bytes 983048 | tf_op jit(solution)/shard_map/ppermute | solution.py:213
  243.3 21.3 %collective-permute-start.23 = (bf16[2,128,640]{2,1,0:T(8,128)(2,1)S(1)}, bf16[2,128,640]{2,1,0:T(8,128)(2,1)S(1)}, u32[]{:S(2)}, u32[]{:S(2)}) collective-permute-start(bf16[2,128,640]{2,1,0:T(8,128)(2,1)S(1)} %get-tuple-element.25), channel_id=1, source_target_pairs={{0,3},{1,2},{2,1},{3,0},{4,7},{5,6},{6,5},{7,4},{8,11},{9,10},{10,... | collective-permute-start | bytes 983048 | tf_op jit(solution)/shard_map/ppermute | solution.py:213
  246.0 22.4 %collective-permute-start.22 = (bf16[2,128,640]{2,1,0:T(8,128)(2,1)S(1)}, bf16[2,128,640]{2,1,0:T(8,128)(2,1)S(1)}, u32[]{:S(2)}, u32[]{:S(2)}) collective-permute-start(bf16[2,128,640]{2,1,0:T(8,128)(2,1)S(1)} %get-tuple-element.26), channel_id=1, source_target_pairs={{0,2},{1,3},{2,0},{3,1},{4,6},{5,7},{6,4},{7,5},{8,10},{9,11},{10,... | collective-permute-start | bytes 983048 | tf_op jit(solution)/shard_map/ppermute | solution.py:213
  261.2 7.3 %collective-permute-start.21 = (bf16[2,128,640]{2,1,0:T(8,128)(2,1)S(1)}, bf16[2,128,640]{2,1,0:T(8,128)(2,1)S(1)}, u32[]{:S(2)}, u32[]{:S(2)}) collective-permute-start(bf16[2,128,640]{2,1,0:T(8,128)(2,1)S(1)} %get-tuple-element.27), channel_id=1, source_target_pairs={{0,1},{1,0},{2,3},{3,2},{4,5},{5,4},{6,7},{7,6},{8,9},{9,8},{10,11... | collective-permute-start | bytes 983048 | tf_op jit(solution)/shard_map/ppermute | solution.py:213

commit v2 on v1

v2 whole, which is shorter than its diff:
```python
import functools
import math

import jax
import jax.numpy as jnp
from jax import lax
from jax.experimental import pallas as pl
from jax.experimental.pallas import tpu as pltpu
from jax.sharding import PartitionSpec as P

HD = 128
FBLK = 32
LEAST_LIVE = 12
SCALE = 1.0 / math.sqrt(HD)
TO_EXP2 = SCALE * math.log2(math.e)
VMEM_LIMIT = 40 * 2**20
MOST_VMEM = 60 * 2**20
SMALL_LIMIT = 16 * 2**20
NN = (((1,), (0,)), ((), ()))
NT = (((1,), (1,)), ((), ()))
TN = (((0,), (0,)), ((), ()))
F32 = jnp.float32
BF16 = jnp.bfloat16


def smem():
    return pl.BlockSpec(memory_space=pltpu.SMEM)


def anywhere():
    return pl.BlockSpec(memory_space=pl.ANY)


def per_head(shape):
    lead = len(shape) - 3
    return pl.BlockSpec((*shape[:lead], None, *shape[-2:]), lambda h: (0,) * lead + (h, 0, 0))


def vmem():
    return pl.BlockSpec(memory_space=pltpu.VMEM)


def stat_block(own):
    return pl.BlockSpec((1, 8, own), lambda h: (h, 0, 0))


def params():
    return pltpu.CompilerParams(vmem_limit_bytes=VMEM_LIMIT, dimension_semantics=("arbitrary",))


def dot(a, b, dims):
    return lax.dot_general(a, b, dims, preferred_element_type=F32)


def column_sum(x):
    return jnp.sum(x, axis=0, keepdims=True)


def rows_of(ref, which, lo, count):
    tok = ref.shape[2]
    return ref[which, lo // tok : (lo + count) // tok].reshape(count, HD)


def load_memory(lists_ref, recv_ref, k_s, v_s):
    for j in range(k_s.shape[0] // FBLK):
        k_s[j * FBLK : (j + 1) * FBLK] = recv_ref[lists_ref[j], 0]
        v_s[j * FBLK : (j + 1) * FBLK] = recv_ref[lists_ref[j], 1]


def masked(s, count, first=0):
    row = lax.broadcasted_iota(jnp.int32, s.shape, 0)
    return jnp.where(row < count * FBLK - first, s, -jnp.inf)


def own_stats_kernel(kc, kv_ref, qd_ref, stat_ref, s_s):
    own = s_s.shape[0]
    q, d = rows_of(qd_ref, 0, 0, own), rows_of(qd_ref, 1, 0, own)
    top = jnp.full((1, own), -jnp.inf, F32)
    for c in range(0, own, kc):
        s = dot(rows_of(kv_ref, 0, c, kc), q, NT)
        s_s[c : c + kc] = s
        top = jnp.maximum(top, jnp.max(s, axis=0, keepdims=True))
    norm = jnp.zeros((1, own), F32)
    mix = jnp.zeros((1, own), F32)
    for c in range(0, own, kc):
        e = jnp.exp2((s_s[c : c + kc] - top) * TO_EXP2)
        norm = norm + column_sum(e)
        mix = mix + column_sum(e * dot(rows_of(kv_ref, 1, c, kc), d, NT))
    stat_ref[0, 0:1] = top
    stat_ref[0, 1:2] = norm
    stat_ref[0, 2:3] = mix


def own_stats(kv, qd, kc=1024):
    _, pieces, nh, tok, _ = kv.shape
    own, width = pieces * tok, nh * HD
    return pl.pallas_call(
        functools.partial(own_stats_kernel, kc),
        grid=(nh,),
        out_shape=jax.ShapeDtypeStruct((nh, 8, own), F32),
        in_specs=[per_head(kv.shape), per_head(qd.shape)],
        out_specs=stat_block(own),
        scratch_shapes=[pltpu.VMEM((own, own), F32)],
        compiler_params=params(),
        cost_estimate=pl.CostEstimate(
            flops=4 * own * own * width, bytes_accessed=8 * own * width, transcendentals=own * own * nh
        ),
        name="own_stats",
    )(kv, qd)


def memory_kernel(kc, lists_ref, stat_ref, recv_ref, qd_ref, ret_ref, fin_ref, k_s, v_s):
    mem, own = k_s.shape[0], stat_ref.shape[2]
    count = lists_ref[mem // FBLK]
    load_memory(lists_ref, recv_ref, k_s, v_s)
    q, d = rows_of(qd_ref, 0, 0, own), rows_of(qd_ref, 1, 0, own)
    top_own = stat_ref[0, 0:1]
    top = top_own
    scores = []
    for c in range(0, mem, kc):
        s = dot(k_s[c : c + kc], q, NT)
        if c + kc > LEAST_LIVE * FBLK:
            s = masked(s, count, c)
        top = jnp.maximum(top, jnp.max(s, axis=0, keepdims=True))
        scores.append(s)
    shrink = jnp.exp2((top_own - top) * TO_EXP2)
    norm = stat_ref[0, 1:2] * shrink
    mix = stat_ref[0, 2:3] * shrink
    parts = []
    for i, s in enumerate(scores):
        e = jnp.exp2((s - top) * TO_EXP2)
        dp = dot(v_s[i * kc : (i + 1) * kc], d, NT)
        norm = norm + column_sum(e)
        mix = mix + column_sum(e * dp)
        parts.append((e, dp))
    inv = 1.0 / norm
    delta = mix * inv
    for i, (e, dp) in enumerate(parts):
        p = e * inv
        ds = (p * (dp - delta)).astype(BF16)
        gk = (dot(ds, q, NN) * SCALE).astype(BF16)
        gv = dot(p.astype(BF16), d, NN).astype(BF16)
        for j in range(kc // FBLK):
            rows = slice(j * FBLK, (j + 1) * FBLK)
            at = lists_ref[i * (kc // FBLK) + j]
            if (i + 1) * kc <= LEAST_LIVE * FBLK:
                ret_ref[at, 0] = gk[rows]
                ret_ref[at, 1] = gv[rows]
            else:

                @pl.when(i * (kc // FBLK) + j < count)
                def _():
                    ret_ref[at, 0] = gk[rows]
                    ret_ref[at, 1] = gv[rows]

    fin_ref[0, 0:1] = top
    fin_ref[0, 1:2] = inv
    fin_ref[0, 2:3] = delta


def memory(lists, stat, recv, qd, kc=128):
    mem = (lists.shape[0] - 1) * FBLK
    nh, _, own = stat.shape
    width = nh * HD
    return pl.pallas_call(
        functools.partial(memory_kernel, kc),
        grid=(nh,),
        out_shape=(
            pltpu.HBM(recv.shape, BF16),
            jax.ShapeDtypeStruct((nh, 8, own), F32),
        ),
        in_specs=[smem(), stat_block(own), per_head(recv.shape), per_head(qd.shape)],
        out_specs=(per_head(recv.shape), stat_block(own)),
        scratch_shapes=[pltpu.VMEM((mem, HD), BF16)] * 2,
        compiler_params=params(),
        cost_estimate=pl.CostEstimate(
            flops=8 * own * mem * width, bytes_accessed=8 * own * width, transcendentals=own * mem * nh
        ),
        name="memory",
    )(lists, stat, recv, qd)


def own_grads_kernel(kc, lists_ref, fin_ref, recv_ref, kv_ref, qd_ref, *refs):
    *dq_refs, own_ref, mk_s, mv_s = refs
    own, mem = fin_ref.shape[2], mk_s.shape[0]
    tok = own // len(dq_refs)
    load_memory(lists_ref, recv_ref, mk_s, mv_s)
    q, d = rows_of(qd_ref, 0, 0, own), rows_of(qd_ref, 1, 0, own)
    top, inv, delta = fin_ref[0, 0:1], fin_ref[0, 1:2], fin_ref[0, 2:3]

    def probabilities(k, v, count=None):
        s = dot(k, q, NT)
        if count is not None:
            s = masked(s, count)
        p = jnp.exp2((s - top) * TO_EXP2) * inv
        return p, (p * (dot(v, d, NT) - delta)).astype(BF16)

    _, ds = probabilities(mk_s[...], mv_s[...], lists_ref[mem // FBLK])
    dq = dot(ds, mk_s[...], TN)
    for c in range(0, own, kc):
        k, v = rows_of(kv_ref, 0, c, kc), rows_of(kv_ref, 1, c, kc)
        p, ds = probabilities(k, v)
        dq = dq + dot(ds, k, TN)
        own_ref[0, c : c + kc] = dot(ds, q, NN) * SCALE
        own_ref[1, c : c + kc] = dot(p.astype(BF16), d, NN)
    dq = (dq * SCALE).astype(BF16)
    for i, ref in enumerate(dq_refs):
        ref[0] = dq[i * tok : (i + 1) * tok]


def own_grads(lists, fin, recv, kv, qd, kc=1024):
    _, pieces, nh, tok, _ = kv.shape
    own, width = pieces * tok, nh * HD
    mem = (lists.shape[0] - 1) * FBLK
    total = own + mem
    piece, whole = (1, nh, tok, HD), (2, nh, own, HD)
    *dq, grads = pl.pallas_call(
        functools.partial(own_grads_kernel, kc),
        grid=(nh,),
        out_shape=[pltpu.HBM(piece, BF16)] * pieces + [pltpu.HBM(whole, F32)],
        in_specs=[smem(), stat_block(own), per_head(recv.shape), per_head(kv.shape), per_head(qd.shape)],
        out_specs=[per_head(piece)] * pieces + [per_head(whole)],
        scratch_shapes=[pltpu.VMEM((mem, HD), BF16)] * 2,
        compiler_params=params(),
        cost_estimate=pl.CostEstimate(
            flops=10 * own * total * width, bytes_accessed=16 * own * width, transcendentals=own * total * nh
        ),
        name="own_grads",
    )(lists, fin, recv, kv, qd)
    return dq, grads


def collect_kernel(blocks_ref, own_ref, back_ref, *refs):
    *out_refs, acc = refs
    slots = back_ref.shape[0]
    tok = acc.shape[1] // len(out_refs)
    acc[...] = own_ref[...]
    for s in range(slots):

        @pl.when(blocks_ref[slots + s] != 0)
        def _():
            rows = pl.ds(pl.multiple_of(blocks_ref[s] * FBLK, FBLK), FBLK)
            acc[:, rows, :] += back_ref[s].astype(F32)

    for i, ref in enumerate(out_refs):
        ref[...] = acc[:, i * tok : (i + 1) * tok, :].astype(BF16)


def collect(blocks, own, back, pieces):
    _, nh, rows, _ = own.shape
    piece = (2, nh, rows // pieces, HD)
    return pl.pallas_call(
        collect_kernel,
        grid=(nh,),
        out_shape=[jax.ShapeDtypeStruct(piece, BF16)] * pieces,
        in_specs=[smem(), per_head(own.shape), per_head(back.shape)],
        out_specs=[per_head(piece)] * pieces,
        scratch_shapes=[pltpu.VMEM((2, rows, HD), F32)],
        compiler_params=params(),
        name="collect",
    )(blocks, own, back)


def pick_kernel(blocks_ref, kv_ref, out_ref, sems):
    per = kv_ref.shape[3] // FBLK
    copies = []
    for s in range(out_ref.shape[0]):
        block = blocks_ref[s]
        rows = pl.ds(pl.multiple_of(lax.rem(block, per) * FBLK, FBLK), FBLK)
        copies.append(
            pltpu.make_async_copy(kv_ref.at[:, lax.div(block, per), :, rows, :], out_ref.at[s], sems.at[s])
        )
    for copy in copies:
        copy.start()
    for copy in copies:
        copy.wait()


def pick(blocks, kv, slots):
    _, _, nh, _, _ = kv.shape
    return pl.pallas_call(
        pick_kernel,
        out_shape=pltpu.HBM((slots, 2, nh, FBLK, HD), BF16),
        in_specs=[smem(), vmem()],
        out_specs=anywhere(),
        scratch_shapes=[pltpu.SemaphoreType.DMA((slots,))],
        compiler_params=pltpu.CompilerParams(vmem_limit_bytes=SMALL_LIMIT),
        name="pick",
    )(blocks, kv)


def cut_kernel(me_ref, a_ref, b_ref, *refs):
    *out_refs, wide, sems = refs
    count = len(out_refs)
    width = wide.shape[3]
    copies = []
    for k in range(count):
        columns = pl.ds(pl.multiple_of(lax.rem(me_ref[0] + k, count) * width, HD), width)
        for i, ref in enumerate((a_ref, b_ref)):
            copies.append(pltpu.make_async_copy(ref.at[:, columns], wide.at[k, i], sems.at[k, i]))
    for copy in copies:
        copy.start()
    for k, out_ref in enumerate(out_refs):
        for i in range(2):
            copies[2 * k + i].wait()
            for h in range(width // HD):
                out_ref[i, h] = wide[k, i, :, h * HD : (h + 1) * HD]


def cut(me, a, b, count):
    tok, width = a.shape
    width //= count
    return pl.pallas_call(
        cut_kernel,
        out_shape=[jax.ShapeDtypeStruct((2, width // HD, tok, HD), BF16)] * count,
        in_specs=[smem(), anywhere(), anywhere()],
        out_specs=[vmem()] * count,
        scratch_shapes=[pltpu.VMEM((count, 2, tok, width), BF16), pltpu.SemaphoreType.DMA((count, 2))],
        compiler_params=pltpu.CompilerParams(vmem_limit_bytes=MOST_VMEM),
        name="cut",
    )(me, a, b)


def place_kernel(count, me_ref, *refs):
    for k, ref in enumerate(refs[:count]):
        heads = ref.shape[1]
        of = lax.rem(me_ref[0] + k, count)
        for h in range(heads):
            columns = pl.ds(pl.multiple_of((of * heads + h) * HD, HD), HD)
            for i, out_ref in enumerate(refs[count:]):
                out_ref[:, columns] = ref[i, h]


def place(me, pieces):
    arrays, nh, tok, _ = pieces[0].shape
    count = len(pieces)
    return pl.pallas_call(
        functools.partial(place_kernel, count),
        out_shape=[jax.ShapeDtypeStruct((tok, nh * HD * count), BF16)] * arrays,
        in_specs=[smem()] + [vmem()] * count,
        out_specs=[vmem()] * arrays,
        compiler_params=pltpu.CompilerParams(vmem_limit_bytes=SMALL_LIMIT),
        name="place",
    )(me, *pieces)


def shift(parts, sign):
    n = len(parts)
    got = {0: parts[0]}
    for k in (1, 7, 2, 6, 3, 5, 4):
        got[k] = lax.ppermute(parts[k], "head", [(i, (i + sign * k) % n) for i in range(n)])
    return [got[k] for k in range(n)]


def body(query, key, value, out_grad, intersection, counts):
    frames, heads = lax.axis_size("tok"), lax.axis_size("head")
    frame, me = lax.axis_index("tok"), lax.axis_index("head")
    me1 = me[None]
    blk_tok = query.shape[0] // FBLK
    blk_dev = blk_tok * heads
    slots = jnp.arange(intersection.shape[1], dtype=jnp.int32)
    live = slots[None, :] < counts[:, None]
    safe = jnp.maximum(intersection, 0)
    mine = live & (safe // blk_dev == frame)
    wanted = jnp.any(mine, axis=1).astype(jnp.int32)
    block = jnp.sum(jnp.where(mine, safe % blk_dev, 0), axis=1)
    piece = (me - block // blk_tok + heads) % heads
    blocks = jnp.concatenate([piece * blk_tok + block % blk_tok, wanted])
    my_ids = lax.dynamic_index_in_dim(safe, frame, 0, keepdims=False) // blk_dev
    my_count = lax.dynamic_index_in_dim(counts, frame, 0, keepdims=True)
    lists = jnp.concatenate([my_ids, my_count])

    kv = jnp.stack(shift(cut(me1, key, value, heads), 1), axis=1)
    sent = pick(blocks, kv, frames)
    query, out_grad, sent = lax.optimization_barrier((query, out_grad, sent))
    recv = lax.all_to_all(sent, "tok", split_axis=0, concat_axis=0, tiled=True)
    qd = jnp.stack(shift(cut(me1, query, out_grad, heads), 1), axis=1)
    stat = own_stats(kv, qd)
    ret, fin = memory(lists, stat, recv, qd)
    back = lax.all_to_all(ret, "tok", split_axis=0, concat_axis=0, tiled=True)
    dq, own = own_grads(lists, fin, recv, kv, qd)
    (dq_out,) = place(me1, shift(dq, -1))
    back, dq_out = lax.optimization_barrier((back, dq_out))
    dk_out, dv_out = place(me1, shift(collect(blocks, own, back, heads), -1))
    return (dq_out, dk_out, dv_out)


def solution(mesh):
    rows = P(("tok", "head"), None)
    return jax.shard_map(
        body,
        mesh=mesh,
        in_specs=(rows, rows, rows, rows, P(), P()),
        out_specs=(rows, rows, rows),
        check_vma=False,
    )
```

time: 271 us -> 242 us (0.89)
  waiting for transfers between devices: 145 us -> 93.6 us
  Pallas kernels: 45.8 us -> 58.7 us
  starting transfers between devices: 60.1 us -> 69.3 us
  other arithmetic: 4.33 us -> 0.85 us
  local copies, waits for them, and re-layouts: 13.7 us -> 16.5 us
    all_to_all x1, waiting for transfers between devices: 51.3 us -> 12.8 us  [body(): back = lax.all_to_all(ret, 'tok', split_axis=0, concat_axis=0, tiled=True)]
    pallas_call x5 -> x9, Pallas kernels: 45.8 us -> 58.7 us  [the longest x1 22.4 us: own_grads(): pl.pallas_call(functools.partial(own_grads_kernel, kc), grid=(nh,), out_s...]
    ppermute x28, starting transfers between devices: 41.6 us -> 53.2 us  [shift(): lax.ppermute(parts[k], 'head', [(i, (i + sign * k) % n) for i in range(n)])]
    unnamed x22 -> x32, local copies, waits for them, and re-layouts: 6.34 us -> 15.6 us
    ppermute x28, waiting for transfers between devices: 75.6 us -> 67.4 us  [shift(): lax.ppermute(parts[k], 'head', [(i, (i + sign * k) % n) for i in range(n)])]
    all_to_all x1, waiting for transfers between devices: 18.4 us -> 13.4 us  [body(): recv = lax.all_to_all(sent, 'tok', split_axis=0, concat_axis=0, tiled=True)]
    another operation x4 -> x2, local copies, waits for them, and re-layouts: 3.91 us -> 0.09 us  [the longest x1 0.05 us: body(): kv = jnp.stack(shift(cut(me1, key, value, heads), 1), axis=1)]
    another operation x15 -> x0, other arithmetic: 3.5 us -> none  [to_heads(): jnp.stack([lax.dynamic_slice(x, (0, (me ^ k) * cols), (tok, cols)) for x...]
  transfers between devices with their start and end apart: 30 -> 30, of which waited for: 16 -> 16; matrix products, arithmetic and copies ran while one was open for 6% -> 3% of each run, Pallas kernels for 2% -> 14%
where the time goes in v2:
time: 242 us; the launch traced here: 240 us
  waiting for transfers between devices  93.6 us (39%)
  starting transfers between devices  69.3 us (29%)
  Pallas kernels  58.7 us (24%)
  local copies, waits for them, and re-layouts  16.5 us (7%)
    ppermute x28, waiting for transfers between devices, shift(): lax.ppermute(parts[k], 'head', [(i, (i + sign * k) % n) for i in range(n)])  67.4 us
    ppermute x28, starting transfers between devices, shift(): lax.ppermute(parts[k], 'head', [(i, (i + sign * k) % n) for i in range(n)])  53.2 us
    pallas_call x1, Pallas kernels, own_grads(): pl.pallas_call(functools.partial(own_grads_kernel, kc), grid=(nh,), out_s...  22.4 us
    unnamed x32, local copies, waits for them, and re-layouts  15.6 us
    all_to_all x1, waiting for transfers between devices, body(): recv = lax.all_to_all(sent, 'tok', split_axis=0, concat_axis=0, tiled=True)  13.4 us
    all_to_all x1, waiting for transfers between devices, body(): back = lax.all_to_all(ret, 'tok', split_axis=0, concat_axis=0, tiled=True)  12.8 us
    pallas_call x1, Pallas kernels, memory(): pl.pallas_call(functools.partial(memory_kernel, kc), grid=(nh,), out_shap...  12.4 us
    all_to_all x1, starting transfers between devices, body(): recv = lax.all_to_all(sent, 'tok', split_axis=0, concat_axis=0, tiled=True)  9.46 us
  transfers between devices with their start and end apart: 30, of which 16 were waited for; matrix products, arithmetic and copies ran while one was open for 3% of the time, Pallas kernels for 14%

profile of v2, /device:TPU:1, one launch (start us, length us, event | category | flops | bytes accessed | tf_op | source)
XLA Modules:
  0.0 239.9 jit_solution(10630526197155134103)
XLA Ops:
  0.7 3.4 %cut.2 = (bf16[2,5,128,128]{3,2,1,0:T(8,128)(2,1)}, bf16[2,5,128,128]{3,2,1,0:T(8,128)(2,1)}, bf16[2,5,128,128]{3,2,1,0:T(8,128)(2,1)}, bf16[2,5,128,128]{3,2,1,...) custom-call(s32[1]{0:T(128)} %bitcast.me_ref, ...), custom_call_target="tpu_custom_call" | custom-call | tf_op jit(solution)/shard_map/cut/pallas_call | solution.py:313
  4.1 2.7 %collective-permute-start = (bf16[2,5,128,128]{3,2,1,0:T(8,128)(2,1)}, bf16[2,5,128,128]{3,2,1,0:T(8,128)(2,1)}, u32[]{:S(2)}, u32[]{:S(2)}) collective-permute-start(bf16[2,5,128,128]{3,2,1,0:T(8,128)(2,1)} %get-tuple-element.46), channel_id=1, source_target_pairs={{0,1},{1,2},{2,3},{3,4},{4,5},{5,6},{6,7},{7,0},{8,9},{9,10},{10,1... | collective-permute-start | bytes 983048 | tf_op jit(solution)/shard_map/ppermute | solution.py:351
  6.8 1.3 collective-permute-start.1
  8.1 1.7 collective-permute-start.2
  9.8 1.3 collective-permute-start.3
  11.1 2.6 %collective-permute-start.4 = (bf16[2,5,128,128]{3,2,1,0:T(8,128)(2,1)}, bf16[2,5,128,128]{3,2,1,0:T(8,128)(2,1)S(1)}, u32[]{:S(2)}, u32[]{:S(2)}) collective-permute-start(bf16[2,5,128,128]{3,2,1,0:T(8,128)(2,1)} %get-tuple-element.50), channel_id=1, source_target_pairs={{0,5},{1,6},{2,7},{3,0},{4,1},{5,2},{6,3},{7,4},{8,13},{9,14},{10,... | collective-permute-start | bytes 983048 | tf_op jit(solution)/shard_map/ppermute | solution.py:351
  14.9 2.2 collective-permute-start.5
  18.1 7.2 %collective-permute-done.1 = bf16[2,5,128,128]{3,2,1,0:T(8,128)(2,1)} collective-permute-done((bf16[2,5,128,128]{3,2,1,0:T(8,128)(2,1)}, bf16[2,5,128,128]{3,2,1,0:T(8,128)(2,1)}, u32[]{:S(2)}, u32[]{:S(2)}) %collective-permute-start.1) | collective-permute-done | bytes 327712 | tf_op jit(solution)/shard_map/ppermute | solution.py:351
  26.4 12.9 %collective-permute-done.2 = bf16[2,5,128,128]{3,2,1,0:T(8,128)(2,1)} collective-permute-done((bf16[2,5,128,128]{3,2,1,0:T(8,128)(2,1)}, bf16[2,5,128,128]{3,2,1,0:T(8,128)(2,1)}, u32[]{:S(2)}, u32[]{:S(2)}) %collective-permute-start.2) | collective-permute-done | bytes 327712 | tf_op jit(solution)/shard_map/ppermute | solution.py:351
  40.5 2.6 %pick.1 = bf16[32,2,5,32,128]{4,3,2,1,0:T(8,128)(2,1)} custom-call(s32[64]{0:T(128)S(1)} %pad_add_fusion.1.blocks_ref, bf16[2,8,5,128,128]{4,3,2,1,0:T(8,128)(2,1)S(1)} %bitcast_dynamic-update-slice_fusion.8.kv_ref), custom_call_target="tpu_custom_call" | custom-call | tf_op jit(solution)/shard_map/pick/pallas_call | solution.py:281
  43.1 9.5 %all-to-all-start = ((bf16[32,2,5,32,128]{4,3,2,1,0:T(8,128)(2,1)}), bf16[32,2,5,32,128]{4,3,2,1,0:T(8,128)(2,1)}, u32[]{:S(2)}, u32[]{:S(2)}) async-start(bf16[32,2,5,32,128]{4,3,2,1,0:T(8,128)(2,1)} %pick.1), calls=%async_computation | async-start | bytes 5242880 | tf_op jit(solution)/shard_map/all_to_all | solution.py:376
  53.4 3.4 %cut.3 = (bf16[2,5,128,128]{3,2,1,0:T(8,128)(2,1)}, bf16[2,5,128,128]{3,2,1,0:T(8,128)(2,1)}, bf16[2,5,128,128]{3,2,1,0:T(8,128)(2,1)}, bf16[2,5,128,128]{3,2,1,...) custom-call(s32[1]{0:T(128)} %bitcast.me_ref, ...), custom_call_target="tpu_custom_call" | custom-call | tf_op jit(solution)/shard_map/cut/pallas_call | solution.py:313
  57.6 2.1 collective-permute-start.8
  60.7 1.8 collective-permute-start.9
  62.5 1.7 collective-permute-start.10
  65.0 7.4 %collective-permute-done.8 = bf16[2,5,128,128]{3,2,1,0:T(8,128)(2,1)S(1)} collective-permute-done((bf16[2,5,128,128]{3,2,1,0:T(8,128)(2,1)}, bf16[2,5,128,128]{3,2,1,0:T(8,128)(2,1)S(1)}, u32[]{:S(2)}, u32[]{:S(2)}) %collective-permute-start.8) | collective-permute-done | bytes 327712 | tf_op jit(solution)/shard_map/ppermute | solution.py:351
  72.5 3.7 %collective-permute-done.9 = bf16[2,5,128,128]{3,2,1,0:T(8,128)(2,1)S(1)} collective-permute-done((bf16[2,5,128,128]{3,2,1,0:T(8,128)(2,1)}, bf16[2,5,128,128]{3,2,1,0:T(8,128)(2,1)S(1)}, u32[]{:S(2)}, u32[]{:S(2)}) %collective-permute-start.9) | collective-permute-done | bytes 327712 | tf_op jit(solution)/shard_map/ppermute | solution.py:351
  76.3 10.9 %collective-permute-done.10 = bf16[2,5,128,128]{3,2,1,0:T(8,128)(2,1)S(1)} collective-permute-done((bf16[2,5,128,128]{3,2,1,0:T(8,128)(2,1)}, bf16[2,5,128,128]{3,2,1,0:T(8,128)(2,1)S(1)}, u32[]{:S(2)}, u32[]{:S(2)}) %collective-permute-start.10) | collective-permute-done | bytes 327712 | tf_op jit(solution)/shard_map/ppermute | solution.py:351
  87.2 2.1 collective-permute-done.11
  89.3 1.8 collective-permute-done.12
  92.3 7.4 %own_stats.1.stat_ref = f32[5,8,1024]{2,1,0:T(8,128)S(1)} custom-call(bf16[2,8,5,128,128]{4,3,2,1,0:T(8,128)(2,1)S(1)} %bitcast_dynamic-update-slice_fusion.8.kv_ref, bf16[2,8,5,128,128]{4,3,2,1,0:T(8,128)(2,1)S(1)} %bitcast_dynamic-update-slice_fusion.qd_ref), custom_call_target="tpu_custom_call" | custom-call | flops 2684354560 | bytes 5242880 | tf_op jit(solution)/shard_map/own_stats/pallas_call | solution.py:97
  99.7 1.6 copy-done.4
  101.3 13.4 %all-to-all-done.recv_ref = bf16[32,2,5,32,128]{4,3,2,1,0:T(8,128)(2,1)} async-done(((bf16[32,2,5,32,128]{4,3,2,1,0:T(8,128)(2,1)}), bf16[32,2,5,32,128]{4,3,2,1,0:T(8,128)(2,1)}, u32[]{:S(2)}, u32[]{:S(2)}) %all-to-all-start) | async-done | bytes 2621472 | tf_op jit(solution)/shard_map/all_to_all | solution.py:376
  114.7 1.7 copy-done.5
  116.5 12.4 %memory.1 = (bf16[32,2,5,32,128]{4,3,2,1,0:T(8,128)(2,1)}, f32[5,8,1024]{2,1,0:T(8,128)S(1)}) custom-call(s32[17]{0:T(128)S(1)} %pad_add_fusion.lists_ref, f32[5,8,1024]{2,1,0:T(8,128)S(1)} %own_stats.1.stat_ref, bf16[32,2,5,32,128]{4,3,2,1,0:T(8,128)(2,1)} %all-to-all-done.recv_ref, bf16[2,8,5,128,128]{4,3,2,1,0:T(8,128)(2,1)S(1)} %copy-done.5), custom_call_target="tpu_custom_call" | custom-call | flops 2684354560 | bytes 5242880 | tf_op jit(solution)/shard_map/memory/pallas_call | solution.py:165
  128.8 6.7 %all-to-all-start.1 = ((bf16[32,2,5,32,128]{4,3,2,1,0:T(8,128)(2,1)}), bf16[32,2,5,32,128]{4,3,2,1,0:T(8,128)(2,1)S(1)}, u32[]{:S(2)}, u32[]{:S(2)}) async-start(bf16[32,2,5,32,128]{4,3,2,1,0:T(8,128)(2,1)} %get-tuple-element.64), calls=%async_computation.1 | async-start | bytes 5242880 | tf_op jit(solution)/shard_map/all_to_all | solution.py:380
  135.5 1.7 copy-done.2
  137.2 1.7 copy-done.6
  138.9 22.4 %own_grads.1 = (bf16[1,5,128,128]{3,2,1,0:T(8,128)(2,1)}, bf16[1,5,128,128]{3,2,1,0:T(8,128)(2,1)}, bf16[1,5,128,128]{3,2,1,0:T(8,128)(2,1)}, bf16[1,5,128,128]{...) custom-call(s32[17]{0:T(128)S(1)} %pad_add_fusion.lists_ref, ...), custom_call_target="tpu_custom_call" | custom-call | flops 10066329600 | bytes 10485760 | tf_op jit(solution)/shard_map/own_grads/pallas_call | solution.py:217
  162.1 1.7 collective-permute-start.15
  163.9 1.4 collective-permute-start.16
  165.3 1.7 collective-permute-start.17
  167.0 1.3 collective-permute-start.18
  169.6 3.6 %collective-permute-start.20 = (bf16[1,5,128,128]{3,2,1,0:T(8,128)(2,1)}, bf16[1,5,128,128]{3,2,1,0:T(8,128)(2,1)S(1)}, u32[]{:S(2)}, u32[]{:S(2)}) collective-permute-start(bf16[1,5,128,128]{3,2,1,0:T(8,128)(2,1)} %get-tuple-element.73), channel_id=1, source_target_pairs={{0,1},{1,2},{2,3},{3,4},{4,5},{5,6},{6,7},{7,0},{8,9},{9,10},{10,1... | collective-permute-start | bytes 491528 | tf_op jit(solution)/shard_map/ppermute | solution.py:351
  173.2 5.5 %collective-permute-done.16.refs_3_ = bf16[1,5,128,128]{3,2,1,0:T(8,128)(2,1)S(1)} collective-permute-done((bf16[1,5,128,128]{3,2,1,0:T(8,128)(2,1)}, bf16[1,5,128,128]{3,2,1,0:T(8,128)(2,1)S(1)}, u32[]{:S(2)}, u32[]{:S(2)}) %collective-permute-start.16) | collective-permute-done | bytes 163872 | tf_op jit(solution)/shard_map/ppermute | solution.py:351
  181.1 1.4 place.2
  182.5 12.8 %all-to-all-done.1.back_ref = bf16[32,2,5,32,128]{4,3,2,1,0:T(8,128)(2,1)S(1)} async-done(((bf16[32,2,5,32,128]{4,3,2,1,0:T(8,128)(2,1)}), bf16[32,2,5,32,128]{4,3,2,1,0:T(8,128)(2,1)S(1)}, u32[]{:S(2)}, u32[]{:S(2)}) %all-to-all-start.1) | async-done | bytes 2621472 | tf_op jit(solution)/shard_map/all_to_all | solution.py:380
  195.4 2.5 %copy-done = f32[2,5,1024,128]{3,2,1,0:T(8,128)S(1)} copy-done((f32[2,5,1024,128]{3,2,1,0:T(8,128)S(1)}, f32[2,5,1024,128]{3,2,1,0:T(8,128)}, u32[]{:S(2)}) %copy-start) | copy-done | bytes 5242904
  197.9 3.4 %collect.1 = (bf16[2,5,128,128]{3,2,1,0:T(8,128)(2,1)S(1)}, bf16[2,5,128,128]{3,2,1,0:T(8,128)(2,1)S(1)}, bf16[2,5,128,128]{3,2,1,0:T(8,128)(2,1)S(1)}, bf16[2,5...) custom-call(s32[64]{0:T(128)S(1)} %pad_add_fusion.1.blocks_ref, ...), custom_call_target="tpu_custom_call" | custom-call | tf_op jit(solution)/shard_map/collect/pallas_call | solution.py:252
  201.3 4.5 %collective-permute-start.21 = (bf16[2,5,128,128]{3,2,1,0:T(8,128)(2,1)S(1)}, bf16[2,5,128,128]{3,2,1,0:T(8,128)(2,1)S(1)}, u32[]{:S(2)}, u32[]{:S(2)}) collective-permute-start(bf16[2,5,128,128]{3,2,1,0:T(8,128)(2,1)S(1)} %get-tuple-element.78), channel_id=1, source_target_pairs={{0,7},{1,0},{2,1},{3,2},{4,3},{5,4},{6,5},{7,6},{8,15},{9,8},{10,9... | collective-permute-start | bytes 983048 | tf_op jit(solution)/shard_map/ppermute | solution.py:351
  205.8 1.8 collective-permute-start.22
  207.6 1.4 collective-permute-start.23
  209.3 2.7 %collective-permute-start.25 = (bf16[2,5,128,128]{3,2,1,0:T(8,128)(2,1)S(1)}, bf16[2,5,128,128]{3,2,1,0:T(8,128)(2,1)S(1)}, u32[]{:S(2)}, u32[]{:S(2)}) collective-permute-start(bf16[2,5,128,128]{3,2,1,0:T(8,128)(2,1)S(1)} %get-tuple-element.82), channel_id=1, source_target_pairs={{0,3},{1,4},{2,5},{3,6},{4,7},{5,0},{6,1},{7,2},{8,11},{9,12},{10,... | collective-permute-start | bytes 983048 | tf_op jit(solution)/shard_map/ppermute | solution.py:351
  212.0 4.6 %collective-permute-start.26 = (bf16[2,5,128,128]{3,2,1,0:T(8,128)(2,1)S(1)}, bf16[2,5,128,128]{3,2,1,0:T(8,128)(2,1)S(1)}, u32[]{:S(2)}, u32[]{:S(2)}) collective-permute-start(bf16[2,5,128,128]{3,2,1,0:T(8,128)(2,1)S(1)} %get-tuple-element.83), channel_id=1, source_target_pairs={{0,2},{1,3},{2,4},{3,5},{4,6},{5,7},{6,0},{7,1},{8,10},{9,11},{10,... | collective-permute-start | bytes 983048 | tf_op jit(solution)/shard_map/ppermute | solution.py:351
  216.6 7.8 %collective-permute-start.27 = (bf16[2,5,128,128]{3,2,1,0:T(8,128)(2,1)S(1)}, bf16[2,5,128,128]{3,2,1,0:T(8,128)(2,1)S(1)}, u32[]{:S(2)}, u32[]{:S(2)}) collective-permute-start(bf16[2,5,128,128]{3,2,1,0:T(8,128)(2,1)S(1)} %get-tuple-element.84), channel_id=1, source_target_pairs={{0,1},{1,2},{2,3},{3,4},{4,5},{5,6},{6,7},{7,0},{8,9},{9,10},{10,1... | collective-permute-start | bytes 983048 | tf_op jit(solution)/shard_map/ppermute | solution.py:351
  224.4 10.2 %collective-permute-done.23.refs_3_ = bf16[2,5,128,128]{3,2,1,0:T(8,128)(2,1)S(1)} collective-permute-done((bf16[2,5,128,128]{3,2,1,0:T(8,128)(2,1)S(1)}, bf16[2,5,128,128]{3,2,1,0:T(8,128)(2,1)S(1)}, u32[]{:S(2)}, u32[]{:S(2)}) %collective-permute-start.23) | collective-permute-done | bytes 327712 | tf_op jit(solution)/shard_map/ppermute | solution.py:351
  234.6 3.1 %collective-permute-done.27.refs_7_ = bf16[2,5,128,128]{3,2,1,0:T(8,128)(2,1)S(1)} collective-permute-done((bf16[2,5,128,128]{3,2,1,0:T(8,128)(2,1)S(1)}, bf16[2,5,128,128]{3,2,1,0:T(8,128)(2,1)S(1)}, u32[]{:S(2)}, u32[]{:S(2)}) %collective-permute-start.27) | collective-permute-done | bytes 327712 | tf_op jit(solution)/shard_map/ppermute | solution.py:351
  237.7 2.2 place.3
  (64 shorter events, 14.0 us)
Async XLA Ops:
  0.6 14.1 %copy-start.8 = (s32[32]{0:T(128)S(1)}, s32[32]{0:T(128)}, u32[]{:S(2)}) copy-start(s32[32]{0:T(128)} %param.11) | copy-start | bytes 388
  0.6 14.1 %copy-start.7 = (s32[32,16]{0,1:T(8,128)S(1)}, s32[32,16]{0,1:T(8,128)}, u32[]{:S(2)}) copy-start(s32[32,16]{0,1:T(8,128)} %param.10) | copy-start | bytes 6148
  4.1 10.8 %collective-permute-start = (bf16[2,5,128,128]{3,2,1,0:T(8,128)(2,1)}, bf16[2,5,128,128]{3,2,1,0:T(8,128)(2,1)}, u32[]{:S(2)}, u32[]{:S(2)}) collective-permute-start(bf16[2,5,128,128]{3,2,1,0:T(8,128)(2,1)} %get-tuple-element.46), channel_id=1, source_target_pairs={{0,1},{1,2},{2,3},{3,4},{4,5},{5,6},{6,7},{7,0},{8,9},{9,10},{10,1... | collective-permute-start | bytes 983048 | tf_op jit(solution)/shard_map/ppermute | solution.py:351
  6.8 18.6 %collective-permute-start.1 = (bf16[2,5,128,128]{3,2,1,0:T(8,128)(2,1)}, bf16[2,5,128,128]{3,2,1,0:T(8,128)(2,1)}, u32[]{:S(2)}, u32[]{:S(2)}) collective-permute-start(bf16[2,5,128,128]{3,2,1,0:T(8,128)(2,1)} %get-tuple-element.47), channel_id=1, source_target_pairs={{0,2},{1,3},{2,4},{3,5},{4,6},{5,7},{6,0},{7,1},{8,10},{9,11},{10,... | collective-permute-start | bytes 983048 | tf_op jit(solution)/shard_map/ppermute | solution.py:351
  8.1 31.2 %collective-permute-start.2 = (bf16[2,5,128,128]{3,2,1,0:T(8,128)(2,1)}, bf16[2,5,128,128]{3,2,1,0:T(8,128)(2,1)}, u32[]{:S(2)}, u32[]{:S(2)}) collective-permute-start(bf16[2,5,128,128]{3,2,1,0:T(8,128)(2,1)} %get-tuple-element.48), channel_id=1, source_target_pairs={{0,3},{1,4},{2,5},{3,6},{4,7},{5,0},{6,1},{7,2},{8,11},{9,12},{10,... | collective-permute-start | bytes 983048 | tf_op jit(solution)/shard_map/ppermute | solution.py:351
  9.8 30.5 %collective-permute-start.3 = (bf16[2,5,128,128]{3,2,1,0:T(8,128)(2,1)}, bf16[2,5,128,128]{3,2,1,0:T(8,128)(2,1)S(1)}, u32[]{:S(2)}, u32[]{:S(2)}) collective-permute-start(bf16[2,5,128,128]{3,2,1,0:T(8,128)(2,1)} %get-tuple-element.49), channel_id=1, source_target_pairs={{0,4},{1,5},{2,6},{3,7},{4,0},{5,1},{6,2},{7,3},{8,12},{9,13},{10,... | collective-permute-start | bytes 983048 | tf_op jit(solution)/shard_map/ppermute | solution.py:351
  11.1 29.3 %collective-permute-start.4 = (bf16[2,5,128,128]{3,2,1,0:T(8,128)(2,1)}, bf16[2,5,128,128]{3,2,1,0:T(8,128)(2,1)S(1)}, u32[]{:S(2)}, u32[]{:S(2)}) collective-permute-start(bf16[2,5,128,128]{3,2,1,0:T(8,128)(2,1)} %get-tuple-element.50), channel_id=1, source_target_pairs={{0,5},{1,6},{2,7},{3,0},{4,1},{5,2},{6,3},{7,4},{8,13},{9,14},{10,... | collective-permute-start | bytes 983048 | tf_op jit(solution)/shard_map/ppermute | solution.py:351
  14.9 25.5 %collective-permute-start.5 = (bf16[2,5,128,128]{3,2,1,0:T(8,128)(2,1)}, bf16[2,5,128,128]{3,2,1,0:T(8,128)(2,1)S(1)}, u32[]{:S(2)}, u32[]{:S(2)}) collective-permute-start(bf16[2,5,128,128]{3,2,1,0:T(8,128)(2,1)} %get-tuple-element.51), channel_id=1, source_target_pairs={{0,6},{1,7},{2,0},{3,1},{4,2},{5,3},{6,4},{7,5},{8,14},{9,15},{10,... | collective-permute-start | bytes 983048 | tf_op jit(solution)/shard_map/ppermute | solution.py:351
  25.4 15.1 %collective-permute-start.6 = (bf16[2,5,128,128]{3,2,1,0:T(8,128)(2,1)}, bf16[2,5,128,128]{3,2,1,0:T(8,128)(2,1)S(1)}, u32[]{:S(2)}, u32[]{:S(2)}) collective-permute-start(bf16[2,5,128,128]{3,2,1,0:T(8,128)(2,1)} %get-tuple-element.52), channel_id=1, source_target_pairs={{0,7},{1,0},{2,1},{3,2},{4,3},{5,4},{6,5},{7,6},{8,15},{9,8},{10,9... | collective-permute-start | bytes 983048 | tf_op jit(solution)/shard_map/ppermute | solution.py:351
  40.5 51.8 %copy-start.1 = (bf16[2,8,5,128,128]{4,3,2,1,0:T(8,128)(2,1)}, bf16[2,8,5,128,128]{4,3,2,1,0:T(8,128)(2,1)S(1)}, u32[]{:S(2)}) copy-start(bf16[2,8,5,128,128]{4,3,2,1,0:T(8,128)(2,1)S(1)} %bitcast_dynamic-update-slice_fusion.8.kv_ref) | copy-start | bytes 7864324
  43.1 71.6 %all-to-all-start = ((bf16[32,2,5,32,128]{4,3,2,1,0:T(8,128)(2,1)}), bf16[32,2,5,32,128]{4,3,2,1,0:T(8,128)(2,1)}, u32[]{:S(2)}, u32[]{:S(2)}) async-start(bf16[32,2,5,32,128]{4,3,2,1,0:T(8,128)(2,1)} %pick.1), calls=%async_computation | async-start | bytes 5242880 | tf_op jit(solution)/shard_map/all_to_all | solution.py:376
  56.9 7.8 %collective-permute-start.7 = (bf16[2,5,128,128]{3,2,1,0:T(8,128)(2,1)}, bf16[2,5,128,128]{3,2,1,0:T(8,128)(2,1)S(1)}, u32[]{:S(2)}, u32[]{:S(2)}) collective-permute-start(bf16[2,5,128,128]{3,2,1,0:T(8,128)(2,1)} %get-tuple-element.56), channel_id=1, source_target_pairs={{0,1},{1,2},{2,3},{3,4},{4,5},{5,6},{6,7},{7,0},{8,9},{9,10},{10,1... | collective-permute-start | bytes 983048 | tf_op jit(solution)/shard_map/ppermute | solution.py:351
  57.6 14.9 %collective-permute-start.8 = (bf16[2,5,128,128]{3,2,1,0:T(8,128)(2,1)}, bf16[2,5,128,128]{3,2,1,0:T(8,128)(2,1)S(1)}, u32[]{:S(2)}, u32[]{:S(2)}) collective-permute-start(bf16[2,5,128,128]{3,2,1,0:T(8,128)(2,1)} %get-tuple-element.57), channel_id=1, source_target_pairs={{0,2},{1,3},{2,4},{3,5},{4,6},{5,7},{6,0},{7,1},{8,10},{9,11},{10,... | collective-permute-start | bytes 983048 | tf_op jit(solution)/shard_map/ppermute | solution.py:351
  60.7 15.5 %collective-permute-start.9 = (bf16[2,5,128,128]{3,2,1,0:T(8,128)(2,1)}, bf16[2,5,128,128]{3,2,1,0:T(8,128)(2,1)S(1)}, u32[]{:S(2)}, u32[]{:S(2)}) collective-permute-start(bf16[2,5,128,128]{3,2,1,0:T(8,128)(2,1)} %get-tuple-element.58), channel_id=1, source_target_pairs={{0,3},{1,4},{2,5},{3,6},{4,7},{5,0},{6,1},{7,2},{8,11},{9,12},{10,... | collective-permute-start | bytes 983048 | tf_op jit(solution)/shard_map/ppermute | solution.py:351
  62.5 24.7 %collective-permute-start.10 = (bf16[2,5,128,128]{3,2,1,0:T(8,128)(2,1)}, bf16[2,5,128,128]{3,2,1,0:T(8,128)(2,1)S(1)}, u32[]{:S(2)}, u32[]{:S(2)}) collective-permute-start(bf16[2,5,128,128]{3,2,1,0:T(8,128)(2,1)} %get-tuple-element.59), channel_id=1, source_target_pairs={{0,4},{1,5},{2,6},{3,7},{4,0},{5,1},{6,2},{7,3},{8,12},{9,13},{10,... | collective-permute-start | bytes 983048 | tf_op jit(solution)/shard_map/ppermute | solution.py:351
  64.2 25.1 %collective-permute-start.11 = (bf16[2,5,128,128]{3,2,1,0:T(8,128)(2,1)}, bf16[2,5,128,128]{3,2,1,0:T(8,128)(2,1)S(1)}, u32[]{:S(2)}, u32[]{:S(2)}) collective-permute-start(bf16[2,5,128,128]{3,2,1,0:T(8,128)(2,1)} %get-tuple-element.60), channel_id=1, source_target_pairs={{0,5},{1,6},{2,7},{3,0},{4,1},{5,2},{6,3},{7,4},{8,13},{9,14},{10,... | collective-permute-start | bytes 983048 | tf_op jit(solution)/shard_map/ppermute | solution.py:351
  64.7 26.4 %collective-permute-start.12 = (bf16[2,5,128,128]{3,2,1,0:T(8,128)(2,1)}, bf16[2,5,128,128]{3,2,1,0:T(8,128)(2,1)S(1)}, u32[]{:S(2)}, u32[]{:S(2)}) collective-permute-start(bf16[2,5,128,128]{3,2,1,0:T(8,128)(2,1)} %get-tuple-element.61), channel_id=1, source_target_pairs={{0,6},{1,7},{2,0},{3,1},{4,2},{5,3},{6,4},{7,5},{8,14},{9,15},{10,... | collective-permute-start | bytes 983048 | tf_op jit(solution)/shard_map/ppermute | solution.py:351
  72.5 19.8 %collective-permute-start.13 = (bf16[2,5,128,128]{3,2,1,0:T(8,128)(2,1)}, bf16[2,5,128,128]{3,2,1,0:T(8,128)(2,1)S(1)}, u32[]{:S(2)}, u32[]{:S(2)}) collective-permute-start(bf16[2,5,128,128]{3,2,1,0:T(8,128)(2,1)} %get-tuple-element.62), channel_id=1, source_target_pairs={{0,7},{1,0},{2,1},{3,2},{4,3},{5,4},{6,5},{7,6},{8,15},{9,8},{10,9... | collective-permute-start | bytes 983048 | tf_op jit(solution)/shard_map/ppermute | solution.py:351
  99.7 1.6 copy-start.4
  114.7 1.7 copy-start.5
  128.8 66.6 %all-to-all-start.1 = ((bf16[32,2,5,32,128]{4,3,2,1,0:T(8,128)(2,1)}), bf16[32,2,5,32,128]{4,3,2,1,0:T(8,128)(2,1)S(1)}, u32[]{:S(2)}, u32[]{:S(2)}) async-start(bf16[32,2,5,32,128]{4,3,2,1,0:T(8,128)(2,1)} %get-tuple-element.64), calls=%async_computation.1 | async-start | bytes 5242880 | tf_op jit(solution)/shard_map/all_to_all | solution.py:380
  135.5 1.7 copy-start.2
  137.2 1.7 copy-start.6
  161.4 6.9 %collective-permute-start.14 = (bf16[1,5,128,128]{3,2,1,0:T(8,128)(2,1)}, bf16[1,5,128,128]{3,2,1,0:T(8,128)(2,1)S(1)}, u32[]{:S(2)}, u32[]{:S(2)}) collective-permute-start(bf16[1,5,128,128]{3,2,1,0:T(8,128)(2,1)} %get-tuple-element.67), channel_id=1, source_target_pairs={{0,7},{1,0},{2,1},{3,2},{4,3},{5,4},{6,5},{7,6},{8,15},{9,8},{10,9... | collective-permute-start | bytes 491528 | tf_op jit(solution)/shard_map/ppermute | solution.py:351
  162.1 7.4 %collective-permute-start.15 = (bf16[1,5,128,128]{3,2,1,0:T(8,128)(2,1)}, bf16[1,5,128,128]{3,2,1,0:T(8,128)(2,1)S(1)}, u32[]{:S(2)}, u32[]{:S(2)}) collective-permute-start(bf16[1,5,128,128]{3,2,1,0:T(8,128)(2,1)} %get-tuple-element.68), channel_id=1, source_target_pairs={{0,6},{1,7},{2,0},{3,1},{4,2},{5,3},{6,4},{7,5},{8,14},{9,15},{10,... | collective-permute-start | bytes 491528 | tf_op jit(solution)/shard_map/ppermute | solution.py:351
  163.9 14.8 %collective-permute-start.16 = (bf16[1,5,128,128]{3,2,1,0:T(8,128)(2,1)}, bf16[1,5,128,128]{3,2,1,0:T(8,128)(2,1)S(1)}, u32[]{:S(2)}, u32[]{:S(2)}) collective-permute-start(bf16[1,5,128,128]{3,2,1,0:T(8,128)(2,1)} %get-tuple-element.69), channel_id=1, source_target_pairs={{0,5},{1,6},{2,7},{3,0},{4,1},{5,2},{6,3},{7,4},{8,13},{9,14},{10,... | collective-permute-start | bytes 491528 | tf_op jit(solution)/shard_map/ppermute | solution.py:351
  165.3 13.4 %collective-permute-start.17 = (bf16[1,5,128,128]{3,2,1,0:T(8,128)(2,1)}, bf16[1,5,128,128]{3,2,1,0:T(8,128)(2,1)S(1)}, u32[]{:S(2)}, u32[]{:S(2)}) collective-permute-start(bf16[1,5,128,128]{3,2,1,0:T(8,128)(2,1)} %get-tuple-element.70), channel_id=1, source_target_pairs={{0,4},{1,5},{2,6},{3,7},{4,0},{5,1},{6,2},{7,3},{8,12},{9,13},{10,... | collective-permute-start | bytes 491528 | tf_op jit(solution)/shard_map/ppermute | solution.py:351
  167.0 12.2 %collective-permute-start.18 = (bf16[1,5,128,128]{3,2,1,0:T(8,128)(2,1)}, bf16[1,5,128,128]{3,2,1,0:T(8,128)(2,1)S(1)}, u32[]{:S(2)}, u32[]{:S(2)}) collective-permute-start(bf16[1,5,128,128]{3,2,1,0:T(8,128)(2,1)} %get-tuple-element.71), channel_id=1, source_target_pairs={{0,3},{1,4},{2,5},{3,6},{4,7},{5,0},{6,1},{7,2},{8,11},{9,12},{10,... | collective-permute-start | bytes 491528 | tf_op jit(solution)/shard_map/ppermute | solution.py:351
  168.3 11.2 %collective-permute-start.19 = (bf16[1,5,128,128]{3,2,1,0:T(8,128)(2,1)}, bf16[1,5,128,128]{3,2,1,0:T(8,128)(2,1)S(1)}, u32[]{:S(2)}, u32[]{:S(2)}) collective-permute-start(bf16[1,5,128,128]{3,2,1,0:T(8,128)(2,1)} %get-tuple-element.72), channel_id=1, source_target_pairs={{0,2},{1,3},{2,4},{3,5},{4,6},{5,7},{6,0},{7,1},{8,10},{9,11},{10,... | collective-permute-start | bytes 491528 | tf_op jit(solution)/shard_map/ppermute | solution.py:351
  169.6 10.7 %collective-permute-start.20 = (bf16[1,5,128,128]{3,2,1,0:T(8,128)(2,1)}, bf16[1,5,128,128]{3,2,1,0:T(8,128)(2,1)S(1)}, u32[]{:S(2)}, u32[]{:S(2)}) collective-permute-start(bf16[1,5,128,128]{3,2,1,0:T(8,128)(2,1)} %get-tuple-element.73), channel_id=1, source_target_pairs={{0,1},{1,2},{2,3},{3,4},{4,5},{5,6},{6,7},{7,0},{8,9},{9,10},{10,1... | collective-permute-start | bytes 491528 | tf_op jit(solution)/shard_map/ppermute | solution.py:351
  180.2 0.9 copy-start.3
  195.4 2.5 %copy-start = (f32[2,5,1024,128]{3,2,1,0:T(8,128)S(1)}, f32[2,5,1024,128]{3,2,1,0:T(8,128)}, u32[]{:S(2)}) copy-start(f32[2,5,1024,128]{3,2,1,0:T(8,128)} %get-tuple-element.75.own_ref) | copy-start | bytes 15728644
  201.3 10.7 %collective-permute-start.21 = (bf16[2,5,128,128]{3,2,1,0:T(8,128)(2,1)S(1)}, bf16[2,5,128,128]{3,2,1,0:T(8,128)(2,1)S(1)}, u32[]{:S(2)}, u32[]{:S(2)}) collective-permute-start(bf16[2,5,128,128]{3,2,1,0:T(8,128)(2,1)S(1)} %get-tuple-element.78), channel_id=1, source_target_pairs={{0,7},{1,0},{2,1},{3,2},{4,3},{5,4},{6,5},{7,6},{8,15},{9,8},{10,9... | collective-permute-start | bytes 983048 | tf_op jit(solution)/shard_map/ppermute | solution.py:351
  205.8 10.8 %collective-permute-start.22 = (bf16[2,5,128,128]{3,2,1,0:T(8,128)(2,1)S(1)}, bf16[2,5,128,128]{3,2,1,0:T(8,128)(2,1)S(1)}, u32[]{:S(2)}, u32[]{:S(2)}) collective-permute-start(bf16[2,5,128,128]{3,2,1,0:T(8,128)(2,1)S(1)} %get-tuple-element.79), channel_id=1, source_target_pairs={{0,6},{1,7},{2,0},{3,1},{4,2},{5,3},{6,4},{7,5},{8,14},{9,15},{10,... | collective-permute-start | bytes 983048 | tf_op jit(solution)/shard_map/ppermute | solution.py:351
  207.6 27.0 %collective-permute-start.23 = (bf16[2,5,128,128]{3,2,1,0:T(8,128)(2,1)S(1)}, bf16[2,5,128,128]{3,2,1,0:T(8,128)(2,1)S(1)}, u32[]{:S(2)}, u32[]{:S(2)}) collective-permute-start(bf16[2,5,128,128]{3,2,1,0:T(8,128)(2,1)S(1)} %get-tuple-element.80), channel_id=1, source_target_pairs={{0,5},{1,6},{2,7},{3,0},{4,1},{5,2},{6,3},{7,4},{8,13},{9,14},{10,... | collective-permute-start | bytes 983048 | tf_op jit(solution)/shard_map/ppermute | solution.py:351
  209.0 25.6 %collective-permute-start.24 = (bf16[2,5,128,128]{3,2,1,0:T(8,128)(2,1)S(1)}, bf16[2,5,128,128]{3,2,1,0:T(8,128)(2,1)S(1)}, u32[]{:S(2)}, u32[]{:S(2)}) collective-permute-start(bf16[2,5,128,128]{3,2,1,0:T(8,128)(2,1)S(1)} %get-tuple-element.81), channel_id=1, source_target_pairs={{0,4},{1,5},{2,6},{3,7},{4,0},{5,1},{6,2},{7,3},{8,12},{9,13},{10,... | collective-permute-start | bytes 983048 | tf_op jit(solution)/shard_map/ppermute | solution.py:351
  209.3 25.3 %collective-permute-start.25 = (bf16[2,5,128,128]{3,2,1,0:T(8,128)(2,1)S(1)}, bf16[2,5,128,128]{3,2,1,0:T(8,128)(2,1)S(1)}, u32[]{:S(2)}, u32[]{:S(2)}) collective-permute-start(bf16[2,5,128,128]{3,2,1,0:T(8,128)(2,1)S(1)} %get-tuple-element.82), channel_id=1, source_target_pairs={{0,3},{1,4},{2,5},{3,6},{4,7},{5,0},{6,1},{7,2},{8,11},{9,12},{10,... | collective-permute-start | bytes 983048 | tf_op jit(solution)/shard_map/ppermute | solution.py:351
  212.0 22.6 %collective-permute-start.26 = (bf16[2,5,128,128]{3,2,1,0:T(8,128)(2,1)S(1)}, bf16[2,5,128,128]{3,2,1,0:T(8,128)(2,1)S(1)}, u32[]{:S(2)}, u32[]{:S(2)}) collective-permute-start(bf16[2,5,128,128]{3,2,1,0:T(8,128)(2,1)S(1)} %get-tuple-element.83), channel_id=1, source_target_pairs={{0,2},{1,3},{2,4},{3,5},{4,6},{5,7},{6,0},{7,1},{8,10},{9,11},{10,... | collective-permute-start | bytes 983048 | tf_op jit(solution)/shard_map/ppermute | solution.py:351
  216.6 21.1 %collective-permute-start.27 = (bf16[2,5,128,128]{3,2,1,0:T(8,128)(2,1)S(1)}, bf16[2,5,128,128]{3,2,1,0:T(8,128)(2,1)S(1)}, u32[]{:S(2)}, u32[]{:S(2)}) collective-permute-start(bf16[2,5,128,128]{3,2,1,0:T(8,128)(2,1)S(1)} %get-tuple-element.84), channel_id=1, source_target_pairs={{0,1},{1,2},{2,3},{3,4},{4,5},{5,6},{6,7},{7,0},{8,9},{9,10},{10,1... | collective-permute-start | bytes 983048 | tf_op jit(solution)/shard_map/ppermute | solution.py:351

commit v3 on v2

--- a/solution.py
+++ b/solution.py
@@ -40,12 +40,17 @@
     return pl.BlockSpec(memory_space=pltpu.VMEM)
 
 
+def array_of(shape, i):
+    lead = len(shape) - 4
+    return pl.BlockSpec((1, *shape[1 : 1 + lead], None, *shape[-2:]), lambda h: (i,) + (0,) * lead + (h, 0, 0))
+
+
 def stat_block(own):
     return pl.BlockSpec((1, 8, own), lambda h: (h, 0, 0))
 
 
-def params():
-    return pltpu.CompilerParams(vmem_limit_bytes=VMEM_LIMIT, dimension_semantics=("arbitrary",))
+def params(limit=VMEM_LIMIT):
+    return pltpu.CompilerParams(vmem_limit_bytes=limit, dimension_semantics=("arbitrary",))
 
 
 def dot(a, b, dims):
@@ -109,75 +114,70 @@
     )(kv, qd)
 
 
-def memory_kernel(kc, lists_ref, stat_ref, recv_ref, qd_ref, ret_ref, fin_ref, k_s, v_s):
+def memory_kernel(tq, lists_ref, stat_ref, recv_ref, q_ref, d_ref, ret_ref, fin_ref, k_s, v_s, g_s):
     mem, own = k_s.shape[0], stat_ref.shape[2]
-    count = lists_ref[mem // FBLK]
+    memd = mem // FBLK
+    count = lists_ref[memd]
+    sure = LEAST_LIVE * FBLK
     load_memory(lists_ref, recv_ref, k_s, v_s)
-    q, d = rows_of(qd_ref, 0, 0, own), rows_of(qd_ref, 1, 0, own)
-    top_own = stat_ref[0, 0:1]
-    top = top_own
-    scores = []
-    for c in range(0, mem, kc):
-        s = dot(k_s[c : c + kc], q, NT)
-        if c + kc > LEAST_LIVE * FBLK:
-            s = masked(s, count, c)
-        top = jnp.maximum(top, jnp.max(s, axis=0, keepdims=True))
-        scores.append(s)
-    shrink = jnp.exp2((top_own - top) * TO_EXP2)
-    norm = stat_ref[0, 1:2] * shrink
-    mix = stat_ref[0, 2:3] * shrink
-    parts = []
-    for i, s in enumerate(scores):
+
+    def products(t):
+        q, d = rows_of(q_ref, 0, t, tq), rows_of(d_ref, 0, t, tq)
+        s, dp = dot(k_s[...], q, NT), dot(v_s[...], d, NT)
+        return q, d, jnp.concatenate([s[:sure], masked(s[sure:], count, sure)]), dp
+
+    def terms(t, q, d, s, dp):
+        qs = slice(t, t + tq)
+        top_own = stat_ref[0, 0:1, qs]
+        top = jnp.maximum(top_own, jnp.max(s, axis=0, keepdims=True))
+        shrink = jnp.exp2((top_own - top) * TO_EXP2)
         e = jnp.exp2((s - top) * TO_EXP2)
-        dp = dot(v_s[i * kc : (i + 1) * kc], d, NT)
-        norm = norm + column_sum(e)
-        mix = mix + column_sum(e * dp)
-        parts.append((e, dp))
-    inv = 1.0 / norm
-    delta = mix * inv
-    for i, (e, dp) in enumerate(parts):
+        inv = 1.0 / (stat_ref[0, 1:2, qs] * shrink + column_sum(e))
+        delta = (stat_ref[0, 2:3, qs] * shrink + column_sum(e * dp)) * inv
+        fin_ref[0, 0:1, qs] = top
+        fin_ref[0, 1:2, qs] = inv
+        fin_ref[0, 2:3, qs] = delta
         p = e * inv
-        ds = (p * (dp - delta)).astype(BF16)
-        gk = (dot(ds, q, NN) * SCALE).astype(BF16)
-        gv = dot(p.astype(BF16), d, NN).astype(BF16)
-        for j in range(kc // FBLK):
-            rows = slice(j * FBLK, (j + 1) * FBLK)
-            at = lists_ref[i * (kc // FBLK) + j]
-            if (i + 1) * kc <= LEAST_LIVE * FBLK:
-                ret_ref[at, 0] = gk[rows]
-                ret_ref[at, 1] = gv[rows]
-            else:
-
-                @pl.when(i * (kc // FBLK) + j < count)
-                def _():
-                    ret_ref[at, 0] = gk[rows]
-                    ret_ref[at, 1] = gv[rows]
-
-    fin_ref[0, 0:1] = top
-    fin_ref[0, 1:2] = inv
-    fin_ref[0, 2:3] = delta
-
-
-def memory(lists, stat, recv, qd, kc=128):
+        gk = dot((p * (dp - delta)).astype(BF16), q, NN)
+        gv = dot(p.astype(BF16), d, NN)
+        g_s[0] = gk if t == 0 else g_s[0] + gk
+        g_s[1] = gv if t == 0 else g_s[1] + gv
+
+    ahead = products(0)
+    for t in range(0, own, tq):
+        now = ahead
+        if t + tq < own:
+            ahead = products(t + tq)
+        terms(t, *now)
+    for j in range(memd):
+        rows = slice(j * FBLK, (j + 1) * FBLK)
+
+        @pl.when(j < count)
+        def _():
+            ret_ref[lists_ref[j], 0] = (g_s[0, rows] * SCALE).astype(BF16)
+            ret_ref[lists_ref[j], 1] = g_s[1, rows].astype(BF16)
+
+
+def memory(lists, stat, recv, qd, tq=512):
     mem = (lists.shape[0] - 1) * FBLK
     nh, _, own = stat.shape
     width = nh * HD
     return pl.pallas_call(
-        functools.partial(memory_kernel, kc),
+        functools.partial(memory_kernel, tq),
         grid=(nh,),
         out_shape=(
             pltpu.HBM(recv.shape, BF16),
             jax.ShapeDtypeStruct((nh, 8, own), F32),
         ),
-        in_specs=[smem(), stat_block(own), per_head(recv.shape), per_head(qd.shape)],
+        in_specs=[smem(), stat_block(own), per_head(recv.shape), array_of(qd.shape, 0), array_of(qd.shape, 1)],
         out_specs=(per_head(recv.shape), stat_block(own)),
-        scratch_shapes=[pltpu.VMEM((mem, HD), BF16)] * 2,
-        compiler_params=params(),
+        scratch_shapes=[pltpu.VMEM((mem, HD), BF16)] * 2 + [pltpu.VMEM((2, mem, HD), F32)],
+        compiler_params=params(MOST_VMEM),
         cost_estimate=pl.CostEstimate(
             flops=8 * own * mem * width, bytes_accessed=8 * own * width, transcendentals=own * mem * nh
         ),
         name="memory",
-    )(lists, stat, recv, qd)
+    )(lists, stat, recv, qd, qd)
 
 
 def own_grads_kernel(kc, lists_ref, fin_ref, recv_ref, kv_ref, qd_ref, *refs):
@@ -233,17 +233,17 @@
 def collect_kernel(blocks_ref, own_ref, back_ref, *refs):
     *out_refs, acc = refs
     slots = back_ref.shape[0]
-    tok = acc.shape[1] // len(out_refs)
+    tok = acc.shape[2] // len(out_refs)
     acc[...] = own_ref[...]
     for s in range(slots):
 
         @pl.when(blocks_ref[slots + s] != 0)
         def _():
             rows = pl.ds(pl.multiple_of(blocks_ref[s] * FBLK, FBLK), FBLK)
-            acc[:, rows, :] += back_ref[s].astype(F32)
+            acc[:, :, rows, :] += back_ref[s].astype(F32)
 
     for i, ref in enumerate(out_refs):
-        ref[...] = acc[:, i * tok : (i + 1) * tok, :].astype(BF16)
+        ref[...] = acc[:, :, i * tok : (i + 1) * tok, :].astype(BF16)
 
 
 def collect(blocks, own, back, pieces):
@@ -251,12 +251,11 @@
     piece = (2, nh, rows // pieces, HD)
     return pl.pallas_call(
         collect_kernel,
-        grid=(nh,),
         out_shape=[jax.ShapeDtypeStruct(piece, BF16)] * pieces,
-        in_specs=[smem(), per_head(own.shape), per_head(back.shape)],
-        out_specs=[per_head(piece)] * pieces,
-        scratch_shapes=[pltpu.VMEM((2, rows, HD), F32)],
-        compiler_params=params(),
+        in_specs=[smem(), vmem(), vmem()],
+        out_specs=[vmem()] * pieces,
+        scratch_shapes=[pltpu.VMEM(own.shape, F32)],
+        compiler_params=pltpu.CompilerParams(vmem_limit_bytes=SMALL_LIMIT),
         name="collect",
     )(blocks, own, back)
 
@@ -322,13 +321,19 @@
 
 
 def place_kernel(count, me_ref, *refs):
+    out_refs, sems = refs[count:-1], refs[-1]
+    copies = []
     for k, ref in enumerate(refs[:count]):
         heads = ref.shape[1]
         of = lax.rem(me_ref[0] + k, count)
         for h in range(heads):
             columns = pl.ds(pl.multiple_of((of * heads + h) * HD, HD), HD)
-            for i, out_ref in enumerate(refs[count:]):
-                out_ref[:, columns] = ref[i, h]
+            for i, out_ref in enumerate(out_refs):
+                copies.append(pltpu.make_async_copy(ref.at[i, h], out_ref.at[:, columns], sems.at[i, k, h]))
+    for copy in copies:
+        copy.start()
+    for copy in copies:
+        copy.wait()
 
 
 def place(me, pieces):
@@ -336,9 +341,10 @@
     count = len(pieces)
     return pl.pallas_call(
         functools.partial(place_kernel, count),
-        out_shape=[jax.ShapeDtypeStruct((tok, nh * HD * count), BF16)] * arrays,
+        out_shape=[pltpu.HBM((tok, nh * HD * count), BF16)] * arrays,
         in_specs=[smem()] + [vmem()] * count,
-        out_specs=[vmem()] * arrays,
+        out_specs=[anywhere()] * arrays,
+        scratch_shapes=[pltpu.SemaphoreType.DMA((arrays, count, nh))],
         compiler_params=pltpu.CompilerParams(vmem_limit_bytes=SMALL_LIMIT),
         name="place",
     )(me, *pieces)

time: 242 us -> 239 us (0.988)
    unnamed x32 -> x36, local copies, waits for them, and re-layouts: 15.6 us -> 14.6 us
  transfers between devices with their start and end apart: 30 -> 30, of which waited for: 16 -> 16; matrix products, arithmetic and copies ran while one was open for 3% -> 3% of each run, Pallas kernels for 14% -> 15%
where the time goes in v3:
time: 239 us; the launch traced here: 237 us
  waiting for transfers between devices  92.3 us (39%)
  starting transfers between devices  69.4 us (29%)
  Pallas kernels  56.9 us (24%)
  local copies, waits for them, and re-layouts  15.5 us (6%)
    ppermute x28, waiting for transfers between devices, shift(): lax.ppermute(parts[k], 'head', [(i, (i + sign * k) % n) for i in range(n)])  67.4 us
    ppermute x28, starting transfers between devices, shift(): lax.ppermute(parts[k], 'head', [(i, (i + sign * k) % n) for i in range(n)])  53.2 us
    pallas_call x1, Pallas kernels, own_grads(): pl.pallas_call(functools.partial(own_grads_kernel, kc), grid=(nh,), out_s...  22.4 us
    unnamed x36, local copies, waits for them, and re-layouts  14.6 us
    all_to_all x1, waiting for transfers between devices, body(): back = lax.all_to_all(ret, 'tok', split_axis=0, concat_axis=0, tiled=True)  12.8 us
    pallas_call x1, Pallas kernels, memory(): pl.pallas_call(functools.partial(memory_kernel, tq), grid=(nh,), out_shap...  12.6 us
    all_to_all x1, waiting for transfers between devices, body(): recv = lax.all_to_all(sent, 'tok', split_axis=0, concat_axis=0, tiled=True)  12.1 us
    all_to_all x1, starting transfers between devices, body(): recv = lax.all_to_all(sent, 'tok', split_axis=0, concat_axis=0, tiled=True)  9.46 us
  transfers between devices with their start and end apart: 30, of which 16 were waited for; matrix products, arithmetic and copies ran while one was open for 3% of the time, Pallas kernels for 15%

profile of v3, /device:TPU:1, one launch (start us, length us, event | category | flops | bytes accessed | tf_op | source)
XLA Modules:
  0.0 236.7 jit_solution(13235872650483636135)
XLA Ops:
  0.7 3.4 %cut.2 = (bf16[2,5,128,128]{3,2,1,0:T(8,128)(2,1)}, bf16[2,5,128,128]{3,2,1,0:T(8,128)(2,1)}, bf16[2,5,128,128]{3,2,1,0:T(8,128)(2,1)}, bf16[2,5,128,128]{3,2,1,...) custom-call(s32[1]{0:T(128)} %bitcast.me_ref, ...), custom_call_target="tpu_custom_call" | custom-call | tf_op jit(solution)/shard_map/cut/pallas_call | solution.py:312
  4.1 2.7 %collective-permute-start = (bf16[2,5,128,128]{3,2,1,0:T(8,128)(2,1)}, bf16[2,5,128,128]{3,2,1,0:T(8,128)(2,1)}, u32[]{:S(2)}, u32[]{:S(2)}) collective-permute-start(bf16[2,5,128,128]{3,2,1,0:T(8,128)(2,1)} %get-tuple-element.46), channel_id=1, source_target_pairs={{0,1},{1,2},{2,3},{3,4},{4,5},{5,6},{6,7},{7,0},{8,9},{9,10},{10,1... | collective-permute-start | bytes 983048 | tf_op jit(solution)/shard_map/ppermute | solution.py:357
  6.8 1.3 collective-permute-start.1
  8.1 1.7 collective-permute-start.2
  9.8 1.3 collective-permute-start.3
  11.1 2.6 %collective-permute-start.4 = (bf16[2,5,128,128]{3,2,1,0:T(8,128)(2,1)}, bf16[2,5,128,128]{3,2,1,0:T(8,128)(2,1)S(1)}, u32[]{:S(2)}, u32[]{:S(2)}) collective-permute-start(bf16[2,5,128,128]{3,2,1,0:T(8,128)(2,1)} %get-tuple-element.50), channel_id=1, source_target_pairs={{0,5},{1,6},{2,7},{3,0},{4,1},{5,2},{6,3},{7,4},{8,13},{9,14},{10,... | collective-permute-start | bytes 983048 | tf_op jit(solution)/shard_map/ppermute | solution.py:357
  14.9 2.2 collective-permute-start.5
  18.2 7.2 %collective-permute-done.1 = bf16[2,5,128,128]{3,2,1,0:T(8,128)(2,1)} collective-permute-done((bf16[2,5,128,128]{3,2,1,0:T(8,128)(2,1)}, bf16[2,5,128,128]{3,2,1,0:T(8,128)(2,1)}, u32[]{:S(2)}, u32[]{:S(2)}) %collective-permute-start.1) | collective-permute-done | bytes 327712 | tf_op jit(solution)/shard_map/ppermute | solution.py:357
  26.4 12.9 %collective-permute-done.2 = bf16[2,5,128,128]{3,2,1,0:T(8,128)(2,1)} collective-permute-done((bf16[2,5,128,128]{3,2,1,0:T(8,128)(2,1)}, bf16[2,5,128,128]{3,2,1,0:T(8,128)(2,1)}, u32[]{:S(2)}, u32[]{:S(2)}) %collective-permute-start.2) | collective-permute-done | bytes 327712 | tf_op jit(solution)/shard_map/ppermute | solution.py:357
  40.5 2.6 %pick.1 = bf16[32,2,5,32,128]{4,3,2,1,0:T(8,128)(2,1)} custom-call(s32[64]{0:T(128)S(1)} %pad_add_fusion.1.blocks_ref, bf16[2,8,5,128,128]{4,3,2,1,0:T(8,128)(2,1)S(1)} %bitcast_dynamic-update-slice_fusion.8.kv_ref), custom_call_target="tpu_custom_call" | custom-call | tf_op jit(solution)/shard_map/pick/pallas_call | solution.py:280
  43.1 9.5 %all-to-all-start = ((bf16[32,2,5,32,128]{4,3,2,1,0:T(8,128)(2,1)}), bf16[32,2,5,32,128]{4,3,2,1,0:T(8,128)(2,1)}, u32[]{:S(2)}, u32[]{:S(2)}) async-start(bf16[32,2,5,32,128]{4,3,2,1,0:T(8,128)(2,1)} %pick.1), calls=%async_computation | async-start | bytes 5242880 | tf_op jit(solution)/shard_map/all_to_all | solution.py:382
  53.4 3.4 %cut.3 = (bf16[2,5,128,128]{3,2,1,0:T(8,128)(2,1)}, bf16[2,5,128,128]{3,2,1,0:T(8,128)(2,1)}, bf16[2,5,128,128]{3,2,1,0:T(8,128)(2,1)}, bf16[2,5,128,128]{3,2,1,...) custom-call(s32[1]{0:T(128)} %bitcast.me_ref, ...), custom_call_target="tpu_custom_call" | custom-call | tf_op jit(solution)/shard_map/cut/pallas_call | solution.py:312
  58.2 2.1 collective-permute-start.8
  61.3 1.8 collective-permute-start.9
  63.1 1.7 collective-permute-start.10
  65.6 6.3 %collective-permute-done.8 = bf16[2,5,128,128]{3,2,1,0:T(8,128)(2,1)S(1)} collective-permute-done((bf16[2,5,128,128]{3,2,1,0:T(8,128)(2,1)}, bf16[2,5,128,128]{3,2,1,0:T(8,128)(2,1)S(1)}, u32[]{:S(2)}, u32[]{:S(2)}) %collective-permute-start.8) | collective-permute-done | bytes 327712 | tf_op jit(solution)/shard_map/ppermute | solution.py:357
  72.0 4.9 %collective-permute-done.9 = bf16[2,5,128,128]{3,2,1,0:T(8,128)(2,1)S(1)} collective-permute-done((bf16[2,5,128,128]{3,2,1,0:T(8,128)(2,1)}, bf16[2,5,128,128]{3,2,1,0:T(8,128)(2,1)S(1)}, u32[]{:S(2)}, u32[]{:S(2)}) %collective-permute-start.9) | collective-permute-done | bytes 327712 | tf_op jit(solution)/shard_map/ppermute | solution.py:357
  76.9 9.7 %collective-permute-done.10 = bf16[2,5,128,128]{3,2,1,0:T(8,128)(2,1)S(1)} collective-permute-done((bf16[2,5,128,128]{3,2,1,0:T(8,128)(2,1)}, bf16[2,5,128,128]{3,2,1,0:T(8,128)(2,1)S(1)}, u32[]{:S(2)}, u32[]{:S(2)}) %collective-permute-start.10) | collective-permute-done | bytes 327712 | tf_op jit(solution)/shard_map/ppermute | solution.py:357
  86.7 2.7 %collective-permute-done.11 = bf16[2,5,128,128]{3,2,1,0:T(8,128)(2,1)S(1)} collective-permute-done((bf16[2,5,128,128]{3,2,1,0:T(8,128)(2,1)}, bf16[2,5,128,128]{3,2,1,0:T(8,128)(2,1)S(1)}, u32[]{:S(2)}, u32[]{:S(2)}) %collective-permute-start.11) | collective-permute-done | bytes 327712 | tf_op jit(solution)/shard_map/ppermute | solution.py:357
  89.4 2.3 collective-permute-done.12
  92.9 7.4 %own_stats.1.stat_ref = f32[5,8,1024]{2,1,0:T(8,128)S(1)} custom-call(bf16[2,8,5,128,128]{4,3,2,1,0:T(8,128)(2,1)S(1)} %bitcast_dynamic-update-slice_fusion.8.kv_ref, bf16[2,8,5,128,128]{4,3,2,1,0:T(8,128)(2,1)S(1)} %bitcast_dynamic-update-slice_fusion.qd_ref.q_ref.d_ref), custom_call_target="tpu_custom_call" | custom-call | flops 2684354560 | bytes 5242880 | tf_op jit(solution)/shard_map/own_stats/pallas_call | solution.py:102
  100.4 1.6 copy-done.4
  102.6 12.1 %all-to-all-done.recv_ref = bf16[32,2,5,32,128]{4,3,2,1,0:T(8,128)(2,1)} async-done(((bf16[32,2,5,32,128]{4,3,2,1,0:T(8,128)(2,1)}), bf16[32,2,5,32,128]{4,3,2,1,0:T(8,128)(2,1)}, u32[]{:S(2)}, u32[]{:S(2)}) %all-to-all-start) | async-done | bytes 2621472 | tf_op jit(solution)/shard_map/all_to_all | solution.py:382
  114.7 12.6 %memory.1 = (bf16[32,2,5,32,128]{4,3,2,1,0:T(8,128)(2,1)}, f32[5,8,1024]{2,1,0:T(8,128)}) custom-call(s32[17]{0:T(128)} %pad_add_fusion.lists_ref, f32[5,8,1024]{2,1,0:T(8,128)} %copy-done.8, bf16[32,2,5,32,128]{4,3,2,1,0:T(8,128)(2,1)} %all-to-all-done.recv_ref, bf16[2,8,5,128,128]{4,3,2,1,0:T(8,128)(2,1)} %copy-done.4, bf16[2,8,5,128,128]{4,3,2,1,0:T(8,128)(2,1)} %copy-done.4), custom_call_target="tpu_custom_call" | custom-call | flops 2684354560 | bytes 5242880 | tf_op jit(solution)/shard_map/memory/pallas_call | solution.py:165
  127.3 6.8 %all-to-all-start.1 = ((bf16[32,2,5,32,128]{4,3,2,1,0:T(8,128)(2,1)}), bf16[32,2,5,32,128]{4,3,2,1,0:T(8,128)(2,1)S(1)}, u32[]{:S(2)}, u32[]{:S(2)}) async-start(bf16[32,2,5,32,128]{4,3,2,1,0:T(8,128)(2,1)} %get-tuple-element.64), calls=%async_computation.1 | async-start | bytes 5242880 | tf_op jit(solution)/shard_map/all_to_all | solution.py:386
  134.1 1.7 copy-done.2
  135.8 1.7 copy-done.5
  137.6 22.4 %own_grads.1 = (bf16[1,5,128,128]{3,2,1,0:T(8,128)(2,1)}, bf16[1,5,128,128]{3,2,1,0:T(8,128)(2,1)}, bf16[1,5,128,128]{3,2,1,0:T(8,128)(2,1)}, bf16[1,5,128,128]{...) custom-call(s32[17]{0:T(128)S(1)} %copy-done.6, ...), custom_call_target="tpu_custom_call" | custom-call | flops 10066329600 | bytes 10485760 | tf_op jit(solution)/shard_map/own_grads/pallas_call | solution.py:217
  160.8 1.7 collective-permute-start.15
  162.5 1.4 collective-permute-start.16
  163.9 1.7 collective-permute-start.17
  165.6 1.3 collective-permute-start.18
  166.9 1.3 collective-permute-start.19
  168.2 3.6 %collective-permute-start.20 = (bf16[1,5,128,128]{3,2,1,0:T(8,128)(2,1)}, bf16[1,5,128,128]{3,2,1,0:T(8,128)(2,1)S(1)}, u32[]{:S(2)}, u32[]{:S(2)}) collective-permute-start(bf16[1,5,128,128]{3,2,1,0:T(8,128)(2,1)} %get-tuple-element.73), channel_id=1, source_target_pairs={{0,1},{1,2},{2,3},{3,4},{4,5},{5,6},{6,7},{7,0},{8,9},{9,10},{10,1... | collective-permute-start | bytes 491528 | tf_op jit(solution)/shard_map/ppermute | solution.py:357
  171.8 5.5 %collective-permute-done.16.refs_3_ = bf16[1,5,128,128]{3,2,1,0:T(8,128)(2,1)S(1)} collective-permute-done((bf16[1,5,128,128]{3,2,1,0:T(8,128)(2,1)}, bf16[1,5,128,128]{3,2,1,0:T(8,128)(2,1)S(1)}, u32[]{:S(2)}, u32[]{:S(2)}) %collective-permute-start.16) | collective-permute-done | bytes 163872 | tf_op jit(solution)/shard_map/ppermute | solution.py:357
  179.8 1.4 place.2
  181.2 12.8 %all-to-all-done.1.back_ref = bf16[32,2,5,32,128]{4,3,2,1,0:T(8,128)(2,1)S(1)} async-done(((bf16[32,2,5,32,128]{4,3,2,1,0:T(8,128)(2,1)}), bf16[32,2,5,32,128]{4,3,2,1,0:T(8,128)(2,1)S(1)}, u32[]{:S(2)}, u32[]{:S(2)}) %all-to-all-start.1) | async-done | bytes 2621472 | tf_op jit(solution)/shard_map/all_to_all | solution.py:386
  194.0 2.5 %copy-done = f32[2,5,1024,128]{3,2,1,0:T(8,128)S(1)} copy-done((f32[2,5,1024,128]{3,2,1,0:T(8,128)S(1)}, f32[2,5,1024,128]{3,2,1,0:T(8,128)}, u32[]{:S(2)}) %copy-start) | copy-done | bytes 5242904
  196.5 1.6 collect.1
  198.0 4.5 %collective-permute-start.21 = (bf16[2,5,128,128]{3,2,1,0:T(8,128)(2,1)S(1)}, bf16[2,5,128,128]{3,2,1,0:T(8,128)(2,1)S(1)}, u32[]{:S(2)}, u32[]{:S(2)}) collective-permute-start(bf16[2,5,128,128]{3,2,1,0:T(8,128)(2,1)S(1)} %get-tuple-element.78), channel_id=1, source_target_pairs={{0,7},{1,0},{2,1},{3,2},{4,3},{5,4},{6,5},{7,6},{8,15},{9,8},{10,9... | collective-permute-start | bytes 983048 | tf_op jit(solution)/shard_map/ppermute | solution.py:357
  202.5 1.8 collective-permute-start.22
  204.3 1.4 collective-permute-start.23
  206.0 2.7 %collective-permute-start.25 = (bf16[2,5,128,128]{3,2,1,0:T(8,128)(2,1)S(1)}, bf16[2,5,128,128]{3,2,1,0:T(8,128)(2,1)S(1)}, u32[]{:S(2)}, u32[]{:S(2)}) collective-permute-start(bf16[2,5,128,128]{3,2,1,0:T(8,128)(2,1)S(1)} %get-tuple-element.82), channel_id=1, source_target_pairs={{0,3},{1,4},{2,5},{3,6},{4,7},{5,0},{6,1},{7,2},{8,11},{9,12},{10,... | collective-permute-start | bytes 983048 | tf_op jit(solution)/shard_map/ppermute | solution.py:357
  208.7 4.6 %collective-permute-start.26 = (bf16[2,5,128,128]{3,2,1,0:T(8,128)(2,1)S(1)}, bf16[2,5,128,128]{3,2,1,0:T(8,128)(2,1)S(1)}, u32[]{:S(2)}, u32[]{:S(2)}) collective-permute-start(bf16[2,5,128,128]{3,2,1,0:T(8,128)(2,1)S(1)} %get-tuple-element.83), channel_id=1, source_target_pairs={{0,2},{1,3},{2,4},{3,5},{4,6},{5,7},{6,0},{7,1},{8,10},{9,11},{10,... | collective-permute-start | bytes 983048 | tf_op jit(solution)/shard_map/ppermute | solution.py:357
  213.3 7.9 %collective-permute-start.27 = (bf16[2,5,128,128]{3,2,1,0:T(8,128)(2,1)S(1)}, bf16[2,5,128,128]{3,2,1,0:T(8,128)(2,1)S(1)}, u32[]{:S(2)}, u32[]{:S(2)}) collective-permute-start(bf16[2,5,128,128]{3,2,1,0:T(8,128)(2,1)S(1)} %get-tuple-element.84), channel_id=1, source_target_pairs={{0,1},{1,2},{2,3},{3,4},{4,5},{5,6},{6,7},{7,0},{8,9},{9,10},{10,1... | collective-permute-start | bytes 983048 | tf_op jit(solution)/shard_map/ppermute | solution.py:357
  221.1 10.2 %collective-permute-done.23.refs_3_ = bf16[2,5,128,128]{3,2,1,0:T(8,128)(2,1)S(1)} collective-permute-done((bf16[2,5,128,128]{3,2,1,0:T(8,128)(2,1)S(1)}, bf16[2,5,128,128]{3,2,1,0:T(8,128)(2,1)S(1)}, u32[]{:S(2)}, u32[]{:S(2)}) %collective-permute-start.23) | collective-permute-done | bytes 327712 | tf_op jit(solution)/shard_map/ppermute | solution.py:357
  231.3 3.1 %collective-permute-done.27.refs_7_ = bf16[2,5,128,128]{3,2,1,0:T(8,128)(2,1)S(1)} collective-permute-done((bf16[2,5,128,128]{3,2,1,0:T(8,128)(2,1)S(1)}, bf16[2,5,128,128]{3,2,1,0:T(8,128)(2,1)S(1)}, u32[]{:S(2)}, u32[]{:S(2)}) %collective-permute-start.27) | collective-permute-done | bytes 327712 | tf_op jit(solution)/shard_map/ppermute | solution.py:357
  234.4 2.2 place.3
  (68 shorter events, 14.0 us)
Async XLA Ops:
  0.6 14.1 %copy-start.10 = (s32[32]{0:T(128)S(1)}, s32[32]{0:T(128)}, u32[]{:S(2)}) copy-start(s32[32]{0:T(128)} %param.11) | copy-start | bytes 388
  0.6 14.1 %copy-start.9 = (s32[32,16]{0,1:T(8,128)S(1)}, s32[32,16]{0,1:T(8,128)}, u32[]{:S(2)}) copy-start(s32[32,16]{0,1:T(8,128)} %param.10) | copy-start | bytes 6148
  4.1 10.8 %collective-permute-start = (bf16[2,5,128,128]{3,2,1,0:T(8,128)(2,1)}, bf16[2,5,128,128]{3,2,1,0:T(8,128)(2,1)}, u32[]{:S(2)}, u32[]{:S(2)}) collective-permute-start(bf16[2,5,128,128]{3,2,1,0:T(8,128)(2,1)} %get-tuple-element.46), channel_id=1, source_target_pairs={{0,1},{1,2},{2,3},{3,4},{4,5},{5,6},{6,7},{7,0},{8,9},{9,10},{10,1... | collective-permute-start | bytes 983048 | tf_op jit(solution)/shard_map/ppermute | solution.py:357
  6.8 18.6 %collective-permute-start.1 = (bf16[2,5,128,128]{3,2,1,0:T(8,128)(2,1)}, bf16[2,5,128,128]{3,2,1,0:T(8,128)(2,1)}, u32[]{:S(2)}, u32[]{:S(2)}) collective-permute-start(bf16[2,5,128,128]{3,2,1,0:T(8,128)(2,1)} %get-tuple-element.47), channel_id=1, source_target_pairs={{0,2},{1,3},{2,4},{3,5},{4,6},{5,7},{6,0},{7,1},{8,10},{9,11},{10,... | collective-permute-start | bytes 983048 | tf_op jit(solution)/shard_map/ppermute | solution.py:357
  8.1 31.2 %collective-permute-start.2 = (bf16[2,5,128,128]{3,2,1,0:T(8,128)(2,1)}, bf16[2,5,128,128]{3,2,1,0:T(8,128)(2,1)}, u32[]{:S(2)}, u32[]{:S(2)}) collective-permute-start(bf16[2,5,128,128]{3,2,1,0:T(8,128)(2,1)} %get-tuple-element.48), channel_id=1, source_target_pairs={{0,3},{1,4},{2,5},{3,6},{4,7},{5,0},{6,1},{7,2},{8,11},{9,12},{10,... | collective-permute-start | bytes 983048 | tf_op jit(solution)/shard_map/ppermute | solution.py:357
  9.8 30.5 %collective-permute-start.3 = (bf16[2,5,128,128]{3,2,1,0:T(8,128)(2,1)}, bf16[2,5,128,128]{3,2,1,0:T(8,128)(2,1)S(1)}, u32[]{:S(2)}, u32[]{:S(2)}) collective-permute-start(bf16[2,5,128,128]{3,2,1,0:T(8,128)(2,1)} %get-tuple-element.49), channel_id=1, source_target_pairs={{0,4},{1,5},{2,6},{3,7},{4,0},{5,1},{6,2},{7,3},{8,12},{9,13},{10,... | collective-permute-start | bytes 983048 | tf_op jit(solution)/shard_map/ppermute | solution.py:357
  11.1 29.3 %collective-permute-start.4 = (bf16[2,5,128,128]{3,2,1,0:T(8,128)(2,1)}, bf16[2,5,128,128]{3,2,1,0:T(8,128)(2,1)S(1)}, u32[]{:S(2)}, u32[]{:S(2)}) collective-permute-start(bf16[2,5,128,128]{3,2,1,0:T(8,128)(2,1)} %get-tuple-element.50), channel_id=1, source_target_pairs={{0,5},{1,6},{2,7},{3,0},{4,1},{5,2},{6,3},{7,4},{8,13},{9,14},{10,... | collective-permute-start | bytes 983048 | tf_op jit(solution)/shard_map/ppermute | solution.py:357
  14.9 25.5 %collective-permute-start.5 = (bf16[2,5,128,128]{3,2,1,0:T(8,128)(2,1)}, bf16[2,5,128,128]{3,2,1,0:T(8,128)(2,1)S(1)}, u32[]{:S(2)}, u32[]{:S(2)}) collective-permute-start(bf16[2,5,128,128]{3,2,1,0:T(8,128)(2,1)} %get-tuple-element.51), channel_id=1, source_target_pairs={{0,6},{1,7},{2,0},{3,1},{4,2},{5,3},{6,4},{7,5},{8,14},{9,15},{10,... | collective-permute-start | bytes 983048 | tf_op jit(solution)/shard_map/ppermute | solution.py:357
  25.4 15.1 %collective-permute-start.6 = (bf16[2,5,128,128]{3,2,1,0:T(8,128)(2,1)}, bf16[2,5,128,128]{3,2,1,0:T(8,128)(2,1)S(1)}, u32[]{:S(2)}, u32[]{:S(2)}) collective-permute-start(bf16[2,5,128,128]{3,2,1,0:T(8,128)(2,1)} %get-tuple-element.52), channel_id=1, source_target_pairs={{0,7},{1,0},{2,1},{3,2},{4,3},{5,4},{6,5},{7,6},{8,15},{9,8},{10,9... | collective-permute-start | bytes 983048 | tf_op jit(solution)/shard_map/ppermute | solution.py:357
  40.5 52.4 %copy-start.1 = (bf16[2,8,5,128,128]{4,3,2,1,0:T(8,128)(2,1)}, bf16[2,8,5,128,128]{4,3,2,1,0:T(8,128)(2,1)S(1)}, u32[]{:S(2)}) copy-start(bf16[2,8,5,128,128]{4,3,2,1,0:T(8,128)(2,1)S(1)} %bitcast_dynamic-update-slice_fusion.8.kv_ref) | copy-start | bytes 7864324
  43.1 71.6 %all-to-all-start = ((bf16[32,2,5,32,128]{4,3,2,1,0:T(8,128)(2,1)}), bf16[32,2,5,32,128]{4,3,2,1,0:T(8,128)(2,1)}, u32[]{:S(2)}, u32[]{:S(2)}) async-start(bf16[32,2,5,32,128]{4,3,2,1,0:T(8,128)(2,1)} %pick.1), calls=%async_computation | async-start | bytes 5242880 | tf_op jit(solution)/shard_map/all_to_all | solution.py:382
  56.9 8.4 %collective-permute-start.7 = (bf16[2,5,128,128]{3,2,1,0:T(8,128)(2,1)}, bf16[2,5,128,128]{3,2,1,0:T(8,128)(2,1)S(1)}, u32[]{:S(2)}, u32[]{:S(2)}) collective-permute-start(bf16[2,5,128,128]{3,2,1,0:T(8,128)(2,1)} %get-tuple-element.56), channel_id=1, source_target_pairs={{0,1},{1,2},{2,3},{3,4},{4,5},{5,6},{6,7},{7,0},{8,9},{9,10},{10,1... | collective-permute-start | bytes 983048 | tf_op jit(solution)/shard_map/ppermute | solution.py:357
  58.2 13.7 %collective-permute-start.8 = (bf16[2,5,128,128]{3,2,1,0:T(8,128)(2,1)}, bf16[2,5,128,128]{3,2,1,0:T(8,128)(2,1)S(1)}, u32[]{:S(2)}, u32[]{:S(2)}) collective-permute-start(bf16[2,5,128,128]{3,2,1,0:T(8,128)(2,1)} %get-tuple-element.57), channel_id=1, source_target_pairs={{0,2},{1,3},{2,4},{3,5},{4,6},{5,7},{6,0},{7,1},{8,10},{9,11},{10,... | collective-permute-start | bytes 983048 | tf_op jit(solution)/shard_map/ppermute | solution.py:357
  61.3 15.6 %collective-permute-start.9 = (bf16[2,5,128,128]{3,2,1,0:T(8,128)(2,1)}, bf16[2,5,128,128]{3,2,1,0:T(8,128)(2,1)S(1)}, u32[]{:S(2)}, u32[]{:S(2)}) collective-permute-start(bf16[2,5,128,128]{3,2,1,0:T(8,128)(2,1)} %get-tuple-element.58), channel_id=1, source_target_pairs={{0,3},{1,4},{2,5},{3,6},{4,7},{5,0},{6,1},{7,2},{8,11},{9,12},{10,... | collective-permute-start | bytes 983048 | tf_op jit(solution)/shard_map/ppermute | solution.py:357
  63.1 23.5 %collective-permute-start.10 = (bf16[2,5,128,128]{3,2,1,0:T(8,128)(2,1)}, bf16[2,5,128,128]{3,2,1,0:T(8,128)(2,1)S(1)}, u32[]{:S(2)}, u32[]{:S(2)}) collective-permute-start(bf16[2,5,128,128]{3,2,1,0:T(8,128)(2,1)} %get-tuple-element.59), channel_id=1, source_target_pairs={{0,4},{1,5},{2,6},{3,7},{4,0},{5,1},{6,2},{7,3},{8,12},{9,13},{10,... | collective-permute-start | bytes 983048 | tf_op jit(solution)/shard_map/ppermute | solution.py:357
  64.8 24.5 %collective-permute-start.11 = (bf16[2,5,128,128]{3,2,1,0:T(8,128)(2,1)}, bf16[2,5,128,128]{3,2,1,0:T(8,128)(2,1)S(1)}, u32[]{:S(2)}, u32[]{:S(2)}) collective-permute-start(bf16[2,5,128,128]{3,2,1,0:T(8,128)(2,1)} %get-tuple-element.60), channel_id=1, source_target_pairs={{0,5},{1,6},{2,7},{3,0},{4,1},{5,2},{6,3},{7,4},{8,13},{9,14},{10,... | collective-permute-start | bytes 983048 | tf_op jit(solution)/shard_map/ppermute | solution.py:357
  65.3 26.4 %collective-permute-start.12 = (bf16[2,5,128,128]{3,2,1,0:T(8,128)(2,1)}, bf16[2,5,128,128]{3,2,1,0:T(8,128)(2,1)S(1)}, u32[]{:S(2)}, u32[]{:S(2)}) collective-permute-start(bf16[2,5,128,128]{3,2,1,0:T(8,128)(2,1)} %get-tuple-element.61), channel_id=1, source_target_pairs={{0,6},{1,7},{2,0},{3,1},{4,2},{5,3},{6,4},{7,5},{8,14},{9,15},{10,... | collective-permute-start | bytes 983048 | tf_op jit(solution)/shard_map/ppermute | solution.py:357
  71.9 20.9 %collective-permute-start.13 = (bf16[2,5,128,128]{3,2,1,0:T(8,128)(2,1)}, bf16[2,5,128,128]{3,2,1,0:T(8,128)(2,1)S(1)}, u32[]{:S(2)}, u32[]{:S(2)}) collective-permute-start(bf16[2,5,128,128]{3,2,1,0:T(8,128)(2,1)} %get-tuple-element.62), channel_id=1, source_target_pairs={{0,7},{1,0},{2,1},{3,2},{4,3},{5,4},{6,5},{7,6},{8,15},{9,8},{10,9... | collective-permute-start | bytes 983048 | tf_op jit(solution)/shard_map/ppermute | solution.py:357
  100.3 1.6 copy-start.4
  101.9 0.7 copy-start.8
  127.3 6.8 %copy-start.6 = (s32[17]{0:T(128)S(1)}, s32[17]{0:T(128)}, u32[]{:S(2)}) copy-start(s32[17]{0:T(128)} %pad_add_fusion.lists_ref) | copy-start | bytes 208
  127.3 6.8 %copy-start.7 = (f32[5,8,1024]{2,1,0:T(8,128)S(1)}, f32[5,8,1024]{2,1,0:T(8,128)}, u32[]{:S(2)}) copy-start(f32[5,8,1024]{2,1,0:T(8,128)} %get-tuple-element.65.fin_ref) | copy-start | bytes 491524
  127.3 66.7 %all-to-all-start.1 = ((bf16[32,2,5,32,128]{4,3,2,1,0:T(8,128)(2,1)}), bf16[32,2,5,32,128]{4,3,2,1,0:T(8,128)(2,1)S(1)}, u32[]{:S(2)}, u32[]{:S(2)}) async-start(bf16[32,2,5,32,128]{4,3,2,1,0:T(8,128)(2,1)} %get-tuple-element.64), calls=%async_computation.1 | async-start | bytes 5242880 | tf_op jit(solution)/shard_map/all_to_all | solution.py:386
  134.1 1.7 copy-start.2
  135.8 1.7 copy-start.5
  160.0 6.9 %collective-permute-start.14 = (bf16[1,5,128,128]{3,2,1,0:T(8,128)(2,1)}, bf16[1,5,128,128]{3,2,1,0:T(8,128)(2,1)S(1)}, u32[]{:S(2)}, u32[]{:S(2)}) collective-permute-start(bf16[1,5,128,128]{3,2,1,0:T(8,128)(2,1)} %get-tuple-element.67), channel_id=1, source_target_pairs={{0,7},{1,0},{2,1},{3,2},{4,3},{5,4},{6,5},{7,6},{8,15},{9,8},{10,9... | collective-permute-start | bytes 491528 | tf_op jit(solution)/shard_map/ppermute | solution.py:357
  160.8 7.4 %collective-permute-start.15 = (bf16[1,5,128,128]{3,2,1,0:T(8,128)(2,1)}, bf16[1,5,128,128]{3,2,1,0:T(8,128)(2,1)S(1)}, u32[]{:S(2)}, u32[]{:S(2)}) collective-permute-start(bf16[1,5,128,128]{3,2,1,0:T(8,128)(2,1)} %get-tuple-element.68), channel_id=1, source_target_pairs={{0,6},{1,7},{2,0},{3,1},{4,2},{5,3},{6,4},{7,5},{8,14},{9,15},{10,... | collective-permute-start | bytes 491528 | tf_op jit(solution)/shard_map/ppermute | solution.py:357
  162.5 14.8 %collective-permute-start.16 = (bf16[1,5,128,128]{3,2,1,0:T(8,128)(2,1)}, bf16[1,5,128,128]{3,2,1,0:T(8,128)(2,1)S(1)}, u32[]{:S(2)}, u32[]{:S(2)}) collective-permute-start(bf16[1,5,128,128]{3,2,1,0:T(8,128)(2,1)} %get-tuple-element.69), channel_id=1, source_target_pairs={{0,5},{1,6},{2,7},{3,0},{4,1},{5,2},{6,3},{7,4},{8,13},{9,14},{10,... | collective-permute-start | bytes 491528 | tf_op jit(solution)/shard_map/ppermute | solution.py:357
  163.9 13.4 %collective-permute-start.17 = (bf16[1,5,128,128]{3,2,1,0:T(8,128)(2,1)}, bf16[1,5,128,128]{3,2,1,0:T(8,128)(2,1)S(1)}, u32[]{:S(2)}, u32[]{:S(2)}) collective-permute-start(bf16[1,5,128,128]{3,2,1,0:T(8,128)(2,1)} %get-tuple-element.70), channel_id=1, source_target_pairs={{0,4},{1,5},{2,6},{3,7},{4,0},{5,1},{6,2},{7,3},{8,12},{9,13},{10,... | collective-permute-start | bytes 491528 | tf_op jit(solution)/shard_map/ppermute | solution.py:357
  165.6 12.2 %collective-permute-start.18 = (bf16[1,5,128,128]{3,2,1,0:T(8,128)(2,1)}, bf16[1,5,128,128]{3,2,1,0:T(8,128)(2,1)S(1)}, u32[]{:S(2)}, u32[]{:S(2)}) collective-permute-start(bf16[1,5,128,128]{3,2,1,0:T(8,128)(2,1)} %get-tuple-element.71), channel_id=1, source_target_pairs={{0,3},{1,4},{2,5},{3,6},{4,7},{5,0},{6,1},{7,2},{8,11},{9,12},{10,... | collective-permute-start | bytes 491528 | tf_op jit(solution)/shard_map/ppermute | solution.py:357
  166.9 11.2 %collective-permute-start.19 = (bf16[1,5,128,128]{3,2,1,0:T(8,128)(2,1)}, bf16[1,5,128,128]{3,2,1,0:T(8,128)(2,1)S(1)}, u32[]{:S(2)}, u32[]{:S(2)}) collective-permute-start(bf16[1,5,128,128]{3,2,1,0:T(8,128)(2,1)} %get-tuple-element.72), channel_id=1, source_target_pairs={{0,2},{1,3},{2,4},{3,5},{4,6},{5,7},{6,0},{7,1},{8,10},{9,11},{10,... | collective-permute-start | bytes 491528 | tf_op jit(solution)/shard_map/ppermute | solution.py:357
  168.2 10.7 %collective-permute-start.20 = (bf16[1,5,128,128]{3,2,1,0:T(8,128)(2,1)}, bf16[1,5,128,128]{3,2,1,0:T(8,128)(2,1)S(1)}, u32[]{:S(2)}, u32[]{:S(2)}) collective-permute-start(bf16[1,5,128,128]{3,2,1,0:T(8,128)(2,1)} %get-tuple-element.73), channel_id=1, source_target_pairs={{0,1},{1,2},{2,3},{3,4},{4,5},{5,6},{6,7},{7,0},{8,9},{9,10},{10,1... | collective-permute-start | bytes 491528 | tf_op jit(solution)/shard_map/ppermute | solution.py:357
  178.9 0.9 copy-start.3
  194.0 2.5 %copy-start = (f32[2,5,1024,128]{3,2,1,0:T(8,128)S(1)}, f32[2,5,1024,128]{3,2,1,0:T(8,128)}, u32[]{:S(2)}) copy-start(f32[2,5,1024,128]{3,2,1,0:T(8,128)} %get-tuple-element.75.own_ref) | copy-start | bytes 15728644
  198.0 10.7 %collective-permute-start.21 = (bf16[2,5,128,128]{3,2,1,0:T(8,128)(2,1)S(1)}, bf16[2,5,128,128]{3,2,1,0:T(8,128)(2,1)S(1)}, u32[]{:S(2)}, u32[]{:S(2)}) collective-permute-start(bf16[2,5,128,128]{3,2,1,0:T(8,128)(2,1)S(1)} %get-tuple-element.78), channel_id=1, source_target_pairs={{0,7},{1,0},{2,1},{3,2},{4,3},{5,4},{6,5},{7,6},{8,15},{9,8},{10,9... | collective-permute-start | bytes 983048 | tf_op jit(solution)/shard_map/ppermute | solution.py:357
  202.5 10.8 %collective-permute-start.22 = (bf16[2,5,128,128]{3,2,1,0:T(8,128)(2,1)S(1)}, bf16[2,5,128,128]{3,2,1,0:T(8,128)(2,1)S(1)}, u32[]{:S(2)}, u32[]{:S(2)}) collective-permute-start(bf16[2,5,128,128]{3,2,1,0:T(8,128)(2,1)S(1)} %get-tuple-element.79), channel_id=1, source_target_pairs={{0,6},{1,7},{2,0},{3,1},{4,2},{5,3},{6,4},{7,5},{8,14},{9,15},{10,... | collective-permute-start | bytes 983048 | tf_op jit(solution)/shard_map/ppermute | solution.py:357
  204.3 27.0 %collective-permute-start.23 = (bf16[2,5,128,128]{3,2,1,0:T(8,128)(2,1)S(1)}, bf16[2,5,128,128]{3,2,1,0:T(8,128)(2,1)S(1)}, u32[]{:S(2)}, u32[]{:S(2)}) collective-permute-start(bf16[2,5,128,128]{3,2,1,0:T(8,128)(2,1)S(1)} %get-tuple-element.80), channel_id=1, source_target_pairs={{0,5},{1,6},{2,7},{3,0},{4,1},{5,2},{6,3},{7,4},{8,13},{9,14},{10,... | collective-permute-start | bytes 983048 | tf_op jit(solution)/shard_map/ppermute | solution.py:357
  205.7 25.6 %collective-permute-start.24 = (bf16[2,5,128,128]{3,2,1,0:T(8,128)(2,1)S(1)}, bf16[2,5,128,128]{3,2,1,0:T(8,128)(2,1)S(1)}, u32[]{:S(2)}, u32[]{:S(2)}) collective-permute-start(bf16[2,5,128,128]{3,2,1,0:T(8,128)(2,1)S(1)} %get-tuple-element.81), channel_id=1, source_target_pairs={{0,4},{1,5},{2,6},{3,7},{4,0},{5,1},{6,2},{7,3},{8,12},{9,13},{10,... | collective-permute-start | bytes 983048 | tf_op jit(solution)/shard_map/ppermute | solution.py:357
  206.0 25.3 %collective-permute-start.25 = (bf16[2,5,128,128]{3,2,1,0:T(8,128)(2,1)S(1)}, bf16[2,5,128,128]{3,2,1,0:T(8,128)(2,1)S(1)}, u32[]{:S(2)}, u32[]{:S(2)}) collective-permute-start(bf16[2,5,128,128]{3,2,1,0:T(8,128)(2,1)S(1)} %get-tuple-element.82), channel_id=1, source_target_pairs={{0,3},{1,4},{2,5},{3,6},{4,7},{5,0},{6,1},{7,2},{8,11},{9,12},{10,... | collective-permute-start | bytes 983048 | tf_op jit(solution)/shard_map/ppermute | solution.py:357
  208.7 22.6 %collective-permute-start.26 = (bf16[2,5,128,128]{3,2,1,0:T(8,128)(2,1)S(1)}, bf16[2,5,128,128]{3,2,1,0:T(8,128)(2,1)S(1)}, u32[]{:S(2)}, u32[]{:S(2)}) collective-permute-start(bf16[2,5,128,128]{3,2,1,0:T(8,128)(2,1)S(1)} %get-tuple-element.83), channel_id=1, source_target_pairs={{0,2},{1,3},{2,4},{3,5},{4,6},{5,7},{6,0},{7,1},{8,10},{9,11},{10,... | collective-permute-start | bytes 983048 | tf_op jit(solution)/shard_map/ppermute | solution.py:357
  213.3 21.1 %collective-permute-start.27 = (bf16[2,5,128,128]{3,2,1,0:T(8,128)(2,1)S(1)}, bf16[2,5,128,128]{3,2,1,0:T(8,128)(2,1)S(1)}, u32[]{:S(2)}, u32[]{:S(2)}) collective-permute-start(bf16[2,5,128,128]{3,2,1,0:T(8,128)(2,1)S(1)} %get-tuple-element.84), channel_id=1, source_target_pairs={{0,1},{1,2},{2,3},{3,4},{4,5},{5,6},{6,7},{7,0},{8,9},{9,10},{10,1... | collective-permute-start | bytes 983048 | tf_op jit(solution)/shard_map/ppermute | solution.py:357

commit v4 on v3

--- a/solution.py
+++ b/solution.py
@@ -11,6 +11,7 @@
 HD = 128
 FBLK = 32
 LEAST_LIVE = 12
+ORDER = (1, 7, 2, 6, 3, 5, 4)
 SCALE = 1.0 / math.sqrt(HD)
 TO_EXP2 = SCALE * math.log2(math.e)
 VMEM_LIMIT = 40 * 2**20
@@ -289,71 +290,76 @@
 
 
 def cut_kernel(me_ref, a_ref, b_ref, *refs):
-    *out_refs, wide, sems = refs
+    *out_refs, sems = refs
     count = len(out_refs)
-    width = wide.shape[3]
     copies = []
-    for k in range(count):
-        columns = pl.ds(pl.multiple_of(lax.rem(me_ref[0] + k, count) * width, HD), width)
-        for i, ref in enumerate((a_ref, b_ref)):
-            copies.append(pltpu.make_async_copy(ref.at[:, columns], wide.at[k, i], sems.at[k, i]))
+    for k in (*ORDER, 0):
+        heads = out_refs[k].shape[1]
+        to = lax.rem(me_ref[0] + k, count)
+        for h in range(heads):
+            columns = pl.ds(pl.multiple_of((to * heads + h) * HD, HD), HD)
+            for i, ref in enumerate((a_ref, b_ref)):
+                copies.append(pltpu.make_async_copy(ref.at[:, columns], out_refs[k].at[i, h], sems.at[i, k, h]))
     for copy in copies:
         copy.start()
-    for k, out_ref in enumerate(out_refs):
-        for i in range(2):
-            copies[2 * k + i].wait()
-            for h in range(width // HD):
-                out_ref[i, h] = wide[k, i, :, h * HD : (h + 1) * HD]
+    for copy in copies:
+        copy.wait()
 
 
 def cut(me, a, b, count):
     tok, width = a.shape
-    width //= count
+    nh = width // count // HD
     return pl.pallas_call(
         cut_kernel,
-        out_shape=[jax.ShapeDtypeStruct((2, width // HD, tok, HD), BF16)] * count,
+        out_shape=[jax.ShapeDtypeStruct((2, nh, tok, HD), BF16)] * count,
         in_specs=[smem(), anywhere(), anywhere()],
         out_specs=[vmem()] * count,
-        scratch_shapes=[pltpu.VMEM((count, 2, tok, width), BF16), pltpu.SemaphoreType.DMA((count, 2))],
+        scratch_shapes=[pltpu.SemaphoreType.DMA((2, count, nh))],
         compiler_params=pltpu.CompilerParams(vmem_limit_bytes=MOST_VMEM),
         name="cut",
     )(me, a, b)
 
 
-def place_kernel(count, me_ref, *refs):
-    out_refs, sems = refs[count:-1], refs[-1]
+def place_kernel(ks, count, arrays, me_ref, *refs):
+    out_refs, sems = refs[-1 - arrays : -1], refs[-1]
     copies = []
-    for k, ref in enumerate(refs[:count]):
+    for n, (k, ref) in enumerate(zip(ks, refs)):
         heads = ref.shape[1]
         of = lax.rem(me_ref[0] + k, count)
         for h in range(heads):
             columns = pl.ds(pl.multiple_of((of * heads + h) * HD, HD), HD)
             for i, out_ref in enumerate(out_refs):
-                copies.append(pltpu.make_async_copy(ref.at[i, h], out_ref.at[:, columns], sems.at[i, k, h]))
+                copies.append(pltpu.make_async_copy(ref.at[i, h], out_ref.at[:, columns], sems.at[i, n, h]))
     for copy in copies:
         copy.start()
     for copy in copies:
         copy.wait()
 
 
-def place(me, pieces):
+def place_some(me, pieces, ks, before):
     arrays, nh, tok, _ = pieces[0].shape
     count = len(pieces)
     return pl.pallas_call(
-        functools.partial(place_kernel, count),
+        functools.partial(place_kernel, ks, count, arrays),
         out_shape=[pltpu.HBM((tok, nh * HD * count), BF16)] * arrays,
-        in_specs=[smem()] + [vmem()] * count,
+        in_specs=[smem()] + [vmem()] * len(ks) + [anywhere()] * len(before),
         out_specs=[anywhere()] * arrays,
-        scratch_shapes=[pltpu.SemaphoreType.DMA((arrays, count, nh))],
+        input_output_aliases={1 + len(ks) + i: i for i in range(len(before))},
+        scratch_shapes=[pltpu.SemaphoreType.DMA((arrays, len(ks), nh))],
         compiler_params=pltpu.CompilerParams(vmem_limit_bytes=SMALL_LIMIT),
         name="place",
-    )(me, *pieces)
+    )(me, *(pieces[k] for k in ks), *before)
+
+
+def place(me, pieces):
+    early = (0, *ORDER[:-2])
+    return place_some(me, pieces, ORDER[-2:], place_some(me, pieces, early, ()))
 
 
 def shift(parts, sign):
     n = len(parts)
     got = {0: parts[0]}
-    for k in (1, 7, 2, 6, 3, 5, 4):
+    for k in ORDER:
         got[k] = lax.ppermute(parts[k], "head", [(i, (i + sign * k) % n) for i in range(n)])
     return [got[k] for k in range(n)]
 

time: 239 us -> 236 us (0.987)
  starting transfers between devices: 69.4 us -> 58.1 us
  waiting for transfers between devices: 92.3 us -> 99.6 us
    ppermute x28, starting transfers between devices: 53.2 us -> 42.1 us  [shift(): lax.ppermute(parts[k], 'head', [(i, (i + sign * k) % n) for i in range(n)])]
    ppermute x28, waiting for transfers between devices: 67.4 us -> 74.9 us  [shift(): lax.ppermute(parts[k], 'head', [(i, (i + sign * k) % n) for i in range(n)])]
    pallas_call x4 -> x6, Pallas kernels: 10.4 us -> 12.6 us  [the longest x2 7.84 us: cut(): pl.pallas_call(cut_kernel, out_shape=[jax.ShapeDtypeStruct((2, nh, tok, H...]
  transfers between devices with their start and end apart: 30 -> 30, of which waited for: 16 -> 16; matrix products, arithmetic and copies ran while one was open for 3% -> 3% of each run, Pallas kernels for 15% -> 16%
where the time goes in v4:
time: 236 us; the launch traced here: 235 us
  waiting for transfers between devices  99.6 us (42%)
  Pallas kernels  59 us (25%)
  starting transfers between devices  58.1 us (25%)
  local copies, waits for them, and re-layouts  15.4 us (7%)
    ppermute x28, waiting for transfers between devices, shift(): lax.ppermute(parts[k], 'head', [(i, (i + sign * k) % n) for i in range(n)])  74.9 us
    ppermute x28, starting transfers between devices, shift(): lax.ppermute(parts[k], 'head', [(i, (i + sign * k) % n) for i in range(n)])  42.1 us
    pallas_call x1, Pallas kernels, own_grads(): pl.pallas_call(functools.partial(own_grads_kernel, kc), grid=(nh,), out_s...  22.4 us
    unnamed x36, local copies, waits for them, and re-layouts  14.6 us
    all_to_all x1, waiting for transfers between devices, body(): back = lax.all_to_all(ret, 'tok', split_axis=0, concat_axis=0, tiled=True)  12.7 us
    pallas_call x1, Pallas kernels, memory(): pl.pallas_call(functools.partial(memory_kernel, tq), grid=(nh,), out_shap...  12.5 us
    all_to_all x1, waiting for transfers between devices, body(): recv = lax.all_to_all(sent, 'tok', split_axis=0, concat_axis=0, tiled=True)  12 us
    all_to_all x1, starting transfers between devices, body(): recv = lax.all_to_all(sent, 'tok', split_axis=0, concat_axis=0, tiled=True)  9.46 us
  transfers between devices with their start and end apart: 30, of which 16 were waited for; matrix products, arithmetic and copies ran while one was open for 3% of the time, Pallas kernels for 16%

profile of v4, /device:TPU:1, one launch (start us, length us, event | category | flops | bytes accessed | tf_op | source)
XLA Modules:
  0.0 234.7 jit_solution(11070719023060024027)
XLA Ops:
  0.7 3.9 %cut.2 = (bf16[2,5,128,128]{3,2,1,0:T(8,128)(2,1)}, bf16[2,5,128,128]{3,2,1,0:T(8,128)(2,1)}, bf16[2,5,128,128]{3,2,1,0:T(8,128)(2,1)}, bf16[2,5,128,128]{3,2,1,...) custom-call(s32[1]{0:T(128)} %bitcast.me_ref, ...), custom_call_target="tpu_custom_call" | custom-call | tf_op jit(solution)/shard_map/cut/pallas_call | solution.py:312
  4.6 2.7 %collective-permute-start = (bf16[2,5,128,128]{3,2,1,0:T(8,128)(2,1)}, bf16[2,5,128,128]{3,2,1,0:T(8,128)(2,1)}, u32[]{:S(2)}, u32[]{:S(2)}) collective-permute-start(bf16[2,5,128,128]{3,2,1,0:T(8,128)(2,1)} %get-tuple-element.48), channel_id=1, source_target_pairs={{0,1},{1,2},{2,3},{3,4},{4,5},{5,6},{6,7},{7,0},{8,9},{9,10},{10,1... | collective-permute-start | bytes 983048 | tf_op jit(solution)/shard_map/ppermute | solution.py:363
  7.3 1.3 collective-permute-start.1
  8.6 1.7 collective-permute-start.2
  10.3 1.3 collective-permute-start.3
  11.6 2.6 %collective-permute-start.4 = (bf16[2,5,128,128]{3,2,1,0:T(8,128)(2,1)}, bf16[2,5,128,128]{3,2,1,0:T(8,128)(2,1)S(1)}, u32[]{:S(2)}, u32[]{:S(2)}) collective-permute-start(bf16[2,5,128,128]{3,2,1,0:T(8,128)(2,1)} %get-tuple-element.52), channel_id=1, source_target_pairs={{0,5},{1,6},{2,7},{3,0},{4,1},{5,2},{6,3},{7,4},{8,13},{9,14},{10,... | collective-permute-start | bytes 983048 | tf_op jit(solution)/shard_map/ppermute | solution.py:363
  15.4 2.2 collective-permute-start.5
  18.6 7.2 %collective-permute-done.1 = bf16[2,5,128,128]{3,2,1,0:T(8,128)(2,1)} collective-permute-done((bf16[2,5,128,128]{3,2,1,0:T(8,128)(2,1)}, bf16[2,5,128,128]{3,2,1,0:T(8,128)(2,1)}, u32[]{:S(2)}, u32[]{:S(2)}) %collective-permute-start.1) | collective-permute-done | bytes 327712 | tf_op jit(solution)/shard_map/ppermute | solution.py:363
  25.9 1.0 bitcast_dynamic-update-slice_fusion.13
  26.9 12.9 %collective-permute-done.2 = bf16[2,5,128,128]{3,2,1,0:T(8,128)(2,1)} collective-permute-done((bf16[2,5,128,128]{3,2,1,0:T(8,128)(2,1)}, bf16[2,5,128,128]{3,2,1,0:T(8,128)(2,1)}, u32[]{:S(2)}, u32[]{:S(2)}) %collective-permute-start.2) | collective-permute-done | bytes 327712 | tf_op jit(solution)/shard_map/ppermute | solution.py:363
  41.0 2.6 %pick.1 = bf16[32,2,5,32,128]{4,3,2,1,0:T(8,128)(2,1)} custom-call(s32[64]{0:T(128)S(1)} %pad_add_fusion.1.blocks_ref, bf16[2,8,5,128,128]{4,3,2,1,0:T(8,128)(2,1)S(1)} %bitcast_dynamic-update-slice_fusion.8.kv_ref), custom_call_target="tpu_custom_call" | custom-call | tf_op jit(solution)/shard_map/pick/pallas_call | solution.py:281
  43.6 9.5 %all-to-all-start = ((bf16[32,2,5,32,128]{4,3,2,1,0:T(8,128)(2,1)}), bf16[32,2,5,32,128]{4,3,2,1,0:T(8,128)(2,1)}, u32[]{:S(2)}, u32[]{:S(2)}) async-start(bf16[32,2,5,32,128]{4,3,2,1,0:T(8,128)(2,1)} %pick.1), calls=%async_computation | async-start | bytes 5242880 | tf_op jit(solution)/shard_map/all_to_all | solution.py:388
  53.9 3.9 %cut.3 = (bf16[2,5,128,128]{3,2,1,0:T(8,128)(2,1)}, bf16[2,5,128,128]{3,2,1,0:T(8,128)(2,1)}, bf16[2,5,128,128]{3,2,1,0:T(8,128)(2,1)}, bf16[2,5,128,128]{3,2,1,...) custom-call(s32[1]{0:T(128)} %bitcast.me_ref, ...), custom_call_target="tpu_custom_call" | custom-call | tf_op jit(solution)/shard_map/cut/pallas_call | solution.py:312
  57.8 1.2 pad_add_fusion.lists_ref
  59.1 2.1 collective-permute-start.8
  62.2 1.8 collective-permute-start.9
  64.0 1.7 collective-permute-start.10
  66.5 6.4 %collective-permute-done.8 = bf16[2,5,128,128]{3,2,1,0:T(8,128)(2,1)S(1)} collective-permute-done((bf16[2,5,128,128]{3,2,1,0:T(8,128)(2,1)}, bf16[2,5,128,128]{3,2,1,0:T(8,128)(2,1)S(1)}, u32[]{:S(2)}, u32[]{:S(2)}) %collective-permute-start.8) | collective-permute-done | bytes 327712 | tf_op jit(solution)/shard_map/ppermute | solution.py:363
  72.9 4.8 %collective-permute-done.9 = bf16[2,5,128,128]{3,2,1,0:T(8,128)(2,1)S(1)} collective-permute-done((bf16[2,5,128,128]{3,2,1,0:T(8,128)(2,1)}, bf16[2,5,128,128]{3,2,1,0:T(8,128)(2,1)S(1)}, u32[]{:S(2)}, u32[]{:S(2)}) %collective-permute-start.9) | collective-permute-done | bytes 327712 | tf_op jit(solution)/shard_map/ppermute | solution.py:363
  77.8 9.8 %collective-permute-done.10 = bf16[2,5,128,128]{3,2,1,0:T(8,128)(2,1)S(1)} collective-permute-done((bf16[2,5,128,128]{3,2,1,0:T(8,128)(2,1)}, bf16[2,5,128,128]{3,2,1,0:T(8,128)(2,1)S(1)}, u32[]{:S(2)}, u32[]{:S(2)}) %collective-permute-start.10) | collective-permute-done | bytes 327712 | tf_op jit(solution)/shard_map/ppermute | solution.py:363
  87.6 2.6 %collective-permute-done.11 = bf16[2,5,128,128]{3,2,1,0:T(8,128)(2,1)S(1)} collective-permute-done((bf16[2,5,128,128]{3,2,1,0:T(8,128)(2,1)}, bf16[2,5,128,128]{3,2,1,0:T(8,128)(2,1)S(1)}, u32[]{:S(2)}, u32[]{:S(2)}) %collective-permute-start.11) | collective-permute-done | bytes 327712 | tf_op jit(solution)/shard_map/ppermute | solution.py:363
  90.3 2.3 collective-permute-done.12
  92.6 1.1 collective-permute-done.13
  93.8 7.4 %own_stats.1.stat_ref = f32[5,8,1024]{2,1,0:T(8,128)S(1)} custom-call(bf16[2,8,5,128,128]{4,3,2,1,0:T(8,128)(2,1)S(1)} %bitcast_dynamic-update-slice_fusion.8.kv_ref, bf16[2,8,5,128,128]{4,3,2,1,0:T(8,128)(2,1)S(1)} %bitcast_dynamic-update-slice_fusion.qd_ref.q_ref.d_ref), custom_call_target="tpu_custom_call" | custom-call | flops 2684354560 | bytes 5242880 | tf_op jit(solution)/shard_map/own_stats/pallas_call | solution.py:103
  101.2 1.6 copy-done.4
  103.4 12.0 %all-to-all-done.recv_ref = bf16[32,2,5,32,128]{4,3,2,1,0:T(8,128)(2,1)} async-done(((bf16[32,2,5,32,128]{4,3,2,1,0:T(8,128)(2,1)}), bf16[32,2,5,32,128]{4,3,2,1,0:T(8,128)(2,1)}, u32[]{:S(2)}, u32[]{:S(2)}) %all-to-all-start) | async-done | bytes 2621472 | tf_op jit(solution)/shard_map/all_to_all | solution.py:388
  115.5 12.5 %memory.1 = (bf16[32,2,5,32,128]{4,3,2,1,0:T(8,128)(2,1)}, f32[5,8,1024]{2,1,0:T(8,128)}) custom-call(s32[17]{0:T(128)} %pad_add_fusion.lists_ref, f32[5,8,1024]{2,1,0:T(8,128)} %copy-done.8, bf16[32,2,5,32,128]{4,3,2,1,0:T(8,128)(2,1)} %all-to-all-done.recv_ref, bf16[2,8,5,128,128]{4,3,2,1,0:T(8,128)(2,1)} %copy-done.4, bf16[2,8,5,128,128]{4,3,2,1,0:T(8,128)(2,1)} %copy-done.4), custom_call_target="tpu_custom_call" | custom-call | flops 2684354560 | bytes 5242880 | tf_op jit(solution)/shard_map/memory/pallas_call | solution.py:166
  128.0 6.5 %all-to-all-start.1 = ((bf16[32,2,5,32,128]{4,3,2,1,0:T(8,128)(2,1)}), bf16[32,2,5,32,128]{4,3,2,1,0:T(8,128)(2,1)S(1)}, u32[]{:S(2)}, u32[]{:S(2)}) async-start(bf16[32,2,5,32,128]{4,3,2,1,0:T(8,128)(2,1)} %get-tuple-element.66), calls=%async_computation.1 | async-start | bytes 5242880 | tf_op jit(solution)/shard_map/all_to_all | solution.py:392
  134.5 1.7 copy-done.2
  136.2 1.7 copy-done.5
  138.0 22.4 %own_grads.1 = (bf16[1,5,128,128]{3,2,1,0:T(8,128)(2,1)}, bf16[1,5,128,128]{3,2,1,0:T(8,128)(2,1)}, bf16[1,5,128,128]{3,2,1,0:T(8,128)(2,1)}, bf16[1,5,128,128]{...) custom-call(s32[17]{0:T(128)S(1)} %copy-done.6, ...), custom_call_target="tpu_custom_call" | custom-call | flops 10066329600 | bytes 10485760 | tf_op jit(solution)/shard_map/own_grads/pallas_call | solution.py:218
  162.1 3.0 %collective-permute-start.18 = (bf16[1,5,128,128]{3,2,1,0:T(8,128)(2,1)}, bf16[1,5,128,128]{3,2,1,0:T(8,128)(2,1)S(1)}, u32[]{:S(2)}, u32[]{:S(2)}) collective-permute-start(bf16[1,5,128,128]{3,2,1,0:T(8,128)(2,1)} %get-tuple-element.73), channel_id=1, source_target_pairs={{0,6},{1,7},{2,0},{3,1},{4,2},{5,3},{6,4},{7,5},{8,14},{9,15},{10,... | collective-permute-start | bytes 491528 | tf_op jit(solution)/shard_map/ppermute | solution.py:363
  165.1 1.7 collective-permute-start.20
  166.8 1.6 collective-permute-start.14
  168.4 1.2 collective-permute-start.15
  169.6 7.6 %collective-permute-done.19.refs_4_ = bf16[1,5,128,128]{3,2,1,0:T(8,128)(2,1)S(1)} collective-permute-done((bf16[1,5,128,128]{3,2,1,0:T(8,128)(2,1)}, bf16[1,5,128,128]{3,2,1,0:T(8,128)(2,1)S(1)}, u32[]{:S(2)}, u32[]{:S(2)}) %collective-permute-start.19) | collective-permute-done | bytes 163872 | tf_op jit(solution)/shard_map/ppermute | solution.py:363
  178.5 1.2 place.4.refs_2_
  179.7 1.1 collective-permute-done.14.refs_0_
  181.7 12.7 %all-to-all-done.1.back_ref = bf16[32,2,5,32,128]{4,3,2,1,0:T(8,128)(2,1)S(1)} async-done(((bf16[32,2,5,32,128]{4,3,2,1,0:T(8,128)(2,1)}), bf16[32,2,5,32,128]{4,3,2,1,0:T(8,128)(2,1)S(1)}, u32[]{:S(2)}, u32[]{:S(2)}) %all-to-all-start.1) | async-done | bytes 2621472 | tf_op jit(solution)/shard_map/all_to_all | solution.py:392
  194.4 2.5 %copy-done = f32[2,5,1024,128]{3,2,1,0:T(8,128)S(1)} copy-done((f32[2,5,1024,128]{3,2,1,0:T(8,128)S(1)}, f32[2,5,1024,128]{3,2,1,0:T(8,128)}, u32[]{:S(2)}) %copy-start) | copy-done | bytes 5242904
  196.9 1.5 collect.1
  198.4 4.5 %collective-permute-start.23 = (bf16[2,5,128,128]{3,2,1,0:T(8,128)(2,1)S(1)}, bf16[2,5,128,128]{3,2,1,0:T(8,128)(2,1)S(1)}, u32[]{:S(2)}, u32[]{:S(2)}) collective-permute-start(bf16[2,5,128,128]{3,2,1,0:T(8,128)(2,1)S(1)} %get-tuple-element.82), channel_id=1, source_target_pairs={{0,7},{1,0},{2,1},{3,2},{4,3},{5,4},{6,5},{7,6},{8,15},{9,8},{10,9... | collective-permute-start | bytes 983048 | tf_op jit(solution)/shard_map/ppermute | solution.py:363
  202.9 2.6 %collective-permute-start.25 = (bf16[2,5,128,128]{3,2,1,0:T(8,128)(2,1)S(1)}, bf16[2,5,128,128]{3,2,1,0:T(8,128)(2,1)S(1)}, u32[]{:S(2)}, u32[]{:S(2)}) collective-permute-start(bf16[2,5,128,128]{3,2,1,0:T(8,128)(2,1)S(1)} %get-tuple-element.84), channel_id=1, source_target_pairs={{0,6},{1,7},{2,0},{3,1},{4,2},{5,3},{6,4},{7,5},{8,14},{9,15},{10,... | collective-permute-start | bytes 983048 | tf_op jit(solution)/shard_map/ppermute | solution.py:363
  205.5 2.8 %collective-permute-start.27 = (bf16[2,5,128,128]{3,2,1,0:T(8,128)(2,1)S(1)}, bf16[2,5,128,128]{3,2,1,0:T(8,128)(2,1)S(1)}, u32[]{:S(2)}, u32[]{:S(2)}) collective-permute-start(bf16[2,5,128,128]{3,2,1,0:T(8,128)(2,1)S(1)} %get-tuple-element.86), channel_id=1, source_target_pairs={{0,5},{1,6},{2,7},{3,0},{4,1},{5,2},{6,3},{7,4},{8,13},{9,14},{10,... | collective-permute-start | bytes 983048 | tf_op jit(solution)/shard_map/ppermute | solution.py:363
  208.3 4.0 %collective-permute-start.21 = (bf16[2,5,128,128]{3,2,1,0:T(8,128)(2,1)S(1)}, bf16[2,5,128,128]{3,2,1,0:T(8,128)(2,1)S(1)}, u32[]{:S(2)}, u32[]{:S(2)}) collective-permute-start(bf16[2,5,128,128]{3,2,1,0:T(8,128)(2,1)S(1)} %get-tuple-element.79), channel_id=1, source_target_pairs={{0,3},{1,4},{2,5},{3,6},{4,7},{5,0},{6,1},{7,2},{8,11},{9,12},{10,... | collective-permute-start | bytes 983048 | tf_op jit(solution)/shard_map/ppermute | solution.py:363
  213.2 5.4 %collective-permute-done.26.refs_4_ = bf16[2,5,128,128]{3,2,1,0:T(8,128)(2,1)S(1)} collective-permute-done((bf16[2,5,128,128]{3,2,1,0:T(8,128)(2,1)S(1)}, bf16[2,5,128,128]{3,2,1,0:T(8,128)(2,1)S(1)}, u32[]{:S(2)}, u32[]{:S(2)}) %collective-permute-start.26) | collective-permute-done | bytes 327712 | tf_op jit(solution)/shard_map/ppermute | solution.py:363
  218.6 13.1 %collective-permute-done.27.refs_5_ = bf16[2,5,128,128]{3,2,1,0:T(8,128)(2,1)S(1)} collective-permute-done((bf16[2,5,128,128]{3,2,1,0:T(8,128)(2,1)S(1)}, bf16[2,5,128,128]{3,2,1,0:T(8,128)(2,1)S(1)}, u32[]{:S(2)}, u32[]{:S(2)}) %collective-permute-start.27) | collective-permute-done | bytes 327712 | tf_op jit(solution)/shard_map/ppermute | solution.py:363
  231.7 1.8 place.6
  (70 shorter events, 12.8 us)
Async XLA Ops:
  0.6 14.6 %copy-start.10 = (s32[32]{0:T(128)S(1)}, s32[32]{0:T(128)}, u32[]{:S(2)}) copy-start(s32[32]{0:T(128)} %param.11) | copy-start | bytes 388
  0.6 14.6 %copy-start.9 = (s32[32,16]{0,1:T(8,128)S(1)}, s32[32,16]{0,1:T(8,128)}, u32[]{:S(2)}) copy-start(s32[32,16]{0,1:T(8,128)} %param.10) | copy-start | bytes 6148
  4.6 10.8 %collective-permute-start = (bf16[2,5,128,128]{3,2,1,0:T(8,128)(2,1)}, bf16[2,5,128,128]{3,2,1,0:T(8,128)(2,1)}, u32[]{:S(2)}, u32[]{:S(2)}) collective-permute-start(bf16[2,5,128,128]{3,2,1,0:T(8,128)(2,1)} %get-tuple-element.48), channel_id=1, source_target_pairs={{0,1},{1,2},{2,3},{3,4},{4,5},{5,6},{6,7},{7,0},{8,9},{9,10},{10,1... | collective-permute-start | bytes 983048 | tf_op jit(solution)/shard_map/ppermute | solution.py:363
  7.3 18.6 %collective-permute-start.1 = (bf16[2,5,128,128]{3,2,1,0:T(8,128)(2,1)}, bf16[2,5,128,128]{3,2,1,0:T(8,128)(2,1)}, u32[]{:S(2)}, u32[]{:S(2)}) collective-permute-start(bf16[2,5,128,128]{3,2,1,0:T(8,128)(2,1)} %get-tuple-element.49), channel_id=1, source_target_pairs={{0,2},{1,3},{2,4},{3,5},{4,6},{5,7},{6,0},{7,1},{8,10},{9,11},{10,... | collective-permute-start | bytes 983048 | tf_op jit(solution)/shard_map/ppermute | solution.py:363
  8.6 31.2 %collective-permute-start.2 = (bf16[2,5,128,128]{3,2,1,0:T(8,128)(2,1)}, bf16[2,5,128,128]{3,2,1,0:T(8,128)(2,1)}, u32[]{:S(2)}, u32[]{:S(2)}) collective-permute-start(bf16[2,5,128,128]{3,2,1,0:T(8,128)(2,1)} %get-tuple-element.50), channel_id=1, source_target_pairs={{0,3},{1,4},{2,5},{3,6},{4,7},{5,0},{6,1},{7,2},{8,11},{9,12},{10,... | collective-permute-start | bytes 983048 | tf_op jit(solution)/shard_map/ppermute | solution.py:363
  10.3 30.5 %collective-permute-start.3 = (bf16[2,5,128,128]{3,2,1,0:T(8,128)(2,1)}, bf16[2,5,128,128]{3,2,1,0:T(8,128)(2,1)S(1)}, u32[]{:S(2)}, u32[]{:S(2)}) collective-permute-start(bf16[2,5,128,128]{3,2,1,0:T(8,128)(2,1)} %get-tuple-element.51), channel_id=1, source_target_pairs={{0,4},{1,5},{2,6},{3,7},{4,0},{5,1},{6,2},{7,3},{8,12},{9,13},{10,... | collective-permute-start | bytes 983048 | tf_op jit(solution)/shard_map/ppermute | solution.py:363
  11.6 29.3 %collective-permute-start.4 = (bf16[2,5,128,128]{3,2,1,0:T(8,128)(2,1)}, bf16[2,5,128,128]{3,2,1,0:T(8,128)(2,1)S(1)}, u32[]{:S(2)}, u32[]{:S(2)}) collective-permute-start(bf16[2,5,128,128]{3,2,1,0:T(8,128)(2,1)} %get-tuple-element.52), channel_id=1, source_target_pairs={{0,5},{1,6},{2,7},{3,0},{4,1},{5,2},{6,3},{7,4},{8,13},{9,14},{10,... | collective-permute-start | bytes 983048 | tf_op jit(solution)/shard_map/ppermute | solution.py:363
  15.4 25.5 %collective-permute-start.5 = (bf16[2,5,128,128]{3,2,1,0:T(8,128)(2,1)}, bf16[2,5,128,128]{3,2,1,0:T(8,128)(2,1)S(1)}, u32[]{:S(2)}, u32[]{:S(2)}) collective-permute-start(bf16[2,5,128,128]{3,2,1,0:T(8,128)(2,1)} %get-tuple-element.53), channel_id=1, source_target_pairs={{0,6},{1,7},{2,0},{3,1},{4,2},{5,3},{6,4},{7,5},{8,14},{9,15},{10,... | collective-permute-start | bytes 983048 | tf_op jit(solution)/shard_map/ppermute | solution.py:363
  25.9 15.1 %collective-permute-start.6 = (bf16[2,5,128,128]{3,2,1,0:T(8,128)(2,1)}, bf16[2,5,128,128]{3,2,1,0:T(8,128)(2,1)S(1)}, u32[]{:S(2)}, u32[]{:S(2)}) collective-permute-start(bf16[2,5,128,128]{3,2,1,0:T(8,128)(2,1)} %get-tuple-element.54), channel_id=1, source_target_pairs={{0,7},{1,0},{2,1},{3,2},{4,3},{5,4},{6,5},{7,6},{8,15},{9,8},{10,9... | collective-permute-start | bytes 983048 | tf_op jit(solution)/shard_map/ppermute | solution.py:363
  41.0 52.8 %copy-start.1 = (bf16[2,8,5,128,128]{4,3,2,1,0:T(8,128)(2,1)}, bf16[2,8,5,128,128]{4,3,2,1,0:T(8,128)(2,1)S(1)}, u32[]{:S(2)}) copy-start(bf16[2,8,5,128,128]{4,3,2,1,0:T(8,128)(2,1)S(1)} %bitcast_dynamic-update-slice_fusion.8.kv_ref) | copy-start | bytes 7864324
  43.6 71.9 %all-to-all-start = ((bf16[32,2,5,32,128]{4,3,2,1,0:T(8,128)(2,1)}), bf16[32,2,5,32,128]{4,3,2,1,0:T(8,128)(2,1)}, u32[]{:S(2)}, u32[]{:S(2)}) async-start(bf16[32,2,5,32,128]{4,3,2,1,0:T(8,128)(2,1)} %pick.1), calls=%async_computation | async-start | bytes 5242880 | tf_op jit(solution)/shard_map/all_to_all | solution.py:388
  57.8 8.3 %collective-permute-start.7 = (bf16[2,5,128,128]{3,2,1,0:T(8,128)(2,1)}, bf16[2,5,128,128]{3,2,1,0:T(8,128)(2,1)S(1)}, u32[]{:S(2)}, u32[]{:S(2)}) collective-permute-start(bf16[2,5,128,128]{3,2,1,0:T(8,128)(2,1)} %get-tuple-element.58), channel_id=1, source_target_pairs={{0,1},{1,2},{2,3},{3,4},{4,5},{5,6},{6,7},{7,0},{8,9},{9,10},{10,1... | collective-permute-start | bytes 983048 | tf_op jit(solution)/shard_map/ppermute | solution.py:363
  59.1 13.8 %collective-permute-start.8 = (bf16[2,5,128,128]{3,2,1,0:T(8,128)(2,1)}, bf16[2,5,128,128]{3,2,1,0:T(8,128)(2,1)S(1)}, u32[]{:S(2)}, u32[]{:S(2)}) collective-permute-start(bf16[2,5,128,128]{3,2,1,0:T(8,128)(2,1)} %get-tuple-element.59), channel_id=1, source_target_pairs={{0,2},{1,3},{2,4},{3,5},{4,6},{5,7},{6,0},{7,1},{8,10},{9,11},{10,... | collective-permute-start | bytes 983048 | tf_op jit(solution)/shard_map/ppermute | solution.py:363
  62.2 15.6 %collective-permute-start.9 = (bf16[2,5,128,128]{3,2,1,0:T(8,128)(2,1)}, bf16[2,5,128,128]{3,2,1,0:T(8,128)(2,1)S(1)}, u32[]{:S(2)}, u32[]{:S(2)}) collective-permute-start(bf16[2,5,128,128]{3,2,1,0:T(8,128)(2,1)} %get-tuple-element.60), channel_id=1, source_target_pairs={{0,3},{1,4},{2,5},{3,6},{4,7},{5,0},{6,1},{7,2},{8,11},{9,12},{10,... | collective-permute-start | bytes 983048 | tf_op jit(solution)/shard_map/ppermute | solution.py:363
  64.0 23.6 %collective-permute-start.10 = (bf16[2,5,128,128]{3,2,1,0:T(8,128)(2,1)}, bf16[2,5,128,128]{3,2,1,0:T(8,128)(2,1)S(1)}, u32[]{:S(2)}, u32[]{:S(2)}) collective-permute-start(bf16[2,5,128,128]{3,2,1,0:T(8,128)(2,1)} %get-tuple-element.61), channel_id=1, source_target_pairs={{0,4},{1,5},{2,6},{3,7},{4,0},{5,1},{6,2},{7,3},{8,12},{9,13},{10,... | collective-permute-start | bytes 983048 | tf_op jit(solution)/shard_map/ppermute | solution.py:363
  65.7 24.6 %collective-permute-start.11 = (bf16[2,5,128,128]{3,2,1,0:T(8,128)(2,1)}, bf16[2,5,128,128]{3,2,1,0:T(8,128)(2,1)S(1)}, u32[]{:S(2)}, u32[]{:S(2)}) collective-permute-start(bf16[2,5,128,128]{3,2,1,0:T(8,128)(2,1)} %get-tuple-element.62), channel_id=1, source_target_pairs={{0,5},{1,6},{2,7},{3,0},{4,1},{5,2},{6,3},{7,4},{8,13},{9,14},{10,... | collective-permute-start | bytes 983048 | tf_op jit(solution)/shard_map/ppermute | solution.py:363
  66.1 26.4 %collective-permute-start.12 = (bf16[2,5,128,128]{3,2,1,0:T(8,128)(2,1)}, bf16[2,5,128,128]{3,2,1,0:T(8,128)(2,1)S(1)}, u32[]{:S(2)}, u32[]{:S(2)}) collective-permute-start(bf16[2,5,128,128]{3,2,1,0:T(8,128)(2,1)} %get-tuple-element.63), channel_id=1, source_target_pairs={{0,6},{1,7},{2,0},{3,1},{4,2},{5,3},{6,4},{7,5},{8,14},{9,15},{10,... | collective-permute-start | bytes 983048 | tf_op jit(solution)/shard_map/ppermute | solution.py:363
  72.9 20.9 %collective-permute-start.13 = (bf16[2,5,128,128]{3,2,1,0:T(8,128)(2,1)}, bf16[2,5,128,128]{3,2,1,0:T(8,128)(2,1)S(1)}, u32[]{:S(2)}, u32[]{:S(2)}) collective-permute-start(bf16[2,5,128,128]{3,2,1,0:T(8,128)(2,1)} %get-tuple-element.64), channel_id=1, source_target_pairs={{0,7},{1,0},{2,1},{3,2},{4,3},{5,4},{6,5},{7,6},{8,15},{9,8},{10,9... | collective-permute-start | bytes 983048 | tf_op jit(solution)/shard_map/ppermute | solution.py:363
  101.2 1.6 copy-start.4
  102.8 0.7 copy-start.8
  127.9 6.5 %copy-start.6 = (s32[17]{0:T(128)S(1)}, s32[17]{0:T(128)}, u32[]{:S(2)}) copy-start(s32[17]{0:T(128)} %pad_add_fusion.lists_ref) | copy-start | bytes 208
  127.9 6.6 %copy-start.7 = (f32[5,8,1024]{2,1,0:T(8,128)S(1)}, f32[5,8,1024]{2,1,0:T(8,128)}, u32[]{:S(2)}) copy-start(f32[5,8,1024]{2,1,0:T(8,128)} %get-tuple-element.67.fin_ref) | copy-start | bytes 491524
  128.0 66.4 %all-to-all-start.1 = ((bf16[32,2,5,32,128]{4,3,2,1,0:T(8,128)(2,1)}), bf16[32,2,5,32,128]{4,3,2,1,0:T(8,128)(2,1)S(1)}, u32[]{:S(2)}, u32[]{:S(2)}) async-start(bf16[32,2,5,32,128]{4,3,2,1,0:T(8,128)(2,1)} %get-tuple-element.66), calls=%async_computation.1 | async-start | bytes 5242880 | tf_op jit(solution)/shard_map/all_to_all | solution.py:392
  134.5 1.7 copy-start.2
  136.2 1.7 copy-start.5
  160.4 6.4 %collective-permute-start.16 = (bf16[1,5,128,128]{3,2,1,0:T(8,128)(2,1)}, bf16[1,5,128,128]{3,2,1,0:T(8,128)(2,1)S(1)}, u32[]{:S(2)}, u32[]{:S(2)}) collective-permute-start(bf16[1,5,128,128]{3,2,1,0:T(8,128)(2,1)} %get-tuple-element.71), channel_id=1, source_target_pairs={{0,7},{1,0},{2,1},{3,2},{4,3},{5,4},{6,5},{7,6},{8,15},{9,8},{10,9... | collective-permute-start | bytes 491528 | tf_op jit(solution)/shard_map/ppermute | solution.py:363
  161.1 7.2 %collective-permute-start.17 = (bf16[1,5,128,128]{3,2,1,0:T(8,128)(2,1)}, bf16[1,5,128,128]{3,2,1,0:T(8,128)(2,1)S(1)}, u32[]{:S(2)}, u32[]{:S(2)}) collective-permute-start(bf16[1,5,128,128]{3,2,1,0:T(8,128)(2,1)} %get-tuple-element.72), channel_id=1, source_target_pairs={{0,1},{1,2},{2,3},{3,4},{4,5},{5,6},{6,7},{7,0},{8,9},{9,10},{10,1... | collective-permute-start | bytes 491528 | tf_op jit(solution)/shard_map/ppermute | solution.py:363
  162.1 7.4 %collective-permute-start.18 = (bf16[1,5,128,128]{3,2,1,0:T(8,128)(2,1)}, bf16[1,5,128,128]{3,2,1,0:T(8,128)(2,1)S(1)}, u32[]{:S(2)}, u32[]{:S(2)}) collective-permute-start(bf16[1,5,128,128]{3,2,1,0:T(8,128)(2,1)} %get-tuple-element.73), channel_id=1, source_target_pairs={{0,6},{1,7},{2,0},{3,1},{4,2},{5,3},{6,4},{7,5},{8,14},{9,15},{10,... | collective-permute-start | bytes 491528 | tf_op jit(solution)/shard_map/ppermute | solution.py:363
  165.1 12.0 %collective-permute-start.19 = (bf16[1,5,128,128]{3,2,1,0:T(8,128)(2,1)}, bf16[1,5,128,128]{3,2,1,0:T(8,128)(2,1)S(1)}, u32[]{:S(2)}, u32[]{:S(2)}) collective-permute-start(bf16[1,5,128,128]{3,2,1,0:T(8,128)(2,1)} %get-tuple-element.74), channel_id=1, source_target_pairs={{0,2},{1,3},{2,4},{3,5},{4,6},{5,7},{6,0},{7,1},{8,10},{9,11},{10,... | collective-permute-start | bytes 491528 | tf_op jit(solution)/shard_map/ppermute | solution.py:363
  165.1 12.5 %collective-permute-start.20 = (bf16[1,5,128,128]{3,2,1,0:T(8,128)(2,1)}, bf16[1,5,128,128]{3,2,1,0:T(8,128)(2,1)S(1)}, u32[]{:S(2)}, u32[]{:S(2)}) collective-permute-start(bf16[1,5,128,128]{3,2,1,0:T(8,128)(2,1)} %get-tuple-element.75), channel_id=1, source_target_pairs={{0,5},{1,6},{2,7},{3,0},{4,1},{5,2},{6,3},{7,4},{8,13},{9,14},{10,... | collective-permute-start | bytes 491528 | tf_op jit(solution)/shard_map/ppermute | solution.py:363
  166.8 14.0 %collective-permute-start.14 = (bf16[1,5,128,128]{3,2,1,0:T(8,128)(2,1)}, bf16[1,5,128,128]{3,2,1,0:T(8,128)(2,1)S(1)}, u32[]{:S(2)}, u32[]{:S(2)}) collective-permute-start(bf16[1,5,128,128]{3,2,1,0:T(8,128)(2,1)} %get-tuple-element.68), channel_id=1, source_target_pairs={{0,3},{1,4},{2,5},{3,6},{4,7},{5,0},{6,1},{7,2},{8,11},{9,12},{10,... | collective-permute-start | bytes 491528 | tf_op jit(solution)/shard_map/ppermute | solution.py:363
  168.4 12.5 %collective-permute-start.15 = (bf16[1,5,128,128]{3,2,1,0:T(8,128)(2,1)}, bf16[1,5,128,128]{3,2,1,0:T(8,128)(2,1)S(1)}, u32[]{:S(2)}, u32[]{:S(2)}) collective-permute-start(bf16[1,5,128,128]{3,2,1,0:T(8,128)(2,1)} %get-tuple-element.69), channel_id=1, source_target_pairs={{0,4},{1,5},{2,6},{3,7},{4,0},{5,1},{6,2},{7,3},{8,12},{9,13},{10,... | collective-permute-start | bytes 491528 | tf_op jit(solution)/shard_map/ppermute | solution.py:363
  177.6 0.9 copy-start.3
  194.4 2.5 %copy-start = (f32[2,5,1024,128]{3,2,1,0:T(8,128)S(1)}, f32[2,5,1024,128]{3,2,1,0:T(8,128)}, u32[]{:S(2)}) copy-start(f32[2,5,1024,128]{3,2,1,0:T(8,128)} %get-tuple-element.77.own_ref) | copy-start | bytes 15728644
  198.4 9.9 %collective-permute-start.23 = (bf16[2,5,128,128]{3,2,1,0:T(8,128)(2,1)S(1)}, bf16[2,5,128,128]{3,2,1,0:T(8,128)(2,1)S(1)}, u32[]{:S(2)}, u32[]{:S(2)}) collective-permute-start(bf16[2,5,128,128]{3,2,1,0:T(8,128)(2,1)S(1)} %get-tuple-element.82), channel_id=1, source_target_pairs={{0,7},{1,0},{2,1},{3,2},{4,3},{5,4},{6,5},{7,6},{8,15},{9,8},{10,9... | collective-permute-start | bytes 983048 | tf_op jit(solution)/shard_map/ppermute | solution.py:363
  202.9 9.4 %collective-permute-start.24 = (bf16[2,5,128,128]{3,2,1,0:T(8,128)(2,1)S(1)}, bf16[2,5,128,128]{3,2,1,0:T(8,128)(2,1)S(1)}, u32[]{:S(2)}, u32[]{:S(2)}) collective-permute-start(bf16[2,5,128,128]{3,2,1,0:T(8,128)(2,1)S(1)} %get-tuple-element.83), channel_id=1, source_target_pairs={{0,1},{1,2},{2,3},{3,4},{4,5},{5,6},{6,7},{7,0},{8,9},{9,10},{10,1... | collective-permute-start | bytes 983048 | tf_op jit(solution)/shard_map/ppermute | solution.py:363
  202.9 10.2 %collective-permute-start.25 = (bf16[2,5,128,128]{3,2,1,0:T(8,128)(2,1)S(1)}, bf16[2,5,128,128]{3,2,1,0:T(8,128)(2,1)S(1)}, u32[]{:S(2)}, u32[]{:S(2)}) collective-permute-start(bf16[2,5,128,128]{3,2,1,0:T(8,128)(2,1)S(1)} %get-tuple-element.84), channel_id=1, source_target_pairs={{0,6},{1,7},{2,0},{3,1},{4,2},{5,3},{6,4},{7,5},{8,14},{9,15},{10,... | collective-permute-start | bytes 983048 | tf_op jit(solution)/shard_map/ppermute | solution.py:363
  205.5 13.1 %collective-permute-start.26 = (bf16[2,5,128,128]{3,2,1,0:T(8,128)(2,1)S(1)}, bf16[2,5,128,128]{3,2,1,0:T(8,128)(2,1)S(1)}, u32[]{:S(2)}, u32[]{:S(2)}) collective-permute-start(bf16[2,5,128,128]{3,2,1,0:T(8,128)(2,1)S(1)} %get-tuple-element.85), channel_id=1, source_target_pairs={{0,2},{1,3},{2,4},{3,5},{4,6},{5,7},{6,0},{7,1},{8,10},{9,11},{10,... | collective-permute-start | bytes 983048 | tf_op jit(solution)/shard_map/ppermute | solution.py:363
  205.5 26.2 %collective-permute-start.27 = (bf16[2,5,128,128]{3,2,1,0:T(8,128)(2,1)S(1)}, bf16[2,5,128,128]{3,2,1,0:T(8,128)(2,1)S(1)}, u32[]{:S(2)}, u32[]{:S(2)}) collective-permute-start(bf16[2,5,128,128]{3,2,1,0:T(8,128)(2,1)S(1)} %get-tuple-element.86), channel_id=1, source_target_pairs={{0,5},{1,6},{2,7},{3,0},{4,1},{5,2},{6,3},{7,4},{8,13},{9,14},{10,... | collective-permute-start | bytes 983048 | tf_op jit(solution)/shard_map/ppermute | solution.py:363
  208.3 25.2 %collective-permute-start.21 = (bf16[2,5,128,128]{3,2,1,0:T(8,128)(2,1)S(1)}, bf16[2,5,128,128]{3,2,1,0:T(8,128)(2,1)S(1)}, u32[]{:S(2)}, u32[]{:S(2)}) collective-permute-start(bf16[2,5,128,128]{3,2,1,0:T(8,128)(2,1)S(1)} %get-tuple-element.79), channel_id=1, source_target_pairs={{0,3},{1,4},{2,5},{3,6},{4,7},{5,0},{6,1},{7,2},{8,11},{9,12},{10,... | collective-permute-start | bytes 983048 | tf_op jit(solution)/shard_map/ppermute | solution.py:363
  212.3 21.2 %collective-permute-start.22 = (bf16[2,5,128,128]{3,2,1,0:T(8,128)(2,1)S(1)}, bf16[2,5,128,128]{3,2,1,0:T(8,128)(2,1)S(1)}, u32[]{:S(2)}, u32[]{:S(2)}) collective-permute-start(bf16[2,5,128,128]{3,2,1,0:T(8,128)(2,1)S(1)} %get-tuple-element.80), channel_id=1, source_target_pairs={{0,4},{1,5},{2,6},{3,7},{4,0},{5,1},{6,2},{7,3},{8,12},{9,13},{10,... | collective-permute-start | bytes 983048 | tf_op jit(solution)/shard_map/ppermute | solution.py:363

commit v5 on v4

--- a/solution.py
+++ b/solution.py
@@ -202,8 +202,8 @@
         k, v = rows_of(kv_ref, 0, c, kc), rows_of(kv_ref, 1, c, kc)
         p, ds = probabilities(k, v)
         dq = dq + dot(ds, k, TN)
-        own_ref[0, c : c + kc] = dot(ds, q, NN) * SCALE
-        own_ref[1, c : c + kc] = dot(p.astype(BF16), d, NN)
+        own_ref[0, c : c + kc] = (dot(ds, q, NN) * SCALE).astype(BF16)
+        own_ref[1, c : c + kc] = dot(p.astype(BF16), d, NN).astype(BF16)
     dq = (dq * SCALE).astype(BF16)
     for i, ref in enumerate(dq_refs):
         ref[0] = dq[i * tok : (i + 1) * tok]
@@ -218,7 +218,7 @@
     *dq, grads = pl.pallas_call(
         functools.partial(own_grads_kernel, kc),
         grid=(nh,),
-        out_shape=[pltpu.HBM(piece, BF16)] * pieces + [pltpu.HBM(whole, F32)],
+        out_shape=[pltpu.HBM(piece, BF16)] * pieces + [pltpu.HBM(whole, BF16)],
         in_specs=[smem(), stat_block(own), per_head(recv.shape), per_head(kv.shape), per_head(qd.shape)],
         out_specs=[per_head(piece)] * pieces + [per_head(whole)],
         scratch_shapes=[pltpu.VMEM((mem, HD), BF16)] * 2,
@@ -235,7 +235,7 @@
     *out_refs, acc = refs
     slots = back_ref.shape[0]
     tok = acc.shape[2] // len(out_refs)
-    acc[...] = own_ref[...]
+    acc[...] = own_ref[...].astype(F32)
     for s in range(slots):
 
         @pl.when(blocks_ref[slots + s] != 0)

time: 236 us -> 235 us (level)
  no operation moved by 1% of the time
where the time goes in v5:
time: 235 us; the launch traced here: 234 us
  waiting for transfers between devices  99.6 us (42%)
  Pallas kernels  58.9 us (25%)
  starting transfers between devices  58.1 us (25%)
  local copies, waits for them, and re-layouts  14.8 us (6%)
    ppermute x28, waiting for transfers between devices, shift(): lax.ppermute(parts[k], 'head', [(i, (i + sign * k) % n) for i in range(n)])  74.9 us
    ppermute x28, starting transfers between devices, shift(): lax.ppermute(parts[k], 'head', [(i, (i + sign * k) % n) for i in range(n)])  42.1 us
    pallas_call x1, Pallas kernels, own_grads(): pl.pallas_call(functools.partial(own_grads_kernel, kc), grid=(nh,), out_s...  22.2 us
    unnamed x36, local copies, waits for them, and re-layouts  13.8 us
    all_to_all x1, waiting for transfers between devices, body(): back = lax.all_to_all(ret, 'tok', split_axis=0, concat_axis=0, tiled=True)  12.9 us
    pallas_call x1, Pallas kernels, memory(): pl.pallas_call(functools.partial(memory_kernel, tq), grid=(nh,), out_shap...  12.6 us
    all_to_all x1, waiting for transfers between devices, body(): recv = lax.all_to_all(sent, 'tok', split_axis=0, concat_axis=0, tiled=True)  11.9 us
    all_to_all x1, starting transfers between devices, body(): recv = lax.all_to_all(sent, 'tok', split_axis=0, concat_axis=0, tiled=True)  9.46 us
  transfers between devices with their start and end apart: 30, of which 16 were waited for; matrix products, arithmetic and copies ran while one was open for 3% of the time, Pallas kernels for 16%

profile of v5, /device:TPU:1, one launch (start us, length us, event | category | flops | bytes accessed | tf_op | source)
XLA Modules:
  0.0 234.0 jit_solution(637105700708304089)
XLA Ops:
  0.7 3.9 %cut.2 = (bf16[2,5,128,128]{3,2,1,0:T(8,128)(2,1)}, bf16[2,5,128,128]{3,2,1,0:T(8,128)(2,1)}, bf16[2,5,128,128]{3,2,1,0:T(8,128)(2,1)}, bf16[2,5,128,128]{3,2,1,...) custom-call(s32[1]{0:T(128)} %bitcast.me_ref, ...), custom_call_target="tpu_custom_call" | custom-call | tf_op jit(solution)/shard_map/cut/pallas_call | solution.py:312
  4.6 2.7 %collective-permute-start = (bf16[2,5,128,128]{3,2,1,0:T(8,128)(2,1)}, bf16[2,5,128,128]{3,2,1,0:T(8,128)(2,1)}, u32[]{:S(2)}, u32[]{:S(2)}) collective-permute-start(bf16[2,5,128,128]{3,2,1,0:T(8,128)(2,1)} %get-tuple-element.48), channel_id=1, source_target_pairs={{0,1},{1,2},{2,3},{3,4},{4,5},{5,6},{6,7},{7,0},{8,9},{9,10},{10,1... | collective-permute-start | bytes 983048 | tf_op jit(solution)/shard_map/ppermute | solution.py:363
  7.3 1.3 collective-permute-start.1
  8.6 1.7 collective-permute-start.2
  10.3 1.3 collective-permute-start.3
  11.6 2.6 %collective-permute-start.4 = (bf16[2,5,128,128]{3,2,1,0:T(8,128)(2,1)}, bf16[2,5,128,128]{3,2,1,0:T(8,128)(2,1)S(1)}, u32[]{:S(2)}, u32[]{:S(2)}) collective-permute-start(bf16[2,5,128,128]{3,2,1,0:T(8,128)(2,1)} %get-tuple-element.52), channel_id=1, source_target_pairs={{0,5},{1,6},{2,7},{3,0},{4,1},{5,2},{6,3},{7,4},{8,13},{9,14},{10,... | collective-permute-start | bytes 983048 | tf_op jit(solution)/shard_map/ppermute | solution.py:363
  15.4 2.2 collective-permute-start.5
  18.7 7.2 %collective-permute-done.1 = bf16[2,5,128,128]{3,2,1,0:T(8,128)(2,1)} collective-permute-done((bf16[2,5,128,128]{3,2,1,0:T(8,128)(2,1)}, bf16[2,5,128,128]{3,2,1,0:T(8,128)(2,1)}, u32[]{:S(2)}, u32[]{:S(2)}) %collective-permute-start.1) | collective-permute-done | bytes 327712 | tf_op jit(solution)/shard_map/ppermute | solution.py:363
  25.9 1.0 bitcast_dynamic-update-slice_fusion.13
  26.9 12.9 %collective-permute-done.2 = bf16[2,5,128,128]{3,2,1,0:T(8,128)(2,1)} collective-permute-done((bf16[2,5,128,128]{3,2,1,0:T(8,128)(2,1)}, bf16[2,5,128,128]{3,2,1,0:T(8,128)(2,1)}, u32[]{:S(2)}, u32[]{:S(2)}) %collective-permute-start.2) | collective-permute-done | bytes 327712 | tf_op jit(solution)/shard_map/ppermute | solution.py:363
  41.0 2.6 %pick.1 = bf16[32,2,5,32,128]{4,3,2,1,0:T(8,128)(2,1)} custom-call(s32[64]{0:T(128)S(1)} %pad_add_fusion.1.blocks_ref, bf16[2,8,5,128,128]{4,3,2,1,0:T(8,128)(2,1)S(1)} %bitcast_dynamic-update-slice_fusion.8.kv_ref), custom_call_target="tpu_custom_call" | custom-call | tf_op jit(solution)/shard_map/pick/pallas_call | solution.py:281
  43.6 9.5 %all-to-all-start = ((bf16[32,2,5,32,128]{4,3,2,1,0:T(8,128)(2,1)}), bf16[32,2,5,32,128]{4,3,2,1,0:T(8,128)(2,1)}, u32[]{:S(2)}, u32[]{:S(2)}) async-start(bf16[32,2,5,32,128]{4,3,2,1,0:T(8,128)(2,1)} %pick.1), calls=%async_computation | async-start | bytes 5242880 | tf_op jit(solution)/shard_map/all_to_all | solution.py:388
  53.9 3.9 %cut.3 = (bf16[2,5,128,128]{3,2,1,0:T(8,128)(2,1)}, bf16[2,5,128,128]{3,2,1,0:T(8,128)(2,1)}, bf16[2,5,128,128]{3,2,1,0:T(8,128)(2,1)}, bf16[2,5,128,128]{3,2,1,...) custom-call(s32[1]{0:T(128)} %bitcast.me_ref, ...), custom_call_target="tpu_custom_call" | custom-call | tf_op jit(solution)/shard_map/cut/pallas_call | solution.py:312
  57.9 1.3 pad_add_fusion.lists_ref
  59.2 2.1 collective-permute-start.8
  62.3 1.8 collective-permute-start.9
  64.1 1.7 collective-permute-start.10
  66.6 6.3 %collective-permute-done.8 = bf16[2,5,128,128]{3,2,1,0:T(8,128)(2,1)S(1)} collective-permute-done((bf16[2,5,128,128]{3,2,1,0:T(8,128)(2,1)}, bf16[2,5,128,128]{3,2,1,0:T(8,128)(2,1)S(1)}, u32[]{:S(2)}, u32[]{:S(2)}) %collective-permute-start.8) | collective-permute-done | bytes 327712 | tf_op jit(solution)/shard_map/ppermute | solution.py:363
  73.0 4.9 %collective-permute-done.9 = bf16[2,5,128,128]{3,2,1,0:T(8,128)(2,1)S(1)} collective-permute-done((bf16[2,5,128,128]{3,2,1,0:T(8,128)(2,1)}, bf16[2,5,128,128]{3,2,1,0:T(8,128)(2,1)S(1)}, u32[]{:S(2)}, u32[]{:S(2)}) %collective-permute-start.9) | collective-permute-done | bytes 327712 | tf_op jit(solution)/shard_map/ppermute | solution.py:363
  77.9 9.7 %collective-permute-done.10 = bf16[2,5,128,128]{3,2,1,0:T(8,128)(2,1)S(1)} collective-permute-done((bf16[2,5,128,128]{3,2,1,0:T(8,128)(2,1)}, bf16[2,5,128,128]{3,2,1,0:T(8,128)(2,1)S(1)}, u32[]{:S(2)}, u32[]{:S(2)}) %collective-permute-start.10) | collective-permute-done | bytes 327712 | tf_op jit(solution)/shard_map/ppermute | solution.py:363
  87.6 2.7 %collective-permute-done.11 = bf16[2,5,128,128]{3,2,1,0:T(8,128)(2,1)S(1)} collective-permute-done((bf16[2,5,128,128]{3,2,1,0:T(8,128)(2,1)}, bf16[2,5,128,128]{3,2,1,0:T(8,128)(2,1)S(1)}, u32[]{:S(2)}, u32[]{:S(2)}) %collective-permute-start.11) | collective-permute-done | bytes 327712 | tf_op jit(solution)/shard_map/ppermute | solution.py:363
  90.3 2.3 %collective-permute-done.12 = bf16[2,5,128,128]{3,2,1,0:T(8,128)(2,1)S(1)} collective-permute-done((bf16[2,5,128,128]{3,2,1,0:T(8,128)(2,1)}, bf16[2,5,128,128]{3,2,1,0:T(8,128)(2,1)S(1)}, u32[]{:S(2)}, u32[]{:S(2)}) %collective-permute-start.12) | collective-permute-done | bytes 327712 | tf_op jit(solution)/shard_map/ppermute | solution.py:363
  92.7 1.1 collective-permute-done.13
  93.9 7.4 %own_stats.1.stat_ref = f32[5,8,1024]{2,1,0:T(8,128)S(1)} custom-call(bf16[2,8,5,128,128]{4,3,2,1,0:T(8,128)(2,1)S(1)} %bitcast_dynamic-update-slice_fusion.8.kv_ref, bf16[2,8,5,128,128]{4,3,2,1,0:T(8,128)(2,1)S(1)} %bitcast_dynamic-update-slice_fusion.qd_ref.q_ref.d_ref), custom_call_target="tpu_custom_call" | custom-call | flops 2684354560 | bytes 5242880 | tf_op jit(solution)/shard_map/own_stats/pallas_call | solution.py:103
  101.3 1.6 copy-done.4
  103.6 11.9 %all-to-all-done.recv_ref = bf16[32,2,5,32,128]{4,3,2,1,0:T(8,128)(2,1)} async-done(((bf16[32,2,5,32,128]{4,3,2,1,0:T(8,128)(2,1)}), bf16[32,2,5,32,128]{4,3,2,1,0:T(8,128)(2,1)}, u32[]{:S(2)}, u32[]{:S(2)}) %all-to-all-start) | async-done | bytes 2621472 | tf_op jit(solution)/shard_map/all_to_all | solution.py:388
  115.5 12.6 %memory.1 = (bf16[32,2,5,32,128]{4,3,2,1,0:T(8,128)(2,1)}, f32[5,8,1024]{2,1,0:T(8,128)}) custom-call(s32[17]{0:T(128)} %pad_add_fusion.lists_ref, f32[5,8,1024]{2,1,0:T(8,128)} %copy-done.8, bf16[32,2,5,32,128]{4,3,2,1,0:T(8,128)(2,1)} %all-to-all-done.recv_ref, bf16[2,8,5,128,128]{4,3,2,1,0:T(8,128)(2,1)} %copy-done.4, bf16[2,8,5,128,128]{4,3,2,1,0:T(8,128)(2,1)} %copy-done.4), custom_call_target="tpu_custom_call" | custom-call | flops 2684354560 | bytes 5242880 | tf_op jit(solution)/shard_map/memory/pallas_call | solution.py:166
  128.1 6.5 %all-to-all-start.1 = ((bf16[32,2,5,32,128]{4,3,2,1,0:T(8,128)(2,1)}), bf16[32,2,5,32,128]{4,3,2,1,0:T(8,128)(2,1)S(1)}, u32[]{:S(2)}, u32[]{:S(2)}) async-start(bf16[32,2,5,32,128]{4,3,2,1,0:T(8,128)(2,1)} %get-tuple-element.66), calls=%async_computation.1 | async-start | bytes 5242880 | tf_op jit(solution)/shard_map/all_to_all | solution.py:392
  134.6 1.7 copy-done.1
  136.3 1.7 copy-done.5
  138.1 22.2 %own_grads.1 = (bf16[1,5,128,128]{3,2,1,0:T(8,128)(2,1)}, bf16[1,5,128,128]{3,2,1,0:T(8,128)(2,1)}, bf16[1,5,128,128]{3,2,1,0:T(8,128)(2,1)}, bf16[1,5,128,128]{...) custom-call(s32[17]{0:T(128)S(1)} %copy-done.6, ...), custom_call_target="tpu_custom_call" | custom-call | flops 10066329600 | bytes 10485760 | tf_op jit(solution)/shard_map/own_grads/pallas_call | solution.py:218
  162.1 3.0 %collective-permute-start.18 = (bf16[1,5,128,128]{3,2,1,0:T(8,128)(2,1)}, bf16[1,5,128,128]{3,2,1,0:T(8,128)(2,1)S(1)}, u32[]{:S(2)}, u32[]{:S(2)}) collective-permute-start(bf16[1,5,128,128]{3,2,1,0:T(8,128)(2,1)} %get-tuple-element.73), channel_id=1, source_target_pairs={{0,6},{1,7},{2,0},{3,1},{4,2},{5,3},{6,4},{7,5},{8,14},{9,15},{10,... | collective-permute-start | bytes 491528 | tf_op jit(solution)/shard_map/ppermute | solution.py:363
  165.1 1.7 collective-permute-start.20
  166.8 1.6 collective-permute-start.14
  168.3 1.2 collective-permute-start.15
  169.5 7.6 %collective-permute-done.19.refs_4_ = bf16[1,5,128,128]{3,2,1,0:T(8,128)(2,1)S(1)} collective-permute-done((bf16[1,5,128,128]{3,2,1,0:T(8,128)(2,1)}, bf16[1,5,128,128]{3,2,1,0:T(8,128)(2,1)S(1)}, u32[]{:S(2)}, u32[]{:S(2)}) %collective-permute-start.19) | collective-permute-done | bytes 163872 | tf_op jit(solution)/shard_map/ppermute | solution.py:363
  178.5 1.2 place.4.refs_2_
  179.7 1.1 collective-permute-done.14.refs_0_
  181.6 12.9 %all-to-all-done.1.back_ref = bf16[32,2,5,32,128]{4,3,2,1,0:T(8,128)(2,1)S(1)} async-done(((bf16[32,2,5,32,128]{4,3,2,1,0:T(8,128)(2,1)}), bf16[32,2,5,32,128]{4,3,2,1,0:T(8,128)(2,1)S(1)}, u32[]{:S(2)}, u32[]{:S(2)}) %all-to-all-start.1) | async-done | bytes 2621472 | tf_op jit(solution)/shard_map/all_to_all | solution.py:392
  194.5 1.7 copy-done.2
  196.2 1.5 collect.1
  197.7 4.5 %collective-permute-start.23 = (bf16[2,5,128,128]{3,2,1,0:T(8,128)(2,1)S(1)}, bf16[2,5,128,128]{3,2,1,0:T(8,128)(2,1)S(1)}, u32[]{:S(2)}, u32[]{:S(2)}) collective-permute-start(bf16[2,5,128,128]{3,2,1,0:T(8,128)(2,1)S(1)} %get-tuple-element.82), channel_id=1, source_target_pairs={{0,7},{1,0},{2,1},{3,2},{4,3},{5,4},{6,5},{7,6},{8,15},{9,8},{10,9... | collective-permute-start | bytes 983048 | tf_op jit(solution)/shard_map/ppermute | solution.py:363
  202.3 2.6 %collective-permute-start.25 = (bf16[2,5,128,128]{3,2,1,0:T(8,128)(2,1)S(1)}, bf16[2,5,128,128]{3,2,1,0:T(8,128)(2,1)S(1)}, u32[]{:S(2)}, u32[]{:S(2)}) collective-permute-start(bf16[2,5,128,128]{3,2,1,0:T(8,128)(2,1)S(1)} %get-tuple-element.84), channel_id=1, source_target_pairs={{0,6},{1,7},{2,0},{3,1},{4,2},{5,3},{6,4},{7,5},{8,14},{9,15},{10,... | collective-permute-start | bytes 983048 | tf_op jit(solution)/shard_map/ppermute | solution.py:363
  204.8 2.8 %collective-permute-start.27 = (bf16[2,5,128,128]{3,2,1,0:T(8,128)(2,1)S(1)}, bf16[2,5,128,128]{3,2,1,0:T(8,128)(2,1)S(1)}, u32[]{:S(2)}, u32[]{:S(2)}) collective-permute-start(bf16[2,5,128,128]{3,2,1,0:T(8,128)(2,1)S(1)} %get-tuple-element.86), channel_id=1, source_target_pairs={{0,5},{1,6},{2,7},{3,0},{4,1},{5,2},{6,3},{7,4},{8,13},{9,14},{10,... | collective-permute-start | bytes 983048 | tf_op jit(solution)/shard_map/ppermute | solution.py:363
  207.7 4.0 %collective-permute-start.21 = (bf16[2,5,128,128]{3,2,1,0:T(8,128)(2,1)S(1)}, bf16[2,5,128,128]{3,2,1,0:T(8,128)(2,1)S(1)}, u32[]{:S(2)}, u32[]{:S(2)}) collective-permute-start(bf16[2,5,128,128]{3,2,1,0:T(8,128)(2,1)S(1)} %get-tuple-element.79), channel_id=1, source_target_pairs={{0,3},{1,4},{2,5},{3,6},{4,7},{5,0},{6,1},{7,2},{8,11},{9,12},{10,... | collective-permute-start | bytes 983048 | tf_op jit(solution)/shard_map/ppermute | solution.py:363
  212.5 5.4 %collective-permute-done.26.refs_4_ = bf16[2,5,128,128]{3,2,1,0:T(8,128)(2,1)S(1)} collective-permute-done((bf16[2,5,128,128]{3,2,1,0:T(8,128)(2,1)S(1)}, bf16[2,5,128,128]{3,2,1,0:T(8,128)(2,1)S(1)}, u32[]{:S(2)}, u32[]{:S(2)}) %collective-permute-start.26) | collective-permute-done | bytes 327712 | tf_op jit(solution)/shard_map/ppermute | solution.py:363
  217.9 13.1 %collective-permute-done.27.refs_5_ = bf16[2,5,128,128]{3,2,1,0:T(8,128)(2,1)S(1)} collective-permute-done((bf16[2,5,128,128]{3,2,1,0:T(8,128)(2,1)S(1)}, bf16[2,5,128,128]{3,2,1,0:T(8,128)(2,1)S(1)}, u32[]{:S(2)}, u32[]{:S(2)}) %collective-permute-start.27) | collective-permute-done | bytes 327712 | tf_op jit(solution)/shard_map/ppermute | solution.py:363
  231.0 1.8 place.6
  (70 shorter events, 12.9 us)
Async XLA Ops:
  0.6 14.6 %copy-start.10 = (s32[32]{0:T(128)S(1)}, s32[32]{0:T(128)}, u32[]{:S(2)}) copy-start(s32[32]{0:T(128)} %param.11) | copy-start | bytes 388
  0.6 14.6 %copy-start.9 = (s32[32,16]{0,1:T(8,128)S(1)}, s32[32,16]{0,1:T(8,128)}, u32[]{:S(2)}) copy-start(s32[32,16]{0,1:T(8,128)} %param.10) | copy-start | bytes 6148
  4.6 10.8 %collective-permute-start = (bf16[2,5,128,128]{3,2,1,0:T(8,128)(2,1)}, bf16[2,5,128,128]{3,2,1,0:T(8,128)(2,1)}, u32[]{:S(2)}, u32[]{:S(2)}) collective-permute-start(bf16[2,5,128,128]{3,2,1,0:T(8,128)(2,1)} %get-tuple-element.48), channel_id=1, source_target_pairs={{0,1},{1,2},{2,3},{3,4},{4,5},{5,6},{6,7},{7,0},{8,9},{9,10},{10,1... | collective-permute-start | bytes 983048 | tf_op jit(solution)/shard_map/ppermute | solution.py:363
  7.3 18.6 %collective-permute-start.1 = (bf16[2,5,128,128]{3,2,1,0:T(8,128)(2,1)}, bf16[2,5,128,128]{3,2,1,0:T(8,128)(2,1)}, u32[]{:S(2)}, u32[]{:S(2)}) collective-permute-start(bf16[2,5,128,128]{3,2,1,0:T(8,128)(2,1)} %get-tuple-element.49), channel_id=1, source_target_pairs={{0,2},{1,3},{2,4},{3,5},{4,6},{5,7},{6,0},{7,1},{8,10},{9,11},{10,... | collective-permute-start | bytes 983048 | tf_op jit(solution)/shard_map/ppermute | solution.py:363
  8.6 31.2 %collective-permute-start.2 = (bf16[2,5,128,128]{3,2,1,0:T(8,128)(2,1)}, bf16[2,5,128,128]{3,2,1,0:T(8,128)(2,1)}, u32[]{:S(2)}, u32[]{:S(2)}) collective-permute-start(bf16[2,5,128,128]{3,2,1,0:T(8,128)(2,1)} %get-tuple-element.50), channel_id=1, source_target_pairs={{0,3},{1,4},{2,5},{3,6},{4,7},{5,0},{6,1},{7,2},{8,11},{9,12},{10,... | collective-permute-start | bytes 983048 | tf_op jit(solution)/shard_map/ppermute | solution.py:363
  10.3 30.5 %collective-permute-start.3 = (bf16[2,5,128,128]{3,2,1,0:T(8,128)(2,1)}, bf16[2,5,128,128]{3,2,1,0:T(8,128)(2,1)S(1)}, u32[]{:S(2)}, u32[]{:S(2)}) collective-permute-start(bf16[2,5,128,128]{3,2,1,0:T(8,128)(2,1)} %get-tuple-element.51), channel_id=1, source_target_pairs={{0,4},{1,5},{2,6},{3,7},{4,0},{5,1},{6,2},{7,3},{8,12},{9,13},{10,... | collective-permute-start | bytes 983048 | tf_op jit(solution)/shard_map/ppermute | solution.py:363
  11.6 29.3 %collective-permute-start.4 = (bf16[2,5,128,128]{3,2,1,0:T(8,128)(2,1)}, bf16[2,5,128,128]{3,2,1,0:T(8,128)(2,1)S(1)}, u32[]{:S(2)}, u32[]{:S(2)}) collective-permute-start(bf16[2,5,128,128]{3,2,1,0:T(8,128)(2,1)} %get-tuple-element.52), channel_id=1, source_target_pairs={{0,5},{1,6},{2,7},{3,0},{4,1},{5,2},{6,3},{7,4},{8,13},{9,14},{10,... | collective-permute-start | bytes 983048 | tf_op jit(solution)/shard_map/ppermute | solution.py:363
  15.4 25.5 %collective-permute-start.5 = (bf16[2,5,128,128]{3,2,1,0:T(8,128)(2,1)}, bf16[2,5,128,128]{3,2,1,0:T(8,128)(2,1)S(1)}, u32[]{:S(2)}, u32[]{:S(2)}) collective-permute-start(bf16[2,5,128,128]{3,2,1,0:T(8,128)(2,1)} %get-tuple-element.53), channel_id=1, source_target_pairs={{0,6},{1,7},{2,0},{3,1},{4,2},{5,3},{6,4},{7,5},{8,14},{9,15},{10,... | collective-permute-start | bytes 983048 | tf_op jit(solution)/shard_map/ppermute | solution.py:363
  25.9 15.1 %collective-permute-start.6 = (bf16[2,5,128,128]{3,2,1,0:T(8,128)(2,1)}, bf16[2,5,128,128]{3,2,1,0:T(8,128)(2,1)S(1)}, u32[]{:S(2)}, u32[]{:S(2)}) collective-permute-start(bf16[2,5,128,128]{3,2,1,0:T(8,128)(2,1)} %get-tuple-element.54), channel_id=1, source_target_pairs={{0,7},{1,0},{2,1},{3,2},{4,3},{5,4},{6,5},{7,6},{8,15},{9,8},{10,9... | collective-permute-start | bytes 983048 | tf_op jit(solution)/shard_map/ppermute | solution.py:363
  41.0 52.9 %copy-start = (bf16[2,8,5,128,128]{4,3,2,1,0:T(8,128)(2,1)}, bf16[2,8,5,128,128]{4,3,2,1,0:T(8,128)(2,1)S(1)}, u32[]{:S(2)}) copy-start(bf16[2,8,5,128,128]{4,3,2,1,0:T(8,128)(2,1)S(1)} %bitcast_dynamic-update-slice_fusion.8.kv_ref) | copy-start | bytes 7864324
  43.6 71.9 %all-to-all-start = ((bf16[32,2,5,32,128]{4,3,2,1,0:T(8,128)(2,1)}), bf16[32,2,5,32,128]{4,3,2,1,0:T(8,128)(2,1)}, u32[]{:S(2)}, u32[]{:S(2)}) async-start(bf16[32,2,5,32,128]{4,3,2,1,0:T(8,128)(2,1)} %pick.1), calls=%async_computation | async-start | bytes 5242880 | tf_op jit(solution)/shard_map/all_to_all | solution.py:388
  57.9 8.4 %collective-permute-start.7 = (bf16[2,5,128,128]{3,2,1,0:T(8,128)(2,1)}, bf16[2,5,128,128]{3,2,1,0:T(8,128)(2,1)S(1)}, u32[]{:S(2)}, u32[]{:S(2)}) collective-permute-start(bf16[2,5,128,128]{3,2,1,0:T(8,128)(2,1)} %get-tuple-element.58), channel_id=1, source_target_pairs={{0,1},{1,2},{2,3},{3,4},{4,5},{5,6},{6,7},{7,0},{8,9},{9,10},{10,1... | collective-permute-start | bytes 983048 | tf_op jit(solution)/shard_map/ppermute | solution.py:363
  59.2 13.7 %collective-permute-start.8 = (bf16[2,5,128,128]{3,2,1,0:T(8,128)(2,1)}, bf16[2,5,128,128]{3,2,1,0:T(8,128)(2,1)S(1)}, u32[]{:S(2)}, u32[]{:S(2)}) collective-permute-start(bf16[2,5,128,128]{3,2,1,0:T(8,128)(2,1)} %get-tuple-element.59), channel_id=1, source_target_pairs={{0,2},{1,3},{2,4},{3,5},{4,6},{5,7},{6,0},{7,1},{8,10},{9,11},{10,... | collective-permute-start | bytes 983048 | tf_op jit(solution)/shard_map/ppermute | solution.py:363
  62.3 15.5 %collective-permute-start.9 = (bf16[2,5,128,128]{3,2,1,0:T(8,128)(2,1)}, bf16[2,5,128,128]{3,2,1,0:T(8,128)(2,1)S(1)}, u32[]{:S(2)}, u32[]{:S(2)}) collective-permute-start(bf16[2,5,128,128]{3,2,1,0:T(8,128)(2,1)} %get-tuple-element.60), channel_id=1, source_target_pairs={{0,3},{1,4},{2,5},{3,6},{4,7},{5,0},{6,1},{7,2},{8,11},{9,12},{10,... | collective-permute-start | bytes 983048 | tf_op jit(solution)/shard_map/ppermute | solution.py:363
  64.1 23.5 %collective-permute-start.10 = (bf16[2,5,128,128]{3,2,1,0:T(8,128)(2,1)}, bf16[2,5,128,128]{3,2,1,0:T(8,128)(2,1)S(1)}, u32[]{:S(2)}, u32[]{:S(2)}) collective-permute-start(bf16[2,5,128,128]{3,2,1,0:T(8,128)(2,1)} %get-tuple-element.61), channel_id=1, source_target_pairs={{0,4},{1,5},{2,6},{3,7},{4,0},{5,1},{6,2},{7,3},{8,12},{9,13},{10,... | collective-permute-start | bytes 983048 | tf_op jit(solution)/shard_map/ppermute | solution.py:363
  65.8 24.5 %collective-permute-start.11 = (bf16[2,5,128,128]{3,2,1,0:T(8,128)(2,1)}, bf16[2,5,128,128]{3,2,1,0:T(8,128)(2,1)S(1)}, u32[]{:S(2)}, u32[]{:S(2)}) collective-permute-start(bf16[2,5,128,128]{3,2,1,0:T(8,128)(2,1)} %get-tuple-element.62), channel_id=1, source_target_pairs={{0,5},{1,6},{2,7},{3,0},{4,1},{5,2},{6,3},{7,4},{8,13},{9,14},{10,... | collective-permute-start | bytes 983048 | tf_op jit(solution)/shard_map/ppermute | solution.py:363
  66.2 26.4 %collective-permute-start.12 = (bf16[2,5,128,128]{3,2,1,0:T(8,128)(2,1)}, bf16[2,5,128,128]{3,2,1,0:T(8,128)(2,1)S(1)}, u32[]{:S(2)}, u32[]{:S(2)}) collective-permute-start(bf16[2,5,128,128]{3,2,1,0:T(8,128)(2,1)} %get-tuple-element.63), channel_id=1, source_target_pairs={{0,6},{1,7},{2,0},{3,1},{4,2},{5,3},{6,4},{7,5},{8,14},{9,15},{10,... | collective-permute-start | bytes 983048 | tf_op jit(solution)/shard_map/ppermute | solution.py:363
  72.9 20.9 %collective-permute-start.13 = (bf16[2,5,128,128]{3,2,1,0:T(8,128)(2,1)}, bf16[2,5,128,128]{3,2,1,0:T(8,128)(2,1)S(1)}, u32[]{:S(2)}, u32[]{:S(2)}) collective-permute-start(bf16[2,5,128,128]{3,2,1,0:T(8,128)(2,1)} %get-tuple-element.64), channel_id=1, source_target_pairs={{0,7},{1,0},{2,1},{3,2},{4,3},{5,4},{6,5},{7,6},{8,15},{9,8},{10,9... | collective-permute-start | bytes 983048 | tf_op jit(solution)/shard_map/ppermute | solution.py:363
  101.3 1.6 copy-start.4
  102.9 0.7 copy-start.8
  128.0 6.5 %copy-start.6 = (s32[17]{0:T(128)S(1)}, s32[17]{0:T(128)}, u32[]{:S(2)}) copy-start(s32[17]{0:T(128)} %pad_add_fusion.lists_ref) | copy-start | bytes 208
  128.0 6.5 %copy-start.7 = (f32[5,8,1024]{2,1,0:T(8,128)S(1)}, f32[5,8,1024]{2,1,0:T(8,128)}, u32[]{:S(2)}) copy-start(f32[5,8,1024]{2,1,0:T(8,128)} %get-tuple-element.67.fin_ref) | copy-start | bytes 491524
  128.1 66.4 %all-to-all-start.1 = ((bf16[32,2,5,32,128]{4,3,2,1,0:T(8,128)(2,1)}), bf16[32,2,5,32,128]{4,3,2,1,0:T(8,128)(2,1)S(1)}, u32[]{:S(2)}, u32[]{:S(2)}) async-start(bf16[32,2,5,32,128]{4,3,2,1,0:T(8,128)(2,1)} %get-tuple-element.66), calls=%async_computation.1 | async-start | bytes 5242880 | tf_op jit(solution)/shard_map/all_to_all | solution.py:392
  134.6 1.7 copy-start.1
  136.3 1.7 copy-start.5
  160.3 6.4 %collective-permute-start.16 = (bf16[1,5,128,128]{3,2,1,0:T(8,128)(2,1)}, bf16[1,5,128,128]{3,2,1,0:T(8,128)(2,1)S(1)}, u32[]{:S(2)}, u32[]{:S(2)}) collective-permute-start(bf16[1,5,128,128]{3,2,1,0:T(8,128)(2,1)} %get-tuple-element.71), channel_id=1, source_target_pairs={{0,7},{1,0},{2,1},{3,2},{4,3},{5,4},{6,5},{7,6},{8,15},{9,8},{10,9... | collective-permute-start | bytes 491528 | tf_op jit(solution)/shard_map/ppermute | solution.py:363
  161.1 7.3 %collective-permute-start.17 = (bf16[1,5,128,128]{3,2,1,0:T(8,128)(2,1)}, bf16[1,5,128,128]{3,2,1,0:T(8,128)(2,1)S(1)}, u32[]{:S(2)}, u32[]{:S(2)}) collective-permute-start(bf16[1,5,128,128]{3,2,1,0:T(8,128)(2,1)} %get-tuple-element.72), channel_id=1, source_target_pairs={{0,1},{1,2},{2,3},{3,4},{4,5},{5,6},{6,7},{7,0},{8,9},{9,10},{10,1... | collective-permute-start | bytes 491528 | tf_op jit(solution)/shard_map/ppermute | solution.py:363
  162.1 7.4 %collective-permute-start.18 = (bf16[1,5,128,128]{3,2,1,0:T(8,128)(2,1)}, bf16[1,5,128,128]{3,2,1,0:T(8,128)(2,1)S(1)}, u32[]{:S(2)}, u32[]{:S(2)}) collective-permute-start(bf16[1,5,128,128]{3,2,1,0:T(8,128)(2,1)} %get-tuple-element.73), channel_id=1, source_target_pairs={{0,6},{1,7},{2,0},{3,1},{4,2},{5,3},{6,4},{7,5},{8,14},{9,15},{10,... | collective-permute-start | bytes 491528 | tf_op jit(solution)/shard_map/ppermute | solution.py:363
  165.0 12.0 %collective-permute-start.19 = (bf16[1,5,128,128]{3,2,1,0:T(8,128)(2,1)}, bf16[1,5,128,128]{3,2,1,0:T(8,128)(2,1)S(1)}, u32[]{:S(2)}, u32[]{:S(2)}) collective-permute-start(bf16[1,5,128,128]{3,2,1,0:T(8,128)(2,1)} %get-tuple-element.74), channel_id=1, source_target_pairs={{0,2},{1,3},{2,4},{3,5},{4,6},{5,7},{6,0},{7,1},{8,10},{9,11},{10,... | collective-permute-start | bytes 491528 | tf_op jit(solution)/shard_map/ppermute | solution.py:363
  165.1 12.5 %collective-permute-start.20 = (bf16[1,5,128,128]{3,2,1,0:T(8,128)(2,1)}, bf16[1,5,128,128]{3,2,1,0:T(8,128)(2,1)S(1)}, u32[]{:S(2)}, u32[]{:S(2)}) collective-permute-start(bf16[1,5,128,128]{3,2,1,0:T(8,128)(2,1)} %get-tuple-element.75), channel_id=1, source_target_pairs={{0,5},{1,6},{2,7},{3,0},{4,1},{5,2},{6,3},{7,4},{8,13},{9,14},{10,... | collective-permute-start | bytes 491528 | tf_op jit(solution)/shard_map/ppermute | solution.py:363
  166.8 14.0 %collective-permute-start.14 = (bf16[1,5,128,128]{3,2,1,0:T(8,128)(2,1)}, bf16[1,5,128,128]{3,2,1,0:T(8,128)(2,1)S(1)}, u32[]{:S(2)}, u32[]{:S(2)}) collective-permute-start(bf16[1,5,128,128]{3,2,1,0:T(8,128)(2,1)} %get-tuple-element.68), channel_id=1, source_target_pairs={{0,3},{1,4},{2,5},{3,6},{4,7},{5,0},{6,1},{7,2},{8,11},{9,12},{10,... | collective-permute-start | bytes 491528 | tf_op jit(solution)/shard_map/ppermute | solution.py:363
  168.3 12.5 %collective-permute-start.15 = (bf16[1,5,128,128]{3,2,1,0:T(8,128)(2,1)}, bf16[1,5,128,128]{3,2,1,0:T(8,128)(2,1)S(1)}, u32[]{:S(2)}, u32[]{:S(2)}) collective-permute-start(bf16[1,5,128,128]{3,2,1,0:T(8,128)(2,1)} %get-tuple-element.69), channel_id=1, source_target_pairs={{0,4},{1,5},{2,6},{3,7},{4,0},{5,1},{6,2},{7,3},{8,12},{9,13},{10,... | collective-permute-start | bytes 491528 | tf_op jit(solution)/shard_map/ppermute | solution.py:363
  177.6 0.9 copy-start.3
  194.5 1.7 copy-start.2
  197.7 9.9 %collective-permute-start.23 = (bf16[2,5,128,128]{3,2,1,0:T(8,128)(2,1)S(1)}, bf16[2,5,128,128]{3,2,1,0:T(8,128)(2,1)S(1)}, u32[]{:S(2)}, u32[]{:S(2)}) collective-permute-start(bf16[2,5,128,128]{3,2,1,0:T(8,128)(2,1)S(1)} %get-tuple-element.82), channel_id=1, source_target_pairs={{0,7},{1,0},{2,1},{3,2},{4,3},{5,4},{6,5},{7,6},{8,15},{9,8},{10,9... | collective-permute-start | bytes 983048 | tf_op jit(solution)/shard_map/ppermute | solution.py:363
  202.3 9.4 %collective-permute-start.24 = (bf16[2,5,128,128]{3,2,1,0:T(8,128)(2,1)S(1)}, bf16[2,5,128,128]{3,2,1,0:T(8,128)(2,1)S(1)}, u32[]{:S(2)}, u32[]{:S(2)}) collective-permute-start(bf16[2,5,128,128]{3,2,1,0:T(8,128)(2,1)S(1)} %get-tuple-element.83), channel_id=1, source_target_pairs={{0,1},{1,2},{2,3},{3,4},{4,5},{5,6},{6,7},{7,0},{8,9},{9,10},{10,1... | collective-permute-start | bytes 983048 | tf_op jit(solution)/shard_map/ppermute | solution.py:363
  202.3 10.3 %collective-permute-start.25 = (bf16[2,5,128,128]{3,2,1,0:T(8,128)(2,1)S(1)}, bf16[2,5,128,128]{3,2,1,0:T(8,128)(2,1)S(1)}, u32[]{:S(2)}, u32[]{:S(2)}) collective-permute-start(bf16[2,5,128,128]{3,2,1,0:T(8,128)(2,1)S(1)} %get-tuple-element.84), channel_id=1, source_target_pairs={{0,6},{1,7},{2,0},{3,1},{4,2},{5,3},{6,4},{7,5},{8,14},{9,15},{10,... | collective-permute-start | bytes 983048 | tf_op jit(solution)/shard_map/ppermute | solution.py:363
  204.8 13.1 %collective-permute-start.26 = (bf16[2,5,128,128]{3,2,1,0:T(8,128)(2,1)S(1)}, bf16[2,5,128,128]{3,2,1,0:T(8,128)(2,1)S(1)}, u32[]{:S(2)}, u32[]{:S(2)}) collective-permute-start(bf16[2,5,128,128]{3,2,1,0:T(8,128)(2,1)S(1)} %get-tuple-element.85), channel_id=1, source_target_pairs={{0,2},{1,3},{2,4},{3,5},{4,6},{5,7},{6,0},{7,1},{8,10},{9,11},{10,... | collective-permute-start | bytes 983048 | tf_op jit(solution)/shard_map/ppermute | solution.py:363
  204.8 26.2 %collective-permute-start.27 = (bf16[2,5,128,128]{3,2,1,0:T(8,128)(2,1)S(1)}, bf16[2,5,128,128]{3,2,1,0:T(8,128)(2,1)S(1)}, u32[]{:S(2)}, u32[]{:S(2)}) collective-permute-start(bf16[2,5,128,128]{3,2,1,0:T(8,128)(2,1)S(1)} %get-tuple-element.86), channel_id=1, source_target_pairs={{0,5},{1,6},{2,7},{3,0},{4,1},{5,2},{6,3},{7,4},{8,13},{9,14},{10,... | collective-permute-start | bytes 983048 | tf_op jit(solution)/shard_map/ppermute | solution.py:363
  207.7 25.2 %collective-permute-start.21 = (bf16[2,5,128,128]{3,2,1,0:T(8,128)(2,1)S(1)}, bf16[2,5,128,128]{3,2,1,0:T(8,128)(2,1)S(1)}, u32[]{:S(2)}, u32[]{:S(2)}) collective-permute-start(bf16[2,5,128,128]{3,2,1,0:T(8,128)(2,1)S(1)} %get-tuple-element.79), channel_id=1, source_target_pairs={{0,3},{1,4},{2,5},{3,6},{4,7},{5,0},{6,1},{7,2},{8,11},{9,12},{10,... | collective-permute-start | bytes 983048 | tf_op jit(solution)/shard_map/ppermute | solution.py:363
  211.7 21.2 %collective-permute-start.22 = (bf16[2,5,128,128]{3,2,1,0:T(8,128)(2,1)S(1)}, bf16[2,5,128,128]{3,2,1,0:T(8,128)(2,1)S(1)}, u32[]{:S(2)}, u32[]{:S(2)}) collective-permute-start(bf16[2,5,128,128]{3,2,1,0:T(8,128)(2,1)S(1)} %get-tuple-element.80), channel_id=1, source_target_pairs={{0,4},{1,5},{2,6},{3,7},{4,0},{5,1},{6,2},{7,3},{8,12},{9,13},{10,... | collective-permute-start | bytes 983048 | tf_op jit(solution)/shard_map/ppermute | solution.py:363
